TPU v7x, 32 devices: a whole 2x2x4 slice. The times are simulated.
32 devices in a mesh: dp: 4 (over y, x), mp: 8 (over z, core).
Axes of the slice: x: 2, y: 2, z: 4, core: 2. Of those that a mesh axis runs over, the one named last changes fastest.
Arguments:
- tokens: bfloat16 [1280, 4096], P(('dp', 'mp')), may hold values from -6 to 6
- w_gate: bfloat16 [4096, 8192], P(None, 'mp'), may hold values from -0.09375 to 0.09375
- w_up: bfloat16 [4096, 8192], P(None, 'mp'), may hold values from -0.09375 to 0.09375
- w_down: bfloat16 [8192, 4096], P('mp'), may hold values from -0.0625 to 0.0625
- cotangent: bfloat16 [1280, 4096], P(('dp', 'mp')), may hold values from -6 to 6
Outputs:
- mixed: bfloat16 [1280, 4096], P(('dp', 'mp'))
- input_grad: bfloat16 [1280, 4096], P(('dp', 'mp'))
- grad_gate: bfloat16 [4096, 8192], P('dp', 'mp')
- grad_up: bfloat16 [4096, 8192], P('dp', 'mp')
- grad_down: bfloat16 [8192, 4096], P('mp', 'dp')
All inputs are finite; a program needn't handle non-finite values.
Results may differ from a plain program's by a relative error of at most 0.019.
Values may be sent and summed in bfloat16 or wider, within the bound.
No kernel may reach another device: no remote copies, remote signals or barrier semaphores. Data moves between devices by JAX's collectives and lax.ppermute only.
A program may use at most 192 MiB of HBM per device.

v0:
```python
import jax
import jax.numpy as jnp
from jax import lax
from jax.sharding import PartitionSpec as P


def contract_rows(left, right):
    return lax.dot_general(
        left, right, (((0,), (0,)), ((), ())), preferred_element_type=jnp.float32
    )


def contract_cols(left, right):
    return lax.dot_general(
        left, right, (((1,), (1,)), ((), ())), preferred_element_type=jnp.float32
    )


def on_device(tokens, w_gate, w_up, w_down, cotangent):
    panel = w_gate.shape[1]
    gathered = lax.all_gather(tokens, "mp", axis=0, tiled=True)
    gate = jnp.dot(gathered, w_gate, preferred_element_type=jnp.float32)
    up = jnp.dot(gathered, w_up, preferred_element_type=jnp.float32)
    swish = jax.nn.silu(gate)
    hidden = (swish * up).astype(jnp.bfloat16)
    mixed = lax.psum_scatter(
        jnp.dot(hidden, w_down, preferred_element_type=jnp.float32).astype(jnp.bfloat16),
        "mp",
        scatter_dimension=0,
        tiled=True,
    )
    upstream = lax.all_gather(cotangent, "mp", axis=0, tiled=True)
    dhidden = contract_cols(upstream, w_down)
    sigma = jax.nn.sigmoid(gate)
    dgate = (dhidden * up * sigma * (1.0 + gate * (1.0 - sigma))).astype(jnp.bfloat16)
    dup = (dhidden * swish).astype(jnp.bfloat16)
    input_grad = lax.psum_scatter(
        (contract_cols(dgate, w_gate) + contract_cols(dup, w_up)).astype(jnp.bfloat16),
        "mp",
        scatter_dimension=0,
        tiled=True,
    )
    summed = lax.psum_scatter(
        jnp.concatenate(
            [
                contract_rows(gathered, dgate),
                contract_rows(gathered, dup),
                contract_rows(upstream, hidden),
            ],
            axis=1,
        ).astype(jnp.bfloat16),
        "dp",
        scatter_dimension=0,
        tiled=True,
    ).astype(jnp.float32)
    grad_gate = summed[:, :panel]
    grad_up = summed[:, panel : 2 * panel]
    grad_down = summed[:, 2 * panel :].T
    return (
        mixed,
        input_grad,
        grad_gate.astype(jnp.bfloat16),
        grad_up.astype(jnp.bfloat16),
        grad_down.astype(jnp.bfloat16),
    )


def solution(mesh):
    in_specs = (
        P(("dp", "mp"), None),
        P(None, "mp"),
        P(None, "mp"),
        P("mp", None),
        P(("dp", "mp"), None),
    )
    out_specs = (
        P(("dp", "mp"), None),
        P(("dp", "mp"), None),
        P("dp", "mp"),
        P("dp", "mp"),
        P("mp", "dp"),
    )
    return jax.shard_map(
        on_device, mesh=mesh, in_specs=in_specs, out_specs=out_specs, check_vma=False
    )
```

profile of v0, /device:TPU:0, one launch (start us, length us, event | category | flops | bytes accessed | tf_op | source)
XLA Modules:
  0.0 434.7 jit_solution(3208026064208609340)
XLA Ops:
  7.2 0.0 all-gather.3.cloned.1.call-start
  7.2 0.7 all-gather.3.cloned.1.call-update
  7.9 0.0 all-gather.5.cloned.1.call-start
  7.9 0.7 all-gather.5.cloned.1.call-update
  8.6 0.0 reduce-scatter.8.cloned.1.call-start
  8.7 37.6 %all-gather.3.cloned.1.call-done = bf16[320,4096]{1,0:T(8,128)(2,1)} async-done(((bf16[40,4096]{1,0:T(8,128)(2,1)}), bf16[320,4096]{1,0:T(8,128)(2,1)}) %all-gather.3.cloned.1.call-update) | async-done | bytes 2621456 | tf_op jit(solution)/shard_map/all_gather | solution.py:21
  46.3 8.2 %fusion.3 = f32[320,1024]{1,0:T(8,128)} fusion(bf16[320,4096]{1,0:T(8,128)(2,1)} %all-gather.3.cloned.1.call-done, bf16[4096,1024]{1,0:T(8,128)(2,1)} %param.7), kind=kOutput, calls=%fused_computation.14 | convolution fusion | flops 2684354560 | bytes 12320768 | tf_op jit(solution)/shard_map/dot_general | solution.py:23
  54.5 7.5 %fusion.2 = f32[320,1024]{1,0:T(8,128)} fusion(bf16[320,4096]{1,0:T(8,128)(2,1)S(1)} %copy-done, bf16[4096,1024]{1,0:T(8,128)(2,1)} %param.6), kind=kOutput, calls=%fused_computation.13 | convolution fusion | flops 2684354560 | bytes 12320768 | tf_op jit(solution)/shard_map/dot_general | solution.py:22
  62.0 18.8 %all-gather.5.cloned.1.call-done = bf16[320,4096]{1,0:T(8,128)(2,1)} async-done(((bf16[40,4096]{1,0:T(8,128)(2,1)}), bf16[320,4096]{1,0:T(8,128)(2,1)}) %all-gather.5.cloned.1.call-update) | async-done | bytes 2621456 | tf_op jit(solution)/shard_map/all_gather | solution.py:32
  80.8 8.3 %multiply_convert_fusion = (bf16[320,1024]{1,0:T(8,128)(2,1)S(1)}, bf16[320,1024]{1,0:T(8,128)(2,1)S(1)}, bf16[320,1024]{1,0:T(8,128)(2,1)S(1)}) fusion(f32[320,1024]{1,0:T(8,128)} %fusion.2, f32[320,1024]{1,0:T(8,128)} %fusion.3, bf16[320,4096]{1,0:T(8,128)(2,1)} %all-gather.5.cloned.1.call-done, bf16[1024,4096]{1,0:T(8,128)(2,1)} %param.8), kind=kOutput, calls=%fused_computation.8 | convolution fusion | flops 2689269760 | bytes 15597568 | tf_op jit(solution)/shard_map/dot_general | solution.py:14
  89.1 0.0 copy-start.4
  89.1 0.0 copy-start.2
  89.2 7.1 %convert_bitcast_fusion = bf16[4096,1024]{0,1:T(8,128)(2,1)} fusion(bf16[320,1024]{1,0:T(8,128)(2,1)S(1)} %get-tuple-element.15, bf16[320,4096]{1,0:T(8,128)(2,1)S(1)} %copy-done.1), kind=kOutput, calls=%fused_computation.1 | convolution fusion | flops 2688548864 | bytes 11665408 | tf_op jit(solution)/shard_map/dot_general | solution.py:8
  96.2 6.9 %convert_bitcast_fusion.1 = bf16[4096,1024]{0,1:T(8,128)(2,1)} fusion(bf16[320,1024]{1,0:T(8,128)(2,1)S(1)} %get-tuple-element.13, bf16[320,4096]{1,0:T(8,128)(2,1)S(1)} %copy-done), kind=kOutput, calls=%fused_computation.2 | convolution fusion | flops 2688548864 | bytes 11665408 | tf_op jit(solution)/shard_map/dot_general | solution.py:8
  103.1 6.8 %convert_bitcast_fusion.2 = bf16[4096,1024]{0,1:T(8,128)(2,1)} fusion(bf16[320,1024]{1,0:T(8,128)(2,1)S(1)} %get-tuple-element.14, bf16[320,4096]{1,0:T(8,128)(2,1)S(1)} %copy-done), kind=kOutput, calls=%fused_computation.3 | convolution fusion | flops 2688548864 | bytes 11665408 | tf_op jit(solution)/shard_map/dot_general | solution.py:8
  109.9 17.6 %pad_maximum_fusion = bf16[4096,3072]{0,1:T(8,128)(2,1)} fusion(bf16[4096,1024]{0,1:T(8,128)(2,1)} %convert_bitcast_fusion, bf16[4096,1024]{0,1:T(8,128)(2,1)} %convert_bitcast_fusion.1, bf16[4096,1024]{0,1:T(8,128)(2,1)} %convert_bitcast_fusion.2), kind=kLoop, calls=%fused_computation | loop fusion | flops 75497472 | bytes 50331648 | tf_op jit(solution)/shard_map/concatenate | solution.py:44
  127.5 0.0 reduce-scatter.8.cloned.1.call-update
  127.6 0.0 reduce-scatter.4.cloned.1.call-start
  127.6 1.0 copy-done.5
  128.6 7.6 %convolution_convert_fusion = bf16[320,4096]{1,0:T(8,128)(2,1)} fusion(bf16[320,1024]{1,0:T(8,128)(2,1)S(1)} %copy-done.5, bf16[1024,4096]{1,0:T(8,128)(2,1)} %param.8), kind=kOutput, calls=%fused_computation.6 | convolution fusion | flops 2685665280 | bytes 11665408 | tf_op jit(solution)/shard_map/dot_general | solution.py:27
  136.2 0.0 reduce-scatter.4.cloned.1.call-update
  136.2 0.0 reduce-scatter.6.cloned.1.call-start
  136.3 1.0 copy-done.3
  137.3 5.3 %fusion.4 = f32[320,4096]{1,0:T(8,128)S(1)} fusion(bf16[320,1024]{1,0:T(8,128)(2,1)S(1)} %copy-done.3, bf16[4096,1024]{1,0:T(8,128)(2,1)} %param.6), kind=kOutput, calls=%fused_computation.15 | convolution fusion | flops 2684354560 | bytes 14286848 | tf_op jit(solution)/shard_map/dot_general | solution.py:14
  142.6 10.6 %fusion = bf16[320,4096]{1,0:T(8,128)(2,1)} fusion(f32[320,4096]{1,0:T(8,128)S(1)} %fusion.4, bf16[320,1024]{1,0:T(8,128)(2,1)S(1)} %get-tuple-element.13, bf16[4096,1024]{1,0:T(8,128)(2,1)} %param.7), kind=kOutput, calls=%fused_computation.5 | convolution fusion | flops 2686976000 | bytes 16908288 | tf_op jit(solution)/shard_map/dot_general | solution.py:14
  153.2 0.0 reduce-scatter.6.cloned.1.call-update
  153.2 195.3 %reduce-scatter.8.cloned.1.call-done = bf16[1024,3072]{0,1:T(8,128)(2,1)} async-done(((bf16[4096,3072]{0,1:T(8,128)(2,1)}), bf16[1024,3072]{0,1:T(8,128)(2,1)}) %reduce-scatter.8.cloned.1.call-update) | async-done | bytes 6291472 | tf_op jit(solution)/shard_map/reduce_scatter | solution.py:43
  348.6 5.6 %slice_bitcast_fusion = (bf16[1024,1024]{1,0:T(8,128)(2,1)}, bf16[1024,1024]{0,1:T(8,128)(2,1)}, bf16[1024,1024]{0,1:T(8,128)(2,1)S(1)}) fusion(bf16[1024,3072]{0,1:T(8,128)(2,1)} %reduce-scatter.8.cloned.1.call-done), kind=kLoop, calls=%fused_computation.7 | loop fusion | bytes 12582912 | tf_op jit(solution)/shard_map/convert_element_type | solution.py:64
  354.1 3.9 copy.11
  358.1 2.5 copy.10
  360.6 28.3 %reduce-scatter.4.cloned.1.call-done = bf16[40,4096]{1,0:T(8,128)(2,1)} async-done(((bf16[320,4096]{1,0:T(8,128)(2,1)}), bf16[40,4096]{1,0:T(8,128)(2,1)}) %reduce-scatter.4.cloned.1.call-update) | async-done | bytes 327696 | tf_op jit(solution)/shard_map/reduce_scatter | solution.py:26
  388.9 39.3 %reduce-scatter.6.cloned.1.call-done = bf16[40,4096]{1,0:T(8,128)(2,1)} async-done(((bf16[320,4096]{1,0:T(8,128)(2,1)}), bf16[40,4096]{1,0:T(8,128)(2,1)}) %reduce-scatter.6.cloned.1.call-update) | async-done | bytes 327696 | tf_op jit(solution)/shard_map/reduce_scatter | solution.py:37
  (8 shorter events, 0.0 us)
Async XLA Ops:
  7.2 39.1 %all-gather.3.cloned.1.call-start = ((), (), s32[]{:S(2)}) async-start(), calls=%async_computation.3 | async-start | bytes 2949120 | tf_op jit(solution)/shard_map/all_gather | solution.py:21
  7.9 72.9 %all-gather.5.cloned.1.call-start = ((), (), s32[]{:S(2)}) async-start(), calls=%async_computation.5 | async-start | bytes 2949120 | tf_op jit(solution)/shard_map/all_gather | solution.py:32
  8.6 339.9 %reduce-scatter.8.cloned.1.call-start = ((), (), s32[]{:S(2)}) async-start(), calls=%async_computation.7 | async-start | bytes 31457280 | tf_op jit(solution)/shard_map/reduce_scatter | solution.py:43
  46.3 8.2 %copy-start = (bf16[320,4096]{1,0:T(8,128)(2,1)S(1)}, bf16[320,4096]{1,0:T(8,128)(2,1)}, u32[]{:S(2)}) copy-start(bf16[320,4096]{1,0:T(8,128)(2,1)} %all-gather.3.cloned.1.call-done) | copy-start | bytes 7864324
  80.8 8.3 %copy-start.1 = (bf16[320,4096]{1,0:T(8,128)(2,1)S(1)}, bf16[320,4096]{1,0:T(8,128)(2,1)}, u32[]{:S(2)}) copy-start(bf16[320,4096]{1,0:T(8,128)(2,1)} %all-gather.5.cloned.1.call-done) | copy-start | bytes 7864324
  89.1 7.1 %copy-start.4 = (bf16[320,1024]{1,0:T(8,128)(2,1)}, bf16[320,1024]{1,0:T(8,128)(2,1)S(1)}, u32[]{:S(2)}) copy-start(bf16[320,1024]{1,0:T(8,128)(2,1)S(1)} %get-tuple-element.15) | copy-start | bytes 1966084
  89.1 14.0 %copy-start.2 = (bf16[320,1024]{1,0:T(8,128)(2,1)}, bf16[320,1024]{1,0:T(8,128)(2,1)S(1)}, u32[]{:S(2)}) copy-start(bf16[320,1024]{1,0:T(8,128)(2,1)S(1)} %get-tuple-element.14) | copy-start | bytes 1966084
  127.5 1.1 copy-start.5
  127.6 261.4 %reduce-scatter.4.cloned.1.call-start = ((), (), s32[]{:S(2)}) async-start(), calls=%async_computation.4 | async-start | bytes 2949120 | tf_op jit(solution)/shard_map/reduce_scatter | solution.py:26
  136.2 1.1 copy-start.3
  136.2 292.0 %reduce-scatter.6.cloned.1.call-start = ((), (), s32[]{:S(2)}) async-start(), calls=%async_computation.6 | async-start | bytes 2949120 | tf_op jit(solution)/shard_map/reduce_scatter | solution.py:37
Sparse Core Ops, SparseCore 0:
  9.6 36.5 all-gather.2
  47.9 32.8 all-gather.4
  127.7 220.8 reduce-scatter.7
  351.4 37.4 reduce-scatter.3
  391.7 36.4 reduce-scatter.5
where the time goes:
time: 435 us
  waiting for transfers between devices  321 us (74%)
  matrix products  68.3 us (16%)
  other arithmetic  17.6 us (4%)
  local copies, waits for them, and re-layouts  14.1 us (3%)
  between operations  13.8 us (3%)
    reduce_scatter x1, waiting for transfers between devices, on_device(): lax.psum_scatter(jnp.concatenate([contract_rows(gathered, dgate), contrac...  195 us
    reduce_scatter x1, waiting for transfers between devices, on_device(): lax.psum_scatter((contract_cols(dgate, w_gate) + contract_cols(dup, w_up)...  39.3 us
    all_gather x1, waiting for transfers between devices, on_device(): gathered = lax.all_gather(tokens, 'mp', axis=0, tiled=True)  37.6 us
    reduce_scatter x1, waiting for transfers between devices, on_device(): lax.psum_scatter(jnp.dot(hidden, w_down, preferred_element_type=jnp.float...  28.3 us
    dot_general x3, matrix products, contract_cols(): lax.dot_general(left, right, (((1,), (1,)), ((), ())), preferred_element_...  24.2 us
    dot_general x3, matrix products, contract_rows(): lax.dot_general(left, right, (((0,), (0,)), ((), ())), preferred_element_...  20.8 us
    all_gather x1, waiting for transfers between devices, on_device(): upstream = lax.all_gather(cotangent, 'mp', axis=0, tiled=True)  18.8 us
    concatenate x1, other arithmetic, on_device(): jnp.concatenate([contract_rows(gathered, dgate), contract_rows(gathered,...  17.6 us
  transfers between devices with their start and end apart: 5, of which 5 were waited for; matrix products, arithmetic and copies ran while one was open for 12% of the time, Pallas kernels for 0%

commit v1 on v0

v1 whole, which is shorter than its diff:
```python
import functools

import jax
import jax.numpy as jnp
from jax import lax
from jax.experimental import pallas as pl
from jax.experimental.pallas import tpu as pltpu
from jax.sharding import PartitionSpec as P

CORES = 2
MIB = 1 << 20


def contract_rows(left, right):
    return lax.dot_general(
        left, right, (((0,), (0,)), ((), ())), preferred_element_type=jnp.float32
    )


def contract_cols(left, right):
    return lax.dot_general(
        left, right, (((1,), (1,)), ((), ())), preferred_element_type=jnp.float32
    )


def product(left, right):
    return jnp.dot(left, right, preferred_element_type=jnp.float32)


def after(value, earlier):
    return lax.optimization_barrier((value, earlier))[0]


SMEM = pl.BlockSpec(memory_space=pltpu.SMEM)
ANY = pl.BlockSpec(memory_space=pl.ANY)


def call(body, steps, ins, in_specs, outs, out_specs, scratch=()):
    return pl.pallas_call(
        body,
        grid=(steps,),
        in_specs=in_specs,
        out_specs=out_specs,
        out_shape=outs,
        scratch_shapes=scratch,
        compiler_params=pltpu.CompilerParams(vmem_limit_bytes=56 * MIB),
        cost_estimate=pl.CostEstimate(flops=0, bytes_accessed=0, transcendentals=0),
    )(*ins)


def whole(array):
    return pl.BlockSpec(array.shape, lambda i: (0,) * len(array.shape))


def out_columns(rows, width):
    return jax.ShapeDtypeStruct((rows, width), jnp.bfloat16)


CHUNK = 64
SPLIT = 2


class Stream:
    def __init__(self, weights, axis, block):
        self.axis, self.block, self.count = axis, block, len(weights)
        self.steps = weights[0].shape[axis] // block
        shape = list(weights[0].shape)
        shape[axis] = block
        slots = (self.count, self.steps)
        self.scratch = (
            pltpu.VMEM((*slots, *shape), weights[0].dtype),
            pltpu.SemaphoreType.DMA((*slots, SPLIT)),
        )

    def copies(self, step, refs, held, sems):
        at = step * self.block
        at = pl.ds(at if isinstance(at, int) else pl.multiple_of(at, self.block), self.block)
        rows = held.shape[2] // SPLIT
        for w, ref in enumerate(refs):
            block = ref.at[:, at] if self.axis else ref.at[at]
            for part in range(SPLIT):
                some = pl.ds(part * rows, rows)
                yield pltpu.make_async_copy(
                    block.at[some], held.at[w, step, some], sems.at[w, step, part]
                )

    def begin(self, refs, held, sems, steps):
        for step in steps:
            for copy in self.copies(step, refs, held, sems):
                copy.start()

    def blocks(self, refs, held, sems):
        step = pl.program_id(0)
        for copy in self.copies(step, refs, held, sems):
            copy.wait()
        return [held[w, step] for w in range(self.count)]


class Gathered:
    def __init__(self, rows):
        self.rows = rows
        self.scratch = (
            pltpu.VMEM(rows.shape, rows.dtype),
            pltpu.SemaphoreType.DMA((rows.shape[0] // CHUNK,)),
        )

    def fill(self, ref, x_ref, sems, then):
        copies = []
        for i in range(x_ref.shape[0] // CHUNK):
            at = pl.ds(i * CHUNK, CHUNK)
            copies.append(pltpu.make_async_copy(ref.at[at], x_ref.at[at], sems.at[i]))
        for copy in copies:
            copy.start()
        then()
        for copy in copies:
            copy.wait()


def hand_out_body(orders, where_ref, rows_ref, *refs):
    *outs, sems = refs
    core, group = where_ref[1], where_ref[2]
    copies = []
    for out, j0, j1 in zip(outs, orders[0][1:], orders[1][1:]):
        half, width = out.shape
        at = (group ^ jnp.where(core == 0, j0, j1)) * width
        at = pl.ds(pl.multiple_of(at, width), width)
        rows = pl.ds(pl.multiple_of(core * half, half), half)
        copies.append(
            pltpu.make_async_copy(rows_ref.at[rows, at], out, sems.at[len(copies)])
        )
    for copy in copies:
        copy.start()
    for copy in copies:
        copy.wait()


def hand_out(where, rows, groups):
    block = out_columns(rows.shape[0] // CORES, rows.shape[1] // groups)
    count = groups - 1
    return call(
        functools.partial(hand_out_body, group_order(groups)),
        1,
        (where, rows),
        [SMEM, ANY],
        (block,) * count,
        (whole(block),) * count,
        (pltpu.SemaphoreType.DMA((count,)),),
    )


def forward_body(
    rows, weights, x_in, w_gate_ref, w_up_ref, hidden_ref, swish_ref, slope_ref, *scratch
):
    x_ref, x_sems, held, sems = scratch
    refs = (w_gate_ref, w_up_ref)

    @pl.when(pl.program_id(0) == 0)
    def _():
        weights.begin(refs, held, sems, [0])
        rest = range(1, weights.steps)
        rows.fill(x_in, x_ref, x_sems, lambda: weights.begin(refs, held, sems, rest))

    w_gate, w_up = weights.blocks(refs, held, sems)
    gate = product(x_ref[...], w_gate)
    up = product(x_ref[...], w_up)
    sigma = jax.nn.sigmoid(gate)
    swish = gate * sigma
    hidden_ref[...] = (swish * up).astype(hidden_ref.dtype)
    swish_ref[...] = swish
    slope_ref[...] = up * sigma * (1.0 + gate * (1.0 - sigma))


def forward(x, w_gate, w_up):
    rows, panel = x.shape[0], w_gate.shape[1]
    held, weights = Gathered(x), Stream((w_gate, w_up), 1, min(256, panel))
    out = pl.BlockSpec((rows, weights.block), lambda i: (0, i))
    kept = jax.ShapeDtypeStruct((rows, panel), jnp.float32)
    return call(
        functools.partial(forward_body, held, weights),
        weights.steps,
        (x, w_gate, w_up),
        [ANY] * 3,
        (out_columns(rows, panel), kept, kept),
        (out, out, out),
        held.scratch + weights.scratch,
    )


def project_body(weights, hidden_ref, w_ref, out_ref, held, sems):
    steps = range(weights.steps)
    pl.when(pl.program_id(0) == 0)(lambda: weights.begin((w_ref,), held, sems, steps))
    (w,) = weights.blocks((w_ref,), held, sems)
    out_ref[...] = product(hidden_ref[...], w).astype(out_ref.dtype)


def project(hidden, w_down):
    rows, depth = hidden.shape[0], w_down.shape[1]
    weights = Stream((w_down,), 1, min(1024, depth))
    return call(
        functools.partial(project_body, weights),
        weights.steps,
        (hidden, w_down),
        [whole(hidden), ANY],
        (jax.ShapeDtypeStruct((rows, depth), jnp.bfloat16),),
        (pl.BlockSpec((rows, weights.block), lambda i: (0, i)),),
        weights.scratch,
    )[0]


def backward_body(
    rows, weights, x_in, w_ref, swish_ref, slope_ref, dgate_ref, dup_ref, *scratch
):
    x_ref, x_sems, held, sems = scratch

    @pl.when(pl.program_id(0) == 0)
    def _():
        weights.begin((w_ref,), held, sems, [0])
        rest = range(1, weights.steps)
        rows.fill(
            x_in, x_ref, x_sems, lambda: weights.begin((w_ref,), held, sems, rest)
        )

    (w,) = weights.blocks((w_ref,), held, sems)
    dhidden = contract_cols(x_ref[...], w)
    dgate_ref[...] = (dhidden * slope_ref[...]).astype(dgate_ref.dtype)
    dup_ref[...] = (dhidden * swish_ref[...]).astype(dup_ref.dtype)


def backward(x, w_down, swish, slope):
    rows, panel = x.shape[0], w_down.shape[0]
    held, weights = Gathered(x), Stream((w_down,), 0, min(256, panel))
    part = pl.BlockSpec((rows, weights.block), lambda i: (0, i))
    return call(
        functools.partial(backward_body, held, weights),
        weights.steps,
        (x, w_down, swish, slope),
        [ANY, ANY, part, part],
        (out_columns(rows, panel),) * 2,
        (part, part),
        held.scratch + weights.scratch,
    )


def input_body(weights, dgate_ref, dup_ref, w_gate_ref, w_up_ref, out_ref, held, sems):
    refs = (w_gate_ref, w_up_ref)
    steps = range(weights.steps)
    pl.when(pl.program_id(0) == 0)(lambda: weights.begin(refs, held, sems, steps))
    w_gate, w_up = weights.blocks(refs, held, sems)
    total = contract_cols(dgate_ref[...], w_gate) + contract_cols(dup_ref[...], w_up)
    out_ref[...] = total.astype(out_ref.dtype)


def input_sum(dgate, dup, w_gate, w_up):
    rows, depth = dgate.shape[0], w_gate.shape[0]
    weights = Stream((w_gate, w_up), 0, min(512, depth))
    return call(
        functools.partial(input_body, weights),
        weights.steps,
        (dgate, dup, w_gate, w_up),
        [whole(dgate), whole(dup), ANY, ANY],
        (jax.ShapeDtypeStruct((rows, depth), jnp.bfloat16),),
        (pl.BlockSpec((rows, weights.block), lambda i: (0, i)),),
        weights.scratch,
    )[0]


def gradient_body(plans, counts, where_ref, *refs):
    out_ref, left_ref, right_ref, sems = refs[-4:]

    @pl.when(pl.program_id(0) == 0)
    def _():
        copies, first = [], 0
        for plan, count, held in zip(plans, counts, (left_ref, right_ref)):
            for source, at in plan(where_ref, *refs[first : first + count]):
                rows = source.shape[0]
                target = held.at[pl.ds(pl.multiple_of(at, 16), rows)]
                copies.append(
                    pltpu.make_async_copy(source, target, sems.at[len(copies)])
                )
            first += count
        for copy in copies:
            copy.start()
        for copy in copies:
            copy.wait()

    block = out_ref.shape[0]
    at = pl.ds(pl.multiple_of(pl.program_id(0) * block, block), block)
    total = contract_rows(left_ref[:, at], right_ref[...])
    out_ref[...] = total.astype(out_ref.dtype)


def gradient(where, plans, lefts, rights, depth, shape):
    block = min(256, shape[0])
    counts = (len(lefts), len(rights))
    return call(
        functools.partial(gradient_body, plans, counts),
        shape[0] // block,
        (where, *lefts, *rights),
        [SMEM] + [ANY] * sum(counts),
        (jax.ShapeDtypeStruct(shape, jnp.bfloat16),),
        (pl.BlockSpec((block, shape[1]), lambda i: (i, 0)),),
        (
            pltpu.VMEM((depth, shape[0]), jnp.bfloat16),
            pltpu.VMEM((depth, shape[1]), jnp.bfloat16),
            pltpu.SemaphoreType.DMA((32,)),
        ),
    )[0]


def pieces_plan(where_ref, *pieces):
    copies, at = [], 0
    for piece in pieces:
        copies.append((piece, at))
        at += piece.shape[0]
    return copies


def columns_plan(where_ref, gathered, *blocks):
    core, group, count = where_ref[1], where_ref[2], len(blocks) // 2
    rows, half, width = gathered.shape[0], *blocks[0].shape
    at = pl.ds(pl.multiple_of(group * width, width), width)
    copies = [(gathered.at[:, at], 0)]
    for label in range(1, count + 1):
        mine = blocks[label - 1]
        theirs = blocks[count + reverse(label, count + 1) - 1]
        copies.append((mine, label * rows + core * half))
        copies.append((theirs, label * rows + (1 - core) * half))
    return copies


def reverse(label, count):
    bits = count.bit_length() - 1
    return sum(1 << (bits - 1 - b) for b in range(bits) if label >> b & 1)


def swap_cores(value, chips):
    pairs = [(i, i ^ 1) for i in range(CORES * chips)]
    return lax.ppermute(value, "mp", pairs)


class Chain:
    def __init__(self, steps, *given):
        next(steps)
        self.steps, self.held, self.done = steps, given, False

    def advance(self):
        if not self.done:
            try:
                self.held = self.steps.send(self.held)
            except StopIteration as stop:
                self.held, self.done = stop.value, True


def fence(chains, *values):
    held, values = lax.optimization_barrier(([c.held for c in chains], values))
    for chain, value in zip(chains, held):
        chain.held = value
    return values


def group_order(groups):
    bits = [1 << b for b in range(groups.bit_length() - 1)]
    orders = []
    for c in range(CORES):
        held = [0]
        for bit in bits if c == 0 else bits[::-1]:
            held = held + [j ^ bit for j in held]
        orders.append(held)
    return orders


def group_pairs(ups, groups, members):
    return [
        (g * members + m, (g ^ ups[m % CORES]) * members + m)
        for g in range(groups)
        for m in range(members)
    ]


def gather_groups(groups, members, held, *plan):
    held += yield
    bits = [1 << b for b in range(groups.bit_length() - 1)]
    steps = list(zip(bits, bits[::-1]))
    for labels in plan:
        first = len(held)
        for label in labels:
            top = label.bit_length() - 1
            pairs = group_pairs(steps[top], groups, members)
            held.append(lax.ppermute(held[label - (1 << top)], ("dp", "mp"), pairs))
        held[first:] = yield held[first:]
    return ()


def exchange_groups(groups, members, mine, theirs):
    blocks = yield
    mine.update(enumerate(blocks, 1))
    bits = [1 << b for b in range(groups.bit_length() - 1)]
    ways = [group_pairs(ups, groups, members) for ups in zip(bits, bits[::-1])]
    left = {at: [w for b, w in zip(bits, ways) if at & b] for at in mine}
    while len(theirs) < len(mine):
        moved = [at for at in mine if left[at]]
        ready = [at for at in mine if not left[at] and at not in theirs]
        came = yield (
            [lax.ppermute(mine[at], ("dp", "mp"), left[at].pop(0)) for at in moved],
            [swap_cores(mine[at], members // CORES) for at in ready],
        )
        mine.update(zip(moved, came[0]))
        theirs.update(zip(ready, came[1]))
    return ()


def on_device(groups, members, tokens, w_gate, w_up, w_down, cotangent):
    group = lax.axis_index("dp")
    place = lax.axis_index("mp") // CORES
    core = lax.rem(lax.axis_index("mp"), CORES)
    where = jnp.stack([place, core, group])
    width = tokens.shape[1] // groups
    phases = groups.bit_length() - 1
    last = groups - 1

    def from_line(value):
        return lax.all_gather(value, "mp", axis=0, tiled=True)

    def over_line(value):
        return lax.psum_scatter(value, "mp", scatter_dimension=0, tiled=True)

    def over_groups(value, held, *plan):
        return Chain(gather_groups(groups, members, held, *plan), value)

    def exchange(blocks, mine, theirs):
        return Chain(exchange_groups(groups, members, mine, theirs), *blocks)

    def columns(gathered, mine, theirs):
        labels = range(1, groups)
        return (gathered, *(mine[at] for at in labels), *(theirs[at] for at in labels))

    upstream = from_line(cotangent)
    (gathered,) = fence([], from_line(tokens))

    blocks = hand_out(where, gathered, groups)
    all_hidden, mine, theirs = [], {}, {}
    across = exchange(blocks, mine, theirs)
    across.advance()
    hidden, swish, slope = fence(
        [across], *forward(after(gathered, blocks), w_gate, w_up)
    )

    hiddens = over_groups(hidden, all_hidden, [1], range(2, last), [last])
    hiddens.advance()
    for _ in range(phases - 1):
        across.advance()
    (partial,) = fence([hiddens, across], project(hidden, w_down))

    hiddens.advance()
    upstream, partial = fence([across], upstream, partial)
    mixed = over_line(partial)

    blocks = hand_out(where, upstream, groups)
    all_dgate, all_dup, mine_up, theirs_up = [], [], {}, {}
    across_up = exchange(blocks, mine_up, theirs_up)
    across_up.advance()
    dgate, dup = backward(after(upstream, blocks), w_down, swish, slope)
    dgate, dup = fence([hiddens, across, across_up], dgate, dup)

    gates = over_groups(dgate, all_dgate, [1], range(2, groups))
    ups = over_groups(dup, all_dup, [1], range(2, groups))
    hiddens.advance()
    gates.advance()
    for _ in range(phases - 1):
        across_up.advance()
    (partial,) = fence(
        [gates, hiddens, across, across_up], input_sum(dgate, dup, w_gate, w_up)
    )
    input_grad = over_line(partial)

    hiddens.advance()
    gates.advance()
    across.advance()
    across_up.advance()
    (mark,) = fence([gates, hiddens, across, across_up], partial)
    gates.advance()
    across.advance()
    across_up.advance()

    depth = groups * hidden.shape[0]
    shape = (width, hidden.shape[1])
    plans = (columns_plan, pieces_plan)
    ins = columns(gathered, mine, theirs)
    ups.advance()
    grad_gate = gradient(where, plans, after(ins, mark), all_dgate, depth, shape)
    (grad_gate,) = fence([ups], grad_gate)

    ups.advance()
    grad_down = gradient(
        where,
        plans[::-1],
        after(all_hidden, grad_gate),
        columns(upstream, mine_up, theirs_up),
        depth,
        shape[::-1],
    )
    (grad_down,) = fence([ups], grad_down)
    ups.advance()
    grad_up = gradient(where, plans, after(ins, grad_down), all_dup, depth, shape)
    return mixed, input_grad, grad_gate, grad_up, grad_down


def solution(mesh):
    in_specs = (
        P(("dp", "mp"), None),
        P(None, "mp"),
        P(None, "mp"),
        P("mp", None),
        P(("dp", "mp"), None),
    )
    out_specs = (
        P(("dp", "mp"), None),
        P(("dp", "mp"), None),
        P("dp", "mp"),
        P("dp", "mp"),
        P("mp", "dp"),
    )
    body = functools.partial(on_device, mesh.shape["dp"], mesh.shape["mp"])
    return jax.shard_map(
        body, mesh=mesh, in_specs=in_specs, out_specs=out_specs, check_vma=False
    )
```

time: 435 us -> 180 us (0.41)
  waiting for transfers between devices: 321 us -> 69.9 us
  Pallas kernels: 0 us -> 72 us
  matrix products: 68.3 us -> 0 us
  starting transfers between devices: 0.2 us -> 20.9 us
  other arithmetic: 17.6 us -> 0.64 us
  local copies, waits for them, and re-layouts: 14.1 us -> 1.77 us
    reduce_scatter x3 -> x2, waiting for transfers between devices: 263 us -> 0.04 us  [over_line(): return lax.psum_scatter(value, 'mp', scatter_dimension=0, tiled=True)]
    pallas_call x0 -> x9, Pallas kernels: none -> 72 us  [call(): pl.pallas_call(body, grid=(steps,), in_specs=in_specs, out_specs=out_spec...]
    dot_general x9 -> x0, matrix products: 68.3 us -> none  [the longest x3 24.2 us: contract_cols(): lax.dot_general(left, right, (((1,), (1,)), ((), ())), preferred_element_...]
    ppermute x0 -> x23, waiting for transfers between devices: none -> 31.6 us  [the longest x9 22.4 us: gather_groups(): held.append(lax.ppermute(held[label - (1 << top)], ('dp', 'mp'), pairs))]
    ppermute x0 -> x23, starting transfers between devices: none -> 20.8 us  [the longest x9 11.8 us: gather_groups(): held.append(lax.ppermute(held[label - (1 << top)], ('dp', 'mp'), pairs))]
    all_gather x2, waiting for transfers between devices: 56.4 us -> 36.9 us  [from_line(): return lax.all_gather(value, 'mp', axis=0, tiled=True)]
    concatenate x1 -> x0, other arithmetic: 17.6 us -> none  [on_device(): jnp.concatenate([contract_rows(gathered, dgate), contract_rows(gathered,...]
    unnamed x14 -> x40, local copies, waits for them, and re-layouts: 8.51 us -> 1.77 us
  transfers between devices with their start and end apart: 5 -> 27, of which waited for: 5 -> 9; matrix products, arithmetic and copies ran while one was open for 12% -> 0% of each run, Pallas kernels for 0% -> 40%
where the time goes in v1:
time: 180 us; the launch traced here: 179 us
  Pallas kernels  72 us (40%)
  waiting for transfers between devices  69.9 us (39%)
  starting transfers between devices  20.9 us (12%)
  between operations  14.2 us (8%)
    pallas_call x9, Pallas kernels, call(): pl.pallas_call(body, grid=(steps,), in_specs=in_specs, out_specs=out_spec...  72 us
    all_gather x2, waiting for transfers between devices, from_line(): return lax.all_gather(value, 'mp', axis=0, tiled=True)  36.9 us
    ppermute x9, waiting for transfers between devices, gather_groups(): held.append(lax.ppermute(held[label - (1 << top)], ('dp', 'mp'), pairs))  22.4 us
    ppermute x9, starting transfers between devices, gather_groups(): held.append(lax.ppermute(held[label - (1 << top)], ('dp', 'mp'), pairs))  11.8 us
    ppermute x8, waiting for transfers between devices, exchange_groups(): lax.ppermute(mine[at], ('dp', 'mp'), left[at].pop(0))  9.12 us
    ppermute x8, starting transfers between devices, exchange_groups(): lax.ppermute(mine[at], ('dp', 'mp'), left[at].pop(0))  7.46 us
  transfers between devices with their start and end apart: 27, of which 9 were waited for; matrix products, arithmetic and copies ran while one was open for 0% of the time, Pallas kernels for 40%

profile of v1, /device:TPU:0, one launch (start us, length us, event | category | flops | bytes accessed | tf_op | source)
XLA Modules:
  0.0 179.5 jit_solution(4238821182361906961)
XLA Ops:
  9.4 36.9 %all-gather.3.cloned.1.call-done.rows_ref.x_in.refs_0_ = bf16[320,4096]{1,0:T(8,128)(2,1)} async-done(((bf16[40,4096]{1,0:T(8,128)(2,1)}), bf16[320,4096]{1,0:T(8,128)(2,1)}) %all-gather.3.cloned.1.call-update) | async-done | bytes 2621456 | tf_op jit(solution)/shard_map/all_gather | solution.py:422
  46.3 2.8 %shard_map.92 = (bf16[160,1024]{1,0:T(8,128)(2,1)}, bf16[160,1024]{1,0:T(8,128)(2,1)}, bf16[160,1024]{1,0:T(8,128)(2,1)}) custom-call(s32[3]{0:T(128)} %pad_add_fusion.where_ref, bf16[320,4096]{1,0:T(8,128)(2,1)} %all-gather.3.cloned.1.call-done.rows_ref.x_in.refs_0_), custom_call_target="tpu_custom_call" | custom-call | tf_op jit(solution)/shard_map/pallas_call | solution.py:39
  49.1 1.5 collective-permute-start
  50.6 1.5 collective-permute-start.1
  52.6 14.3 %shard_map.93 = (bf16[320,1024]{1,0:T(8,128)(2,1)}, f32[320,1024]{1,0:T(8,128)}, f32[320,1024]{1,0:T(8,128)}) custom-call(bf16[320,4096]{1,0:T(8,128)(2,1)} %all-gather.3.cloned.1.call-done.rows_ref.x_in.refs_0_, bf16[4096,1024]{1,0:T(8,128)(2,1)} %w_gate_ref.3, bf16[4096,1024]{1,0:T(8,128)(2,1)} %w_up_ref.3), custom_call_target="tpu_custom_call" | custom-call | tf_op jit(solution)/shard_map/pallas_call | solution.py:39
  67.0 1.6 collective-permute-start.3
  69.7 7.1 %shard_map.94 = bf16[320,4096]{1,0:T(8,128)(2,1)} custom-call(bf16[320,1024]{1,0:T(8,128)(2,1)} %get-tuple-element.136.hidden_ref.refs_0_, bf16[1024,4096]{1,0:T(8,128)(2,1)} %w_ref.3), custom_call_target="tpu_custom_call" | custom-call | tf_op jit(solution)/shard_map/pallas_call | solution.py:39
  76.8 2.4 %collective-permute-done.4.refs_3_ = bf16[160,1024]{1,0:T(8,128)(2,1)S(1)} collective-permute-done((bf16[160,1024]{1,0:T(8,128)(2,1)S(1)}, bf16[160,1024]{1,0:T(8,128)(2,1)S(1)}, u32[]{:S(2)}, u32[]{:S(2)}) %collective-permute-start.4) | collective-permute-done | bytes 327712 | tf_op jit(solution)/shard_map/ppermute | solution.py:404
  79.3 1.7 collective-permute-done.3.refs_1_
  81.0 1.4 collective-permute-start.7
  82.4 2.8 %shard_map.95 = (bf16[160,1024]{1,0:T(8,128)(2,1)}, bf16[160,1024]{1,0:T(8,128)(2,1)}, bf16[160,1024]{1,0:T(8,128)(2,1)}) custom-call(s32[3]{0:T(128)} %pad_add_fusion.where_ref, bf16[320,4096]{1,0:T(8,128)(2,1)} %all-gather.5.cloned.1.call-done.rows_ref.x_in.refs_4_), custom_call_target="tpu_custom_call" | custom-call | tf_op jit(solution)/shard_map/pallas_call | solution.py:39
  85.3 1.5 collective-permute-start.8
  87.4 0.7 collective-permute-start.10
  88.1 1.3 collective-permute-start.12
  89.4 9.7 %shard_map.96 = (bf16[320,1024]{1,0:T(8,128)(2,1)}, bf16[320,1024]{1,0:T(8,128)(2,1)}) custom-call(bf16[320,4096]{1,0:T(8,128)(2,1)} %all-gather.5.cloned.1.call-done.rows_ref.x_in.refs_4_, bf16[1024,4096]{1,0:T(8,128)(2,1)} %w_ref.3, f32[320,1024]{1,0:T(8,128)} %get-tuple-element.103.swish_ref, f32[320,1024]{1,0:T(8,128)} %get-tuple-element.104.slope_ref), custom_call_target="tpu_custom_call" | custom-call | tf_op jit(solution)/shard_map/pallas_call | solution.py:39
  99.2 3.0 %collective-permute-done.9.refs_6_ = bf16[160,1024]{1,0:T(8,128)(2,1)S(1)} collective-permute-done((bf16[160,1024]{1,0:T(8,128)(2,1)}, bf16[160,1024]{1,0:T(8,128)(2,1)S(1)}, u32[]{:S(2)}, u32[]{:S(2)}) %collective-permute-start.9) | collective-permute-done | bytes 327712 | tf_op jit(solution)/shard_map/ppermute | solution.py:404
  102.2 1.1 collective-permute-done.10
  103.3 1.5 collective-permute-start.11
  105.9 11.3 %shard_map.97 = bf16[320,4096]{1,0:T(8,128)(2,1)} custom-call(bf16[320,1024]{1,0:T(8,128)(2,1)} %get-tuple-element.107.dgate_ref.refs_7_, bf16[320,1024]{1,0:T(8,128)(2,1)} %get-tuple-element.115.dup_ref.refs_7_, bf16[4096,1024]{1,0:T(8,128)(2,1)} %w_gate_ref.3, bf16[4096,1024]{1,0:T(8,128)(2,1)} %w_up_ref.3), custom_call_target="tpu_custom_call" | custom-call | tf_op jit(solution)/shard_map/pallas_call | solution.py:39
  117.2 2.5 %collective-permute-done.13.refs_7_ = bf16[160,1024]{1,0:T(8,128)(2,1)S(1)} collective-permute-done((bf16[160,1024]{1,0:T(8,128)(2,1)}, bf16[160,1024]{1,0:T(8,128)(2,1)S(1)}, u32[]{:S(2)}, u32[]{:S(2)}) %collective-permute-start.13) | collective-permute-done | bytes 327712 | tf_op jit(solution)/shard_map/ppermute | solution.py:404
  119.8 1.4 collective-permute-start.17
  121.9 1.3 collective-permute-start.16
  123.8 13.6 %collective-permute-done.17.refs_9_ = bf16[320,1024]{1,0:T(8,128)(2,1)S(1)} collective-permute-done((bf16[320,1024]{1,0:T(8,128)(2,1)S(1)}, bf16[320,1024]{1,0:T(8,128)(2,1)S(1)}, u32[]{:S(2)}, u32[]{:S(2)}) %collective-permute-start.17) | collective-permute-done | bytes 655392 | tf_op jit(solution)/shard_map/ppermute | solution.py:389
  137.3 1.2 collective-permute-start.21
  138.5 6.0 %collective-permute-done.18.refs_10_ = bf16[320,1024]{1,0:T(8,128)(2,1)S(1)} collective-permute-done((bf16[320,1024]{1,0:T(8,128)(2,1)}, bf16[320,1024]{1,0:T(8,128)(2,1)S(1)}, u32[]{:S(2)}, u32[]{:S(2)}) %collective-permute-start.18) | collective-permute-done | bytes 655392 | tf_op jit(solution)/shard_map/ppermute | solution.py:389
  144.5 0.8 copy-done.14
  145.4 8.0 %shard_map.98 = bf16[1024,1024]{1,0:T(8,128)(2,1)} custom-call(s32[3]{0:T(128)} %pad_add_fusion.where_ref, bf16[320,4096]{1,0:T(8,128)(2,1)} %all-gather.3.cloned.1.call-done.rows_ref.x_in.refs_0_, bf16[160,1024]{1,0:T(8,128)(2,1)} %copy-done.3, bf16[160,1024]{1,0:T(8,128)(2,1)} %copy-done.4, bf16[160,1024]{1,0:T(8,128)(2,1)} %copy-done.5, ...), custom_call_target="tpu_custom_call" | custom-call | tf_op jit(solution)/shard_map/pallas_call | solution.py:39
  153.4 1.4 collective-permute-start.22
  154.8 8.0 %shard_map.99 = bf16[1024,1024]{1,0:T(8,128)(2,1)} custom-call(s32[3]{0:T(128)} %pad_add_fusion.where_ref, bf16[320,1024]{1,0:T(8,128)(2,1)} %get-tuple-element.136.hidden_ref.refs_0_, bf16[320,1024]{1,0:T(8,128)(2,1)} %collective-permute-done.3.refs_1_, bf16[320,1024]{1,0:T(8,128)(2,1)} %copy-done.9, bf16[320,1024]{1,0:T(8,128)(2,1)} %copy-done.10, ...), custom_call_target="tpu_custom_call" | custom-call | tf_op jit(solution)/shard_map/pallas_call | solution.py:39
  162.8 1.2 collective-permute-done.22.refs_10_
  164.1 0.9 copy-done.15
  164.9 8.0 %shard_map.100 = bf16[1024,1024]{1,0:T(8,128)(2,1)} custom-call(s32[3]{0:T(128)} %pad_add_fusion.where_ref, bf16[320,4096]{1,0:T(8,128)(2,1)} %all-gather.3.cloned.1.call-done.rows_ref.x_in.refs_0_, bf16[160,1024]{1,0:T(8,128)(2,1)} %copy-done.3, bf16[160,1024]{1,0:T(8,128)(2,1)} %copy-done.4, bf16[160,1024]{1,0:T(8,128)(2,1)} %copy-done.5, ...), custom_call_target="tpu_custom_call" | custom-call | tf_op jit(solution)/shard_map/pallas_call | solution.py:39
  (76 shorter events, 6.8 us)
Async XLA Ops:
  7.2 39.1 %all-gather.3.cloned.1.call-start = ((), (), s32[]{:S(2)}) async-start(), calls=%async_computation.2 | async-start | bytes 2949120 | tf_op jit(solution)/shard_map/all_gather | solution.py:422
  7.9 73.0 %all-gather.5.cloned.1.call-start = ((), (), s32[]{:S(2)}) async-start(), calls=%async_computation.3 | async-start | bytes 2949120 | tf_op jit(solution)/shard_map/all_gather | solution.py:422
  8.6 164.3 %reduce-scatter.3.cloned.1.call-start = ((), (), s32[]{:S(2)}) async-start(), calls=%async_computation.4 | async-start | bytes 2949120 | tf_op jit(solution)/shard_map/reduce_scatter | solution.py:425
  49.1 17.9 %collective-permute-start = (bf16[160,1024]{1,0:T(8,128)(2,1)}, bf16[160,1024]{1,0:T(8,128)(2,1)S(1)}, u32[]{:S(2)}, u32[]{:S(2)}) collective-permute-start(bf16[160,1024]{1,0:T(8,128)(2,1)} %get-tuple-element.79), channel_id=1, source_target_pairs={{0,8},{1,17},{2,10},{3,19},{4,12},{5,21},{6,14},{7,23},{8,0},{9,25... | collective-permute-start | bytes 983048 | tf_op jit(solution)/shard_map/ppermute | solution.py:404
  50.6 16.4 %collective-permute-start.1 = (bf16[160,1024]{1,0:T(8,128)(2,1)}, bf16[160,1024]{1,0:T(8,128)(2,1)S(1)}, u32[]{:S(2)}, u32[]{:S(2)}) collective-permute-start(bf16[160,1024]{1,0:T(8,128)(2,1)} %get-tuple-element.80), channel_id=1, source_target_pairs={{0,16},{1,9},{2,18},{3,11},{4,20},{5,13},{6,22},{7,15},{8,24},{9,1... | collective-permute-start | bytes 983048 | tf_op jit(solution)/shard_map/ppermute | solution.py:404
  52.1 14.9 %collective-permute-start.2 = (bf16[160,1024]{1,0:T(8,128)(2,1)}, bf16[160,1024]{1,0:T(8,128)(2,1)S(1)}, u32[]{:S(2)}, u32[]{:S(2)}) collective-permute-start(bf16[160,1024]{1,0:T(8,128)(2,1)} %get-tuple-element.81), channel_id=1, source_target_pairs={{0,8},{1,17},{2,10},{3,19},{4,12},{5,21},{6,14},{7,23},{8,0},{9,25... | collective-permute-start | bytes 983048 | tf_op jit(solution)/shard_map/ppermute | solution.py:404
  67.0 13.9 %collective-permute-start.3 = (bf16[320,1024]{1,0:T(8,128)(2,1)}, bf16[320,1024]{1,0:T(8,128)(2,1)}, u32[]{:S(2)}, u32[]{:S(2)}) collective-permute-start(bf16[320,1024]{1,0:T(8,128)(2,1)} %get-tuple-element.136.hidden_ref.refs_0_), channel_id=1, source_target_pairs={{0,8},{1,17},{2,10},{3,19},{4,12},{5,21},{6,14},{7,23},{8,0},{9,25... | collective-permute-start | bytes 1966088 | tf_op jit(solution)/shard_map/ppermute | solution.py:389
  68.6 10.6 %collective-permute-start.4 = (bf16[160,1024]{1,0:T(8,128)(2,1)S(1)}, bf16[160,1024]{1,0:T(8,128)(2,1)S(1)}, u32[]{:S(2)}, u32[]{:S(2)}) collective-permute-start(bf16[160,1024]{1,0:T(8,128)(2,1)S(1)} %collective-permute-done.2), channel_id=1, source_target_pairs={{0,16},{1,9},{2,18},{3,11},{4,20},{5,13},{6,22},{7,15},{8,24},{9,1... | collective-permute-start | bytes 983048 | tf_op jit(solution)/shard_map/ppermute | solution.py:404
  69.1 10.1 %collective-permute-start.5 = (bf16[160,1024]{1,0:T(8,128)(2,1)S(1)}, bf16[160,1024]{1,0:T(8,128)(2,1)S(1)}, u32[]{:S(2)}, u32[]{:S(2)}) collective-permute-start(bf16[160,1024]{1,0:T(8,128)(2,1)S(1)} %collective-permute-done.refs_1_), channel_id=1, source_target_pairs={{0,1},{1,0},{2,3},{3,2},{4,5},{5,4},{6,7},{7,6},{8,9},{9,8},{10,11... | collective-permute-start | bytes 983048 | tf_op jit(solution)/shard_map/ppermute | solution.py:338
  69.1 10.1 %collective-permute-start.6 = (bf16[160,1024]{1,0:T(8,128)(2,1)S(1)}, bf16[160,1024]{1,0:T(8,128)(2,1)S(1)}, u32[]{:S(2)}, u32[]{:S(2)}) collective-permute-start(bf16[160,1024]{1,0:T(8,128)(2,1)S(1)} %collective-permute-done.1.refs_2_), channel_id=1, source_target_pairs={{0,1},{1,0},{2,3},{3,2},{4,5},{5,4},{6,7},{7,6},{8,9},{9,8},{10,11... | collective-permute-start | bytes 983048 | tf_op jit(solution)/shard_map/ppermute | solution.py:338
  79.2 44.0 %copy-start.5 = (bf16[160,1024]{1,0:T(8,128)(2,1)}, bf16[160,1024]{1,0:T(8,128)(2,1)S(1)}, u32[]{:S(2)}) copy-start(bf16[160,1024]{1,0:T(8,128)(2,1)S(1)} %collective-permute-done.4.refs_3_) | copy-start | bytes 983044
  81.0 92.0 %reduce-scatter.5.cloned.1.call-start = ((), (), s32[]{:S(2)}) async-start(), calls=%async_computation.5 | async-start | bytes 2949120 | tf_op jit(solution)/shard_map/reduce_scatter | solution.py:425
  81.0 18.1 %collective-permute-start.7 = (bf16[320,1024]{1,0:T(8,128)(2,1)S(1)}, bf16[320,1024]{1,0:T(8,128)(2,1)S(1)}, u32[]{:S(2)}, u32[]{:S(2)}) collective-permute-start(bf16[320,1024]{1,0:T(8,128)(2,1)S(1)} %copy-done), channel_id=1, source_target_pairs={{0,16},{1,9},{2,18},{3,11},{4,20},{5,13},{6,22},{7,15},{8,24},{9,1... | collective-permute-start | bytes 1966088 | tf_op jit(solution)/shard_map/ppermute | solution.py:389
  85.3 13.9 %collective-permute-start.8 = (bf16[160,1024]{1,0:T(8,128)(2,1)}, bf16[160,1024]{1,0:T(8,128)(2,1)S(1)}, u32[]{:S(2)}, u32[]{:S(2)}) collective-permute-start(bf16[160,1024]{1,0:T(8,128)(2,1)} %get-tuple-element.99), channel_id=1, source_target_pairs={{0,8},{1,17},{2,10},{3,19},{4,12},{5,21},{6,14},{7,23},{8,0},{9,25... | collective-permute-start | bytes 983048 | tf_op jit(solution)/shard_map/ppermute | solution.py:404
  86.8 15.4 %collective-permute-start.9 = (bf16[160,1024]{1,0:T(8,128)(2,1)}, bf16[160,1024]{1,0:T(8,128)(2,1)S(1)}, u32[]{:S(2)}, u32[]{:S(2)}) collective-permute-start(bf16[160,1024]{1,0:T(8,128)(2,1)} %get-tuple-element.100), channel_id=1, source_target_pairs={{0,16},{1,9},{2,18},{3,11},{4,20},{5,13},{6,22},{7,15},{8,24},{9,1... | collective-permute-start | bytes 983048 | tf_op jit(solution)/shard_map/ppermute | solution.py:404
  87.4 16.0 %collective-permute-start.10 = (bf16[160,1024]{1,0:T(8,128)(2,1)}, bf16[160,1024]{1,0:T(8,128)(2,1)}, u32[]{:S(2)}, u32[]{:S(2)}) collective-permute-start(bf16[160,1024]{1,0:T(8,128)(2,1)} %get-tuple-element.101), channel_id=1, source_target_pairs={{0,8},{1,17},{2,10},{3,19},{4,12},{5,21},{6,14},{7,23},{8,0},{9,25... | collective-permute-start | bytes 983048 | tf_op jit(solution)/shard_map/ppermute | solution.py:404
  88.1 29.2 %collective-permute-start.12 = (bf16[320,1024]{1,0:T(8,128)(2,1)}, bf16[320,1024]{1,0:T(8,128)(2,1)S(1)}, u32[]{:S(2)}, u32[]{:S(2)}) collective-permute-start(bf16[320,1024]{1,0:T(8,128)(2,1)} %collective-permute-done.3.refs_1_), channel_id=1, source_target_pairs={{0,16},{1,9},{2,18},{3,11},{4,20},{5,13},{6,22},{7,15},{8,24},{9,1... | collective-permute-start | bytes 1966088 | tf_op jit(solution)/shard_map/ppermute | solution.py:389
  99.2 18.0 %copy-start.16 = (bf16[160,1024]{1,0:T(8,128)(2,1)}, bf16[160,1024]{1,0:T(8,128)(2,1)S(1)}, u32[]{:S(2)}) copy-start(bf16[160,1024]{1,0:T(8,128)(2,1)S(1)} %collective-permute-done.8.refs_5_) | copy-start | bytes 983044
  103.3 16.4 %collective-permute-start.11 = (bf16[320,1024]{1,0:T(8,128)(2,1)}, bf16[320,1024]{1,0:T(8,128)(2,1)}, u32[]{:S(2)}, u32[]{:S(2)}) collective-permute-start(bf16[320,1024]{1,0:T(8,128)(2,1)} %get-tuple-element.107.dgate_ref.refs_7_), channel_id=1, source_target_pairs={{0,8},{1,17},{2,10},{3,19},{4,12},{5,21},{6,14},{7,23},{8,0},{9,25... | collective-permute-start | bytes 1966088 | tf_op jit(solution)/shard_map/ppermute | solution.py:389
  104.8 15.0 %collective-permute-start.13 = (bf16[160,1024]{1,0:T(8,128)(2,1)}, bf16[160,1024]{1,0:T(8,128)(2,1)S(1)}, u32[]{:S(2)}, u32[]{:S(2)}) collective-permute-start(bf16[160,1024]{1,0:T(8,128)(2,1)} %collective-permute-done.10), channel_id=1, source_target_pairs={{0,16},{1,9},{2,18},{3,11},{4,20},{5,13},{6,22},{7,15},{8,24},{9,1... | collective-permute-start | bytes 983048 | tf_op jit(solution)/shard_map/ppermute | solution.py:404
  105.3 14.4 %collective-permute-start.14 = (bf16[160,1024]{1,0:T(8,128)(2,1)S(1)}, bf16[160,1024]{1,0:T(8,128)(2,1)}, u32[]{:S(2)}, u32[]{:S(2)}) collective-permute-start(bf16[160,1024]{1,0:T(8,128)(2,1)S(1)} %collective-permute-done.8.refs_5_), channel_id=1, source_target_pairs={{0,1},{1,0},{2,3},{3,2},{4,5},{5,4},{6,7},{7,6},{8,9},{9,8},{10,11... | collective-permute-start | bytes 983048 | tf_op jit(solution)/shard_map/ppermute | solution.py:338
  105.3 14.4 %collective-permute-start.15 = (bf16[160,1024]{1,0:T(8,128)(2,1)S(1)}, bf16[160,1024]{1,0:T(8,128)(2,1)}, u32[]{:S(2)}, u32[]{:S(2)}) collective-permute-start(bf16[160,1024]{1,0:T(8,128)(2,1)S(1)} %collective-permute-done.9.refs_6_), channel_id=1, source_target_pairs={{0,1},{1,0},{2,3},{3,2},{4,5},{5,4},{6,7},{7,6},{8,9},{9,8},{10,11... | collective-permute-start | bytes 983048 | tf_op jit(solution)/shard_map/ppermute | solution.py:338
  117.2 36.1 %copy-start.10 = (bf16[320,1024]{1,0:T(8,128)(2,1)}, bf16[320,1024]{1,0:T(8,128)(2,1)S(1)}, u32[]{:S(2)}) copy-start(bf16[320,1024]{1,0:T(8,128)(2,1)S(1)} %collective-permute-done.12.refs_3_) | copy-start | bytes 1966084
  119.8 33.6 %copy-start.18 = (bf16[160,1024]{1,0:T(8,128)(2,1)}, bf16[160,1024]{1,0:T(8,128)(2,1)S(1)}, u32[]{:S(2)}) copy-start(bf16[160,1024]{1,0:T(8,128)(2,1)S(1)} %collective-permute-done.13.refs_7_) | copy-start | bytes 983044
  119.8 17.5 %collective-permute-start.17 = (bf16[320,1024]{1,0:T(8,128)(2,1)S(1)}, bf16[320,1024]{1,0:T(8,128)(2,1)S(1)}, u32[]{:S(2)}, u32[]{:S(2)}) collective-permute-start(bf16[320,1024]{1,0:T(8,128)(2,1)S(1)} %copy-done.2), channel_id=1, source_target_pairs={{0,16},{1,9},{2,18},{3,11},{4,20},{5,13},{6,22},{7,15},{8,24},{9,1... | collective-permute-start | bytes 1966088 | tf_op jit(solution)/shard_map/ppermute | solution.py:389
  121.2 23.3 %collective-permute-start.18 = (bf16[320,1024]{1,0:T(8,128)(2,1)}, bf16[320,1024]{1,0:T(8,128)(2,1)S(1)}, u32[]{:S(2)}, u32[]{:S(2)}) collective-permute-start(bf16[320,1024]{1,0:T(8,128)(2,1)} %collective-permute-done.11.refs_8_), channel_id=1, source_target_pairs={{0,16},{1,9},{2,18},{3,11},{4,20},{5,13},{6,22},{7,15},{8,24},{9,1... | collective-permute-start | bytes 1966088 | tf_op jit(solution)/shard_map/ppermute | solution.py:389
  121.9 31.5 %collective-permute-start.16 = (bf16[320,1024]{1,0:T(8,128)(2,1)S(1)}, bf16[320,1024]{1,0:T(8,128)(2,1)S(1)}, u32[]{:S(2)}, u32[]{:S(2)}) collective-permute-start(bf16[320,1024]{1,0:T(8,128)(2,1)S(1)} %copy-done.1), channel_id=1, source_target_pairs={{0,8},{1,17},{2,10},{3,19},{4,12},{5,21},{6,14},{7,23},{8,0},{9,25... | collective-permute-start | bytes 1966088 | tf_op jit(solution)/shard_map/ppermute | solution.py:389
  123.2 15.3 %collective-permute-start.19 = (bf16[160,1024]{1,0:T(8,128)(2,1)S(1)}, bf16[160,1024]{1,0:T(8,128)(2,1)S(1)}, u32[]{:S(2)}, u32[]{:S(2)}) collective-permute-start(bf16[160,1024]{1,0:T(8,128)(2,1)S(1)} %collective-permute-done.4.refs_3_), channel_id=1, source_target_pairs={{0,1},{1,0},{2,3},{3,2},{4,5},{5,4},{6,7},{7,6},{8,9},{9,8},{10,11... | collective-permute-start | bytes 983048 | tf_op jit(solution)/shard_map/ppermute | solution.py:338
  123.2 15.3 %collective-permute-start.20 = (bf16[160,1024]{1,0:T(8,128)(2,1)S(1)}, bf16[160,1024]{1,0:T(8,128)(2,1)S(1)}, u32[]{:S(2)}, u32[]{:S(2)}) collective-permute-start(bf16[160,1024]{1,0:T(8,128)(2,1)S(1)} %collective-permute-done.13.refs_7_), channel_id=1, source_target_pairs={{0,1},{1,0},{2,3},{3,2},{4,5},{5,4},{6,7},{7,6},{8,9},{9,8},{10,11... | collective-permute-start | bytes 983048 | tf_op jit(solution)/shard_map/ppermute | solution.py:338
  137.3 25.5 %collective-permute-start.21 = (bf16[320,1024]{1,0:T(8,128)(2,1)S(1)}, bf16[320,1024]{1,0:T(8,128)(2,1)S(1)}, u32[]{:S(2)}, u32[]{:S(2)}) collective-permute-start(bf16[320,1024]{1,0:T(8,128)(2,1)S(1)} %copy-done.1), channel_id=1, source_target_pairs={{0,16},{1,9},{2,18},{3,11},{4,20},{5,13},{6,22},{7,15},{8,24},{9,1... | collective-permute-start | bytes 1966088 | tf_op jit(solution)/shard_map/ppermute | solution.py:389
  138.5 16.3 %copy-start.19 = (bf16[160,1024]{1,0:T(8,128)(2,1)}, bf16[160,1024]{1,0:T(8,128)(2,1)S(1)}, u32[]{:S(2)}) copy-start(bf16[160,1024]{1,0:T(8,128)(2,1)S(1)} %collective-permute-done.20.refs_10_) | copy-start | bytes 983044
  153.4 10.7 %collective-permute-start.22 = (bf16[320,1024]{1,0:T(8,128)(2,1)S(1)}, bf16[320,1024]{1,0:T(8,128)(2,1)S(1)}, u32[]{:S(2)}, u32[]{:S(2)}) collective-permute-start(bf16[320,1024]{1,0:T(8,128)(2,1)S(1)} %collective-permute-done.16.refs_8_), channel_id=1, source_target_pairs={{0,16},{1,9},{2,18},{3,11},{4,20},{5,13},{6,22},{7,15},{8,24},{9,1... | collective-permute-start | bytes 1966088 | tf_op jit(solution)/shard_map/ppermute | solution.py:389
  (15 other events, 90.4 us)
Sparse Core Ops, SparseCore 0:
  9.6 36.5 all-gather.2
  47.9 32.8 all-gather.4
  83.7 36.4 reduce-scatter.2
  122.9 36.5 reduce-scatter.4

commit v2 on v1

--- a/solution.py
+++ b/solution.py
@@ -57,6 +57,7 @@
 
 
 CHUNK = 64
+AHEAD = 2
 SPLIT = 2
 
 
@@ -91,6 +92,12 @@
 
     def blocks(self, refs, held, sems):
         step = pl.program_id(0)
+
+        @pl.when(step + AHEAD < self.steps)
+        def _():
+            for copy in self.copies(step + AHEAD, refs, held, sems):
+                copy.start()
+
         for copy in self.copies(step, refs, held, sems):
             copy.wait()
         return [held[w, step] for w in range(self.count)]
@@ -157,7 +164,7 @@
     @pl.when(pl.program_id(0) == 0)
     def _():
         weights.begin(refs, held, sems, [0])
-        rest = range(1, weights.steps)
+        rest = range(1, min(AHEAD, weights.steps))
         rows.fill(x_in, x_ref, x_sems, lambda: weights.begin(refs, held, sems, rest))
 
     w_gate, w_up = weights.blocks(refs, held, sems)
@@ -187,7 +194,7 @@
 
 
 def project_body(weights, hidden_ref, w_ref, out_ref, held, sems):
-    steps = range(weights.steps)
+    steps = range(min(AHEAD, weights.steps))
     pl.when(pl.program_id(0) == 0)(lambda: weights.begin((w_ref,), held, sems, steps))
     (w,) = weights.blocks((w_ref,), held, sems)
     out_ref[...] = product(hidden_ref[...], w).astype(out_ref.dtype)
@@ -215,7 +222,7 @@
     @pl.when(pl.program_id(0) == 0)
     def _():
         weights.begin((w_ref,), held, sems, [0])
-        rest = range(1, weights.steps)
+        rest = range(1, min(AHEAD, weights.steps))
         rows.fill(
             x_in, x_ref, x_sems, lambda: weights.begin((w_ref,), held, sems, rest)
         )
@@ -243,7 +250,7 @@
 
 def input_body(weights, dgate_ref, dup_ref, w_gate_ref, w_up_ref, out_ref, held, sems):
     refs = (w_gate_ref, w_up_ref)
-    steps = range(weights.steps)
+    steps = range(min(AHEAD, weights.steps))
     pl.when(pl.program_id(0) == 0)(lambda: weights.begin(refs, held, sems, steps))
     w_gate, w_up = weights.blocks(refs, held, sems)
     total = contract_cols(dgate_ref[...], w_gate) + contract_cols(dup_ref[...], w_up)
@@ -252,7 +259,7 @@
 
 def input_sum(dgate, dup, w_gate, w_up):
     rows, depth = dgate.shape[0], w_gate.shape[0]
-    weights = Stream((w_gate, w_up), 0, min(512, depth))
+    weights = Stream((w_gate, w_up), 0, min(1024, depth))
     return call(
         functools.partial(input_body, weights),
         weights.steps,
@@ -475,33 +482,33 @@
 
     hiddens.advance()
     gates.advance()
+    ups.advance()
     across.advance()
     across_up.advance()
-    (mark,) = fence([gates, hiddens, across, across_up], partial)
-    gates.advance()
+    (mark,) = fence([hiddens, across, across_up], partial)
     across.advance()
     across_up.advance()
 
     depth = groups * hidden.shape[0]
     shape = (width, hidden.shape[1])
     plans = (columns_plan, pieces_plan)
-    ins = columns(gathered, mine, theirs)
-    ups.advance()
-    grad_gate = gradient(where, plans, after(ins, mark), all_dgate, depth, shape)
-    (grad_gate,) = fence([ups], grad_gate)
-
-    ups.advance()
     grad_down = gradient(
         where,
         plans[::-1],
-        after(all_hidden, grad_gate),
+        after(all_hidden, mark),
         columns(upstream, mine_up, theirs_up),
         depth,
         shape[::-1],
     )
-    (grad_down,) = fence([ups], grad_down)
+    (grad_down,) = fence([gates, ups], grad_down)
+    gates.advance()
+
     ups.advance()
-    grad_up = gradient(where, plans, after(ins, grad_down), all_dup, depth, shape)
+    ins = after(columns(gathered, mine, theirs), grad_down)
+    grad_gate = gradient(where, plans, ins, all_dgate, depth, shape)
+    (grad_gate,) = fence([ups], grad_gate)
+    ups.advance()
+    grad_up = gradient(where, plans, after(ins, grad_gate), all_dup, depth, shape)
     return mixed, input_grad, grad_gate, grad_up, grad_down
 
 

time: 180 us -> 174 us (0.967)
  Pallas kernels: 72 us -> 68.4 us
  waiting for transfers between devices: 69.9 us -> 67.5 us
    ppermute x9, waiting for transfers between devices: 22.4 us -> 15 us  [gather_groups(): held.append(lax.ppermute(held[label - (1 << top)], ('dp', 'mp'), pairs))]
    pallas_call x9, Pallas kernels: 72 us -> 68.4 us  [call(): pl.pallas_call(body, grid=(steps,), in_specs=in_specs, out_specs=out_spec...]
    all_gather x2, waiting for transfers between devices: 36.9 us -> 39.3 us  [from_line(): return lax.all_gather(value, 'mp', axis=0, tiled=True)]
  transfers between devices with their start and end apart: 27 -> 27, of which waited for: 9 -> 12; matrix products, arithmetic and copies ran while one was open for 0% -> 0% of each run, Pallas kernels for 40% -> 40%
where the time goes in v2:
time: 174 us; the launch traced here: 173 us
  Pallas kernels  68.4 us (39%)
  waiting for transfers between devices  67.5 us (39%)
  starting transfers between devices  21.5 us (12%)
  between operations  14.1 us (8%)
    pallas_call x9, Pallas kernels, call(): pl.pallas_call(body, grid=(steps,), in_specs=in_specs, out_specs=out_spec...  68.4 us
    all_gather x2, waiting for transfers between devices, from_line(): return lax.all_gather(value, 'mp', axis=0, tiled=True)  39.3 us
    ppermute x9, waiting for transfers between devices, gather_groups(): held.append(lax.ppermute(held[label - (1 << top)], ('dp', 'mp'), pairs))  15 us
    ppermute x9, starting transfers between devices, gather_groups(): held.append(lax.ppermute(held[label - (1 << top)], ('dp', 'mp'), pairs))  12.5 us
    ppermute x8, waiting for transfers between devices, exchange_groups(): lax.ppermute(mine[at], ('dp', 'mp'), left[at].pop(0))  10.4 us
    ppermute x8, starting transfers between devices, exchange_groups(): lax.ppermute(mine[at], ('dp', 'mp'), left[at].pop(0))  7.25 us
  transfers between devices with their start and end apart: 27, of which 12 were waited for; matrix products, arithmetic and copies ran while one was open for 0% of the time, Pallas kernels for 40%

profile of v2, /device:TPU:0, one launch (start us, length us, event | category | flops | bytes accessed | tf_op | source)
XLA Modules:
  0.0 173.1 jit_solution(1117220043091605554)
XLA Ops:
  9.3 37.0 %all-gather.3.cloned.1.call-done.rows_ref.x_in.refs_0_ = bf16[320,4096]{1,0:T(8,128)(2,1)} async-done(((bf16[40,4096]{1,0:T(8,128)(2,1)}), bf16[320,4096]{1,0:T(8,128)(2,1)}) %all-gather.3.cloned.1.call-update) | async-done | bytes 2621456 | tf_op jit(solution)/shard_map/all_gather | solution.py:429
  46.3 2.8 %shard_map.92 = (bf16[160,1024]{1,0:T(8,128)(2,1)}, bf16[160,1024]{1,0:T(8,128)(2,1)}, bf16[160,1024]{1,0:T(8,128)(2,1)}) custom-call(s32[3]{0:T(128)} %pad_add_fusion.where_ref, bf16[320,4096]{1,0:T(8,128)(2,1)} %all-gather.3.cloned.1.call-done.rows_ref.x_in.refs_0_), custom_call_target="tpu_custom_call" | custom-call | tf_op jit(solution)/shard_map/pallas_call | solution.py:39
  49.1 1.5 collective-permute-start
  50.6 1.5 collective-permute-start.1
  52.6 11.8 %shard_map.93 = (bf16[320,1024]{1,0:T(8,128)(2,1)}, f32[320,1024]{1,0:T(8,128)}, f32[320,1024]{1,0:T(8,128)}) custom-call(bf16[320,4096]{1,0:T(8,128)(2,1)} %all-gather.3.cloned.1.call-done.rows_ref.x_in.refs_0_, bf16[4096,1024]{1,0:T(8,128)(2,1)} %w_gate_ref.3, bf16[4096,1024]{1,0:T(8,128)(2,1)} %w_up_ref.3), custom_call_target="tpu_custom_call" | custom-call | tf_op jit(solution)/shard_map/pallas_call | solution.py:39
  64.5 1.6 collective-permute-start.3
  67.1 7.4 %shard_map.94 = bf16[320,4096]{1,0:T(8,128)(2,1)} custom-call(bf16[320,1024]{1,0:T(8,128)(2,1)} %get-tuple-element.120.hidden_ref.refs_0_, bf16[1024,4096]{1,0:T(8,128)(2,1)} %w_ref.3), custom_call_target="tpu_custom_call" | custom-call | tf_op jit(solution)/shard_map/pallas_call | solution.py:39
  74.5 2.3 %collective-permute-done.4.refs_3_ = bf16[160,1024]{1,0:T(8,128)(2,1)S(1)} collective-permute-done((bf16[160,1024]{1,0:T(8,128)(2,1)S(1)}, bf16[160,1024]{1,0:T(8,128)(2,1)S(1)}, u32[]{:S(2)}, u32[]{:S(2)}) %collective-permute-start.4) | collective-permute-done | bytes 327712 | tf_op jit(solution)/shard_map/ppermute | solution.py:411
  76.8 1.7 collective-permute-done.3.refs_1_
  78.4 2.4 %all-gather.5.cloned.1.call-done.rows_ref.x_in.refs_4_ = bf16[320,4096]{1,0:T(8,128)(2,1)} async-done(((bf16[40,4096]{1,0:T(8,128)(2,1)}), bf16[320,4096]{1,0:T(8,128)(2,1)}) %all-gather.5.cloned.1.call-update) | async-done | bytes 2621456 | tf_op jit(solution)/shard_map/all_gather | solution.py:429
  80.9 1.5 collective-permute-start.7
  82.4 2.8 %shard_map.95 = (bf16[160,1024]{1,0:T(8,128)(2,1)}, bf16[160,1024]{1,0:T(8,128)(2,1)}, bf16[160,1024]{1,0:T(8,128)(2,1)}) custom-call(s32[3]{0:T(128)} %pad_add_fusion.where_ref, bf16[320,4096]{1,0:T(8,128)(2,1)} %all-gather.5.cloned.1.call-done.rows_ref.x_in.refs_4_), custom_call_target="tpu_custom_call" | custom-call | tf_op jit(solution)/shard_map/pallas_call | solution.py:39
  85.3 1.5 collective-permute-start.8
  87.9 1.5 collective-permute-start.12
  89.4 8.7 %shard_map.96 = (bf16[320,1024]{1,0:T(8,128)(2,1)}, bf16[320,1024]{1,0:T(8,128)(2,1)}) custom-call(bf16[320,4096]{1,0:T(8,128)(2,1)} %all-gather.5.cloned.1.call-done.rows_ref.x_in.refs_4_, bf16[1024,4096]{1,0:T(8,128)(2,1)} %w_ref.3, f32[320,1024]{1,0:T(8,128)} %get-tuple-element.103.swish_ref, f32[320,1024]{1,0:T(8,128)} %get-tuple-element.104.slope_ref), custom_call_target="tpu_custom_call" | custom-call | tf_op jit(solution)/shard_map/pallas_call | solution.py:39
  98.1 3.9 %collective-permute-done.9.refs_6_ = bf16[160,1024]{1,0:T(8,128)(2,1)S(1)} collective-permute-done((bf16[160,1024]{1,0:T(8,128)(2,1)}, bf16[160,1024]{1,0:T(8,128)(2,1)S(1)}, u32[]{:S(2)}, u32[]{:S(2)}) %collective-permute-start.9) | collective-permute-done | bytes 327712 | tf_op jit(solution)/shard_map/ppermute | solution.py:411
  101.9 1.4 collective-permute-done.10
  103.3 1.5 collective-permute-start.11
  105.8 10.9 %shard_map.97 = bf16[320,4096]{1,0:T(8,128)(2,1)} custom-call(bf16[320,1024]{1,0:T(8,128)(2,1)} %get-tuple-element.107.dgate_ref.refs_7_, bf16[320,1024]{1,0:T(8,128)(2,1)} %get-tuple-element.115.dup_ref.refs_7_, bf16[4096,1024]{1,0:T(8,128)(2,1)} %w_gate_ref.3, bf16[4096,1024]{1,0:T(8,128)(2,1)} %w_up_ref.3), custom_call_target="tpu_custom_call" | custom-call | tf_op jit(solution)/shard_map/pallas_call | solution.py:39
  116.8 2.9 %collective-permute-done.13.refs_7_ = bf16[160,1024]{1,0:T(8,128)(2,1)} collective-permute-done((bf16[160,1024]{1,0:T(8,128)(2,1)}, bf16[160,1024]{1,0:T(8,128)(2,1)}, u32[]{:S(2)}, u32[]{:S(2)}) %collective-permute-start.13) | collective-permute-done | bytes 327712 | tf_op jit(solution)/shard_map/ppermute | solution.py:411
  119.8 1.5 collective-permute-start.17
  121.3 1.5 collective-permute-start.19
  123.9 1.3 collective-permute-done.21.refs_10_
  125.2 1.5 collective-permute-start.16
  126.7 8.1 %shard_map.98 = bf16[1024,1024]{1,0:T(8,128)(2,1)} custom-call(s32[3]{0:T(128)} %pad_add_fusion.where_ref, bf16[320,1024]{1,0:T(8,128)(2,1)} %get-tuple-element.120.hidden_ref.refs_0_, bf16[320,1024]{1,0:T(8,128)(2,1)} %collective-permute-done.3.refs_1_, bf16[320,1024]{1,0:T(8,128)(2,1)} %copy-done.9, bf16[320,1024]{1,0:T(8,128)(2,1)} %copy-done.10, ...), custom_call_target="tpu_custom_call" | custom-call | tf_op jit(solution)/shard_map/pallas_call | solution.py:39
  134.8 1.8 %collective-permute-done.17.refs_9_ = bf16[320,1024]{1,0:T(8,128)(2,1)S(1)} collective-permute-done((bf16[320,1024]{1,0:T(8,128)(2,1)S(1)}, bf16[320,1024]{1,0:T(8,128)(2,1)S(1)}, u32[]{:S(2)}, u32[]{:S(2)}) %collective-permute-start.17) | collective-permute-done | bytes 655392 | tf_op jit(solution)/shard_map/ppermute | solution.py:396
  136.6 2.4 %collective-permute-done.19.refs_8_ = bf16[320,1024]{1,0:T(8,128)(2,1)S(1)} collective-permute-done((bf16[320,1024]{1,0:T(8,128)(2,1)S(1)}, bf16[320,1024]{1,0:T(8,128)(2,1)S(1)}, u32[]{:S(2)}, u32[]{:S(2)}) %collective-permute-start.19) | collective-permute-done | bytes 655392 | tf_op jit(solution)/shard_map/ppermute | solution.py:396
  139.0 4.6 %collective-permute-done.18.refs_10_ = bf16[320,1024]{1,0:T(8,128)(2,1)S(1)} collective-permute-done((bf16[320,1024]{1,0:T(8,128)(2,1)}, bf16[320,1024]{1,0:T(8,128)(2,1)S(1)}, u32[]{:S(2)}, u32[]{:S(2)}) %collective-permute-start.18) | collective-permute-done | bytes 655392 | tf_op jit(solution)/shard_map/ppermute | solution.py:396
  143.6 1.5 collective-permute-start.22
  145.1 8.0 %shard_map.99 = bf16[1024,1024]{1,0:T(8,128)(2,1)} custom-call(s32[3]{0:T(128)} %pad_add_fusion.where_ref, bf16[320,4096]{1,0:T(8,128)(2,1)} %all-gather.3.cloned.1.call-done.rows_ref.x_in.refs_0_, bf16[160,1024]{1,0:T(8,128)(2,1)} %copy-done.3, bf16[160,1024]{1,0:T(8,128)(2,1)} %copy-done.4, bf16[160,1024]{1,0:T(8,128)(2,1)} %copy-done.5, ...), custom_call_target="tpu_custom_call" | custom-call | tf_op jit(solution)/shard_map/pallas_call | solution.py:39
  153.1 4.5 %collective-permute-done.22.refs_10_ = bf16[320,1024]{1,0:T(8,128)(2,1)S(1)} collective-permute-done((bf16[320,1024]{1,0:T(8,128)(2,1)S(1)}, bf16[320,1024]{1,0:T(8,128)(2,1)S(1)}, u32[]{:S(2)}, u32[]{:S(2)}) %collective-permute-start.22) | collective-permute-done | bytes 655392 | tf_op jit(solution)/shard_map/ppermute | solution.py:396
  158.5 8.0 %shard_map.100 = bf16[1024,1024]{1,0:T(8,128)(2,1)} custom-call(s32[3]{0:T(128)} %pad_add_fusion.where_ref, bf16[320,4096]{1,0:T(8,128)(2,1)} %all-gather.3.cloned.1.call-done.rows_ref.x_in.refs_0_, bf16[160,1024]{1,0:T(8,128)(2,1)} %copy-done.3, bf16[160,1024]{1,0:T(8,128)(2,1)} %copy-done.4, bf16[160,1024]{1,0:T(8,128)(2,1)} %copy-done.5, ...), custom_call_target="tpu_custom_call" | custom-call | tf_op jit(solution)/shard_map/pallas_call | solution.py:39
  (76 shorter events, 8.0 us)
Async XLA Ops:
  7.2 39.1 %all-gather.3.cloned.1.call-start = ((), (), s32[]{:S(2)}) async-start(), calls=%async_computation.2 | async-start | bytes 2949120 | tf_op jit(solution)/shard_map/all_gather | solution.py:429
  7.9 72.9 %all-gather.5.cloned.1.call-start = ((), (), s32[]{:S(2)}) async-start(), calls=%async_computation.3 | async-start | bytes 2949120 | tf_op jit(solution)/shard_map/all_gather | solution.py:429
  8.6 157.9 %reduce-scatter.3.cloned.1.call-start = ((), (), s32[]{:S(2)}) async-start(), calls=%async_computation.4 | async-start | bytes 2949120 | tf_op jit(solution)/shard_map/reduce_scatter | solution.py:432
  49.1 15.4 %collective-permute-start = (bf16[160,1024]{1,0:T(8,128)(2,1)}, bf16[160,1024]{1,0:T(8,128)(2,1)S(1)}, u32[]{:S(2)}, u32[]{:S(2)}) collective-permute-start(bf16[160,1024]{1,0:T(8,128)(2,1)} %get-tuple-element.79), channel_id=1, source_target_pairs={{0,8},{1,17},{2,10},{3,19},{4,12},{5,21},{6,14},{7,23},{8,0},{9,25... | collective-permute-start | bytes 983048 | tf_op jit(solution)/shard_map/ppermute | solution.py:411
  50.6 13.9 %collective-permute-start.1 = (bf16[160,1024]{1,0:T(8,128)(2,1)}, bf16[160,1024]{1,0:T(8,128)(2,1)S(1)}, u32[]{:S(2)}, u32[]{:S(2)}) collective-permute-start(bf16[160,1024]{1,0:T(8,128)(2,1)} %get-tuple-element.80), channel_id=1, source_target_pairs={{0,16},{1,9},{2,18},{3,11},{4,20},{5,13},{6,22},{7,15},{8,24},{9,1... | collective-permute-start | bytes 983048 | tf_op jit(solution)/shard_map/ppermute | solution.py:411
  52.1 12.4 %collective-permute-start.2 = (bf16[160,1024]{1,0:T(8,128)(2,1)}, bf16[160,1024]{1,0:T(8,128)(2,1)S(1)}, u32[]{:S(2)}, u32[]{:S(2)}) collective-permute-start(bf16[160,1024]{1,0:T(8,128)(2,1)} %get-tuple-element.81), channel_id=1, source_target_pairs={{0,8},{1,17},{2,10},{3,19},{4,12},{5,21},{6,14},{7,23},{8,0},{9,25... | collective-permute-start | bytes 983048 | tf_op jit(solution)/shard_map/ppermute | solution.py:411
  64.5 10.0 %copy-start.3 = (bf16[160,1024]{1,0:T(8,128)(2,1)}, bf16[160,1024]{1,0:T(8,128)(2,1)S(1)}, u32[]{:S(2)}) copy-start(bf16[160,1024]{1,0:T(8,128)(2,1)S(1)} %collective-permute-done.refs_1_) | copy-start | bytes 983044
  64.5 13.9 %collective-permute-start.3 = (bf16[320,1024]{1,0:T(8,128)(2,1)}, bf16[320,1024]{1,0:T(8,128)(2,1)}, u32[]{:S(2)}, u32[]{:S(2)}) collective-permute-start(bf16[320,1024]{1,0:T(8,128)(2,1)} %get-tuple-element.120.hidden_ref.refs_0_), channel_id=1, source_target_pairs={{0,8},{1,17},{2,10},{3,19},{4,12},{5,21},{6,14},{7,23},{8,0},{9,25... | collective-permute-start | bytes 1966088 | tf_op jit(solution)/shard_map/ppermute | solution.py:396
  66.1 10.6 %collective-permute-start.4 = (bf16[160,1024]{1,0:T(8,128)(2,1)S(1)}, bf16[160,1024]{1,0:T(8,128)(2,1)S(1)}, u32[]{:S(2)}, u32[]{:S(2)}) collective-permute-start(bf16[160,1024]{1,0:T(8,128)(2,1)S(1)} %collective-permute-done.2), channel_id=1, source_target_pairs={{0,16},{1,9},{2,18},{3,11},{4,20},{5,13},{6,22},{7,15},{8,24},{9,1... | collective-permute-start | bytes 983048 | tf_op jit(solution)/shard_map/ppermute | solution.py:411
  66.6 10.2 %collective-permute-start.5 = (bf16[160,1024]{1,0:T(8,128)(2,1)S(1)}, bf16[160,1024]{1,0:T(8,128)(2,1)S(1)}, u32[]{:S(2)}, u32[]{:S(2)}) collective-permute-start(bf16[160,1024]{1,0:T(8,128)(2,1)S(1)} %collective-permute-done.refs_1_), channel_id=1, source_target_pairs={{0,1},{1,0},{2,3},{3,2},{4,5},{5,4},{6,7},{7,6},{8,9},{9,8},{10,11... | collective-permute-start | bytes 983048 | tf_op jit(solution)/shard_map/ppermute | solution.py:345
  66.6 10.2 %collective-permute-start.6 = (bf16[160,1024]{1,0:T(8,128)(2,1)S(1)}, bf16[160,1024]{1,0:T(8,128)(2,1)S(1)}, u32[]{:S(2)}, u32[]{:S(2)}) collective-permute-start(bf16[160,1024]{1,0:T(8,128)(2,1)S(1)} %collective-permute-done.1.refs_2_), channel_id=1, source_target_pairs={{0,1},{1,0},{2,3},{3,2},{4,5},{5,4},{6,7},{7,6},{8,9},{9,8},{10,11... | collective-permute-start | bytes 983048 | tf_op jit(solution)/shard_map/ppermute | solution.py:345
  76.7 46.6 %copy-start.5 = (bf16[160,1024]{1,0:T(8,128)(2,1)}, bf16[160,1024]{1,0:T(8,128)(2,1)S(1)}, u32[]{:S(2)}) copy-start(bf16[160,1024]{1,0:T(8,128)(2,1)S(1)} %collective-permute-done.4.refs_3_) | copy-start | bytes 983044
  80.8 85.8 %reduce-scatter.5.cloned.1.call-start = ((), (), s32[]{:S(2)}) async-start(), calls=%async_computation.5 | async-start | bytes 2949120 | tf_op jit(solution)/shard_map/reduce_scatter | solution.py:432
  80.9 17.2 %collective-permute-start.7 = (bf16[320,1024]{1,0:T(8,128)(2,1)S(1)}, bf16[320,1024]{1,0:T(8,128)(2,1)S(1)}, u32[]{:S(2)}, u32[]{:S(2)}) collective-permute-start(bf16[320,1024]{1,0:T(8,128)(2,1)S(1)} %copy-done), channel_id=1, source_target_pairs={{0,16},{1,9},{2,18},{3,11},{4,20},{5,13},{6,22},{7,15},{8,24},{9,1... | collective-permute-start | bytes 1966088 | tf_op jit(solution)/shard_map/ppermute | solution.py:396
  85.3 12.8 %collective-permute-start.8 = (bf16[160,1024]{1,0:T(8,128)(2,1)}, bf16[160,1024]{1,0:T(8,128)(2,1)S(1)}, u32[]{:S(2)}, u32[]{:S(2)}) collective-permute-start(bf16[160,1024]{1,0:T(8,128)(2,1)} %get-tuple-element.99), channel_id=1, source_target_pairs={{0,8},{1,17},{2,10},{3,19},{4,12},{5,21},{6,14},{7,23},{8,0},{9,25... | collective-permute-start | bytes 983048 | tf_op jit(solution)/shard_map/ppermute | solution.py:411
  86.8 15.2 %collective-permute-start.9 = (bf16[160,1024]{1,0:T(8,128)(2,1)}, bf16[160,1024]{1,0:T(8,128)(2,1)S(1)}, u32[]{:S(2)}, u32[]{:S(2)}) collective-permute-start(bf16[160,1024]{1,0:T(8,128)(2,1)} %get-tuple-element.100), channel_id=1, source_target_pairs={{0,16},{1,9},{2,18},{3,11},{4,20},{5,13},{6,22},{7,15},{8,24},{9,1... | collective-permute-start | bytes 983048 | tf_op jit(solution)/shard_map/ppermute | solution.py:411
  87.3 16.0 %collective-permute-start.10 = (bf16[160,1024]{1,0:T(8,128)(2,1)}, bf16[160,1024]{1,0:T(8,128)(2,1)}, u32[]{:S(2)}, u32[]{:S(2)}) collective-permute-start(bf16[160,1024]{1,0:T(8,128)(2,1)} %get-tuple-element.101), channel_id=1, source_target_pairs={{0,8},{1,17},{2,10},{3,19},{4,12},{5,21},{6,14},{7,23},{8,0},{9,25... | collective-permute-start | bytes 983048 | tf_op jit(solution)/shard_map/ppermute | solution.py:411
  87.9 28.9 %collective-permute-start.12 = (bf16[320,1024]{1,0:T(8,128)(2,1)}, bf16[320,1024]{1,0:T(8,128)(2,1)S(1)}, u32[]{:S(2)}, u32[]{:S(2)}) collective-permute-start(bf16[320,1024]{1,0:T(8,128)(2,1)} %collective-permute-done.3.refs_1_), channel_id=1, source_target_pairs={{0,16},{1,9},{2,18},{3,11},{4,20},{5,13},{6,22},{7,15},{8,24},{9,1... | collective-permute-start | bytes 1966088 | tf_op jit(solution)/shard_map/ppermute | solution.py:396
  98.1 18.6 %copy-start.16 = (bf16[160,1024]{1,0:T(8,128)(2,1)}, bf16[160,1024]{1,0:T(8,128)(2,1)S(1)}, u32[]{:S(2)}) copy-start(bf16[160,1024]{1,0:T(8,128)(2,1)S(1)} %collective-permute-done.8.refs_5_) | copy-start | bytes 983044
  101.9 14.8 %copy-start.17 = (bf16[160,1024]{1,0:T(8,128)(2,1)}, bf16[160,1024]{1,0:T(8,128)(2,1)S(1)}, u32[]{:S(2)}) copy-start(bf16[160,1024]{1,0:T(8,128)(2,1)S(1)} %collective-permute-done.9.refs_6_) | copy-start | bytes 983044
  103.3 16.4 %collective-permute-start.11 = (bf16[320,1024]{1,0:T(8,128)(2,1)}, bf16[320,1024]{1,0:T(8,128)(2,1)}, u32[]{:S(2)}, u32[]{:S(2)}) collective-permute-start(bf16[320,1024]{1,0:T(8,128)(2,1)} %get-tuple-element.107.dgate_ref.refs_7_), channel_id=1, source_target_pairs={{0,8},{1,17},{2,10},{3,19},{4,12},{5,21},{6,14},{7,23},{8,0},{9,25... | collective-permute-start | bytes 1966088 | tf_op jit(solution)/shard_map/ppermute | solution.py:396
  104.8 15.0 %collective-permute-start.13 = (bf16[160,1024]{1,0:T(8,128)(2,1)}, bf16[160,1024]{1,0:T(8,128)(2,1)}, u32[]{:S(2)}, u32[]{:S(2)}) collective-permute-start(bf16[160,1024]{1,0:T(8,128)(2,1)} %collective-permute-done.10), channel_id=1, source_target_pairs={{0,16},{1,9},{2,18},{3,11},{4,20},{5,13},{6,22},{7,15},{8,24},{9,1... | collective-permute-start | bytes 983048 | tf_op jit(solution)/shard_map/ppermute | solution.py:411
  105.3 14.4 %collective-permute-start.14 = (bf16[160,1024]{1,0:T(8,128)(2,1)S(1)}, bf16[160,1024]{1,0:T(8,128)(2,1)S(1)}, u32[]{:S(2)}, u32[]{:S(2)}) collective-permute-start(bf16[160,1024]{1,0:T(8,128)(2,1)S(1)} %collective-permute-done.8.refs_5_), channel_id=1, source_target_pairs={{0,1},{1,0},{2,3},{3,2},{4,5},{5,4},{6,7},{7,6},{8,9},{9,8},{10,11... | collective-permute-start | bytes 983048 | tf_op jit(solution)/shard_map/ppermute | solution.py:345
  105.3 14.4 %collective-permute-start.15 = (bf16[160,1024]{1,0:T(8,128)(2,1)S(1)}, bf16[160,1024]{1,0:T(8,128)(2,1)}, u32[]{:S(2)}, u32[]{:S(2)}) collective-permute-start(bf16[160,1024]{1,0:T(8,128)(2,1)S(1)} %collective-permute-done.9.refs_6_), channel_id=1, source_target_pairs={{0,1},{1,0},{2,3},{3,2},{4,5},{5,4},{6,7},{7,6},{8,9},{9,8},{10,11... | collective-permute-start | bytes 983048 | tf_op jit(solution)/shard_map/ppermute | solution.py:345
  119.8 16.8 %collective-permute-start.17 = (bf16[320,1024]{1,0:T(8,128)(2,1)S(1)}, bf16[320,1024]{1,0:T(8,128)(2,1)S(1)}, u32[]{:S(2)}, u32[]{:S(2)}) collective-permute-start(bf16[320,1024]{1,0:T(8,128)(2,1)S(1)} %copy-done.2), channel_id=1, source_target_pairs={{0,16},{1,9},{2,18},{3,11},{4,20},{5,13},{6,22},{7,15},{8,24},{9,1... | collective-permute-start | bytes 1966088 | tf_op jit(solution)/shard_map/ppermute | solution.py:396
  121.3 17.7 %collective-permute-start.19 = (bf16[320,1024]{1,0:T(8,128)(2,1)S(1)}, bf16[320,1024]{1,0:T(8,128)(2,1)S(1)}, u32[]{:S(2)}, u32[]{:S(2)}) collective-permute-start(bf16[320,1024]{1,0:T(8,128)(2,1)S(1)} %copy-done.1), channel_id=1, source_target_pairs={{0,8},{1,17},{2,10},{3,19},{4,12},{5,21},{6,14},{7,23},{8,0},{9,25... | collective-permute-start | bytes 1966088 | tf_op jit(solution)/shard_map/ppermute | solution.py:396
  122.8 20.8 %collective-permute-start.18 = (bf16[320,1024]{1,0:T(8,128)(2,1)}, bf16[320,1024]{1,0:T(8,128)(2,1)S(1)}, u32[]{:S(2)}, u32[]{:S(2)}) collective-permute-start(bf16[320,1024]{1,0:T(8,128)(2,1)} %collective-permute-done.11.refs_8_), channel_id=1, source_target_pairs={{0,16},{1,9},{2,18},{3,11},{4,20},{5,13},{6,22},{7,15},{8,24},{9,1... | collective-permute-start | bytes 1966088 | tf_op jit(solution)/shard_map/ppermute | solution.py:396
  123.3 1.8 %collective-permute-start.21 = (bf16[160,1024]{1,0:T(8,128)(2,1)}, bf16[160,1024]{1,0:T(8,128)(2,1)S(1)}, u32[]{:S(2)}, u32[]{:S(2)}) collective-permute-start(bf16[160,1024]{1,0:T(8,128)(2,1)} %collective-permute-done.13.refs_7_), channel_id=1, source_target_pairs={{0,1},{1,0},{2,3},{3,2},{4,5},{5,4},{6,7},{7,6},{8,9},{9,8},{10,11... | collective-permute-start | bytes 983048 | tf_op jit(solution)/shard_map/ppermute | solution.py:345
  123.4 3.3 %collective-permute-start.20 = (bf16[160,1024]{1,0:T(8,128)(2,1)S(1)}, bf16[160,1024]{1,0:T(8,128)(2,1)S(1)}, u32[]{:S(2)}, u32[]{:S(2)}) collective-permute-start(bf16[160,1024]{1,0:T(8,128)(2,1)S(1)} %collective-permute-done.4.refs_3_), channel_id=1, source_target_pairs={{0,1},{1,0},{2,3},{3,2},{4,5},{5,4},{6,7},{7,6},{8,9},{9,8},{10,11... | collective-permute-start | bytes 983048 | tf_op jit(solution)/shard_map/ppermute | solution.py:345
  125.2 27.9 %collective-permute-start.16 = (bf16[320,1024]{1,0:T(8,128)(2,1)S(1)}, bf16[320,1024]{1,0:T(8,128)(2,1)S(1)}, u32[]{:S(2)}, u32[]{:S(2)}) collective-permute-start(bf16[320,1024]{1,0:T(8,128)(2,1)S(1)} %copy-done.1), channel_id=1, source_target_pairs={{0,16},{1,9},{2,18},{3,11},{4,20},{5,13},{6,22},{7,15},{8,24},{9,1... | collective-permute-start | bytes 1966088 | tf_op jit(solution)/shard_map/ppermute | solution.py:396
  139.0 14.1 %copy-start.11 = (bf16[320,1024]{1,0:T(8,128)(2,1)}, bf16[320,1024]{1,0:T(8,128)(2,1)S(1)}, u32[]{:S(2)}) copy-start(bf16[320,1024]{1,0:T(8,128)(2,1)S(1)} %collective-permute-done.19.refs_8_) | copy-start | bytes 1966084
  143.6 14.0 %collective-permute-start.22 = (bf16[320,1024]{1,0:T(8,128)(2,1)S(1)}, bf16[320,1024]{1,0:T(8,128)(2,1)S(1)}, u32[]{:S(2)}, u32[]{:S(2)}) collective-permute-start(bf16[320,1024]{1,0:T(8,128)(2,1)S(1)} %collective-permute-done.19.refs_8_), channel_id=1, source_target_pairs={{0,16},{1,9},{2,18},{3,11},{4,20},{5,13},{6,22},{7,15},{8,24},{9,1... | collective-permute-start | bytes 1966088 | tf_op jit(solution)/shard_map/ppermute | solution.py:396
  (15 other events, 87.3 us)
Sparse Core Ops, SparseCore 0:
  9.6 36.5 all-gather.2
  47.9 32.8 all-gather.4
  83.7 36.4 reduce-scatter.2
  122.9 36.5 reduce-scatter.4

commit v3 on v2

--- a/solution.py
+++ b/solution.py
@@ -473,10 +473,12 @@
     ups = over_groups(dup, all_dup, [1], range(2, groups))
     hiddens.advance()
     gates.advance()
+    ups.advance()
     for _ in range(phases - 1):
         across_up.advance()
     (partial,) = fence(
-        [gates, hiddens, across, across_up], input_sum(dgate, dup, w_gate, w_up)
+        [gates, ups, hiddens, across, across_up],
+        input_sum(dgate, dup, w_gate, w_up),
     )
     input_grad = over_line(partial)
 
@@ -500,10 +502,9 @@
         depth,
         shape[::-1],
     )
-    (grad_down,) = fence([gates, ups], grad_down)
+    (grad_down,) = fence([gates], grad_down)
     gates.advance()
 
-    ups.advance()
     ins = after(columns(gathered, mine, theirs), grad_down)
     grad_gate = gradient(where, plans, ins, all_dgate, depth, shape)
     (grad_gate,) = fence([ups], grad_gate)

time: 174 us -> 174 us (level)
  local copies, waits for them, and re-layouts: 1 us -> 3.4 us
  starting transfers between devices: 21.5 us -> 19.2 us
    ppermute x8, waiting for transfers between devices: 10.4 us -> 7.46 us  [exchange_groups(): lax.ppermute(mine[at], ('dp', 'mp'), left[at].pop(0))]
    ppermute x9, waiting for transfers between devices: 15 us -> 17.8 us  [gather_groups(): held.append(lax.ppermute(held[label - (1 << top)], ('dp', 'mp'), pairs))]
    unnamed x40 -> x38, local copies, waits for them, and re-layouts: 1 us -> 3.4 us
    ppermute x9, starting transfers between devices: 12.5 us -> 10.7 us  [gather_groups(): held.append(lax.ppermute(held[label - (1 << top)], ('dp', 'mp'), pairs))]
  transfers between devices with their start and end apart: 27 -> 27, of which waited for: 12 -> 11; matrix products, arithmetic and copies ran while one was open for 0% -> 0% of each run, Pallas kernels for 40% -> 39%
where the time goes in v3:
time: 174 us
  Pallas kernels  68.3 us (39%)
  waiting for transfers between devices  67.9 us (39%)
  starting transfers between devices  19.2 us (11%)
  between operations  14.1 us (8%)
  local copies, waits for them, and re-layouts  3.4 us (2%)
    pallas_call x9, Pallas kernels, call(): pl.pallas_call(body, grid=(steps,), in_specs=in_specs, out_specs=out_spec...  68.3 us
    all_gather x2, waiting for transfers between devices, from_line(): return lax.all_gather(value, 'mp', axis=0, tiled=True)  39.3 us
    ppermute x9, waiting for transfers between devices, gather_groups(): held.append(lax.ppermute(held[label - (1 << top)], ('dp', 'mp'), pairs))  17.8 us
    ppermute x9, starting transfers between devices, gather_groups(): held.append(lax.ppermute(held[label - (1 << top)], ('dp', 'mp'), pairs))  10.7 us
    ppermute x8, waiting for transfers between devices, exchange_groups(): lax.ppermute(mine[at], ('dp', 'mp'), left[at].pop(0))  7.46 us
    ppermute x8, starting transfers between devices, exchange_groups(): lax.ppermute(mine[at], ('dp', 'mp'), left[at].pop(0))  7.24 us
  transfers between devices with their start and end apart: 27, of which 11 were waited for; matrix products, arithmetic and copies ran while one was open for 0% of the time, Pallas kernels for 39%

profile of v3, /device:TPU:0, one launch (start us, length us, event | category | flops | bytes accessed | tf_op | source)
XLA Modules:
  0.0 173.7 jit_solution(7074166307616919431)
XLA Ops:
  9.4 36.9 %all-gather.3.cloned.1.call-done.rows_ref.x_in.refs_0_ = bf16[320,4096]{1,0:T(8,128)(2,1)} async-done(((bf16[40,4096]{1,0:T(8,128)(2,1)}), bf16[320,4096]{1,0:T(8,128)(2,1)}) %all-gather.3.cloned.1.call-update) | async-done | bytes 2621456 | tf_op jit(solution)/shard_map/all_gather | solution.py:429
  46.3 2.8 %shard_map.92 = (bf16[160,1024]{1,0:T(8,128)(2,1)}, bf16[160,1024]{1,0:T(8,128)(2,1)}, bf16[160,1024]{1,0:T(8,128)(2,1)}) custom-call(s32[3]{0:T(128)} %pad_add_fusion.where_ref, bf16[320,4096]{1,0:T(8,128)(2,1)} %all-gather.3.cloned.1.call-done.rows_ref.x_in.refs_0_), custom_call_target="tpu_custom_call" | custom-call | tf_op jit(solution)/shard_map/pallas_call | solution.py:39
  49.1 1.5 collective-permute-start
  50.6 1.5 collective-permute-start.1
  52.6 11.8 %shard_map.93 = (bf16[320,1024]{1,0:T(8,128)(2,1)}, f32[320,1024]{1,0:T(8,128)}, f32[320,1024]{1,0:T(8,128)}) custom-call(bf16[320,4096]{1,0:T(8,128)(2,1)} %all-gather.3.cloned.1.call-done.rows_ref.x_in.refs_0_, bf16[4096,1024]{1,0:T(8,128)(2,1)} %w_gate_ref.3, bf16[4096,1024]{1,0:T(8,128)(2,1)} %w_up_ref.3), custom_call_target="tpu_custom_call" | custom-call | tf_op jit(solution)/shard_map/pallas_call | solution.py:39
  64.5 1.6 collective-permute-start.3
  67.1 7.4 %shard_map.94 = bf16[320,4096]{1,0:T(8,128)(2,1)} custom-call(bf16[320,1024]{1,0:T(8,128)(2,1)} %get-tuple-element.126.hidden_ref.refs_0_, bf16[1024,4096]{1,0:T(8,128)(2,1)} %w_ref.3), custom_call_target="tpu_custom_call" | custom-call | tf_op jit(solution)/shard_map/pallas_call | solution.py:39
  74.5 2.2 %collective-permute-done.4.refs_3_ = bf16[160,1024]{1,0:T(8,128)(2,1)S(1)} collective-permute-done((bf16[160,1024]{1,0:T(8,128)(2,1)S(1)}, bf16[160,1024]{1,0:T(8,128)(2,1)S(1)}, u32[]{:S(2)}, u32[]{:S(2)}) %collective-permute-start.4) | collective-permute-done | bytes 327712 | tf_op jit(solution)/shard_map/ppermute | solution.py:411
  76.8 1.6 collective-permute-done.3.refs_1_
  78.3 2.5 %all-gather.5.cloned.1.call-done.rows_ref.x_in.refs_4_ = bf16[320,4096]{1,0:T(8,128)(2,1)} async-done(((bf16[40,4096]{1,0:T(8,128)(2,1)}), bf16[320,4096]{1,0:T(8,128)(2,1)}) %all-gather.5.cloned.1.call-update) | async-done | bytes 2621456 | tf_op jit(solution)/shard_map/all_gather | solution.py:429
  80.9 1.5 collective-permute-start.7
  82.4 2.8 %shard_map.95 = (bf16[160,1024]{1,0:T(8,128)(2,1)}, bf16[160,1024]{1,0:T(8,128)(2,1)}, bf16[160,1024]{1,0:T(8,128)(2,1)}) custom-call(s32[3]{0:T(128)} %pad_add_fusion.where_ref, bf16[320,4096]{1,0:T(8,128)(2,1)} %all-gather.5.cloned.1.call-done.rows_ref.x_in.refs_4_), custom_call_target="tpu_custom_call" | custom-call | tf_op jit(solution)/shard_map/pallas_call | solution.py:39
  85.2 1.5 collective-permute-start.8
  87.9 1.5 collective-permute-start.13
  89.4 8.7 %shard_map.96 = (bf16[320,1024]{1,0:T(8,128)(2,1)}, bf16[320,1024]{1,0:T(8,128)(2,1)}) custom-call(bf16[320,4096]{1,0:T(8,128)(2,1)} %all-gather.5.cloned.1.call-done.rows_ref.x_in.refs_4_, bf16[1024,4096]{1,0:T(8,128)(2,1)} %w_ref.3, f32[320,1024]{1,0:T(8,128)} %get-tuple-element.103.swish_ref, f32[320,1024]{1,0:T(8,128)} %get-tuple-element.104.slope_ref), custom_call_target="tpu_custom_call" | custom-call | tf_op jit(solution)/shard_map/pallas_call | solution.py:39
  98.1 4.0 %collective-permute-done.9.refs_6_ = bf16[160,1024]{1,0:T(8,128)(2,1)} collective-permute-done((bf16[160,1024]{1,0:T(8,128)(2,1)}, bf16[160,1024]{1,0:T(8,128)(2,1)}, u32[]{:S(2)}, u32[]{:S(2)}) %collective-permute-start.9) | collective-permute-done | bytes 327712 | tf_op jit(solution)/shard_map/ppermute | solution.py:411
  102.0 1.2 collective-permute-done.10
  103.3 1.5 collective-permute-start.11
  105.9 7.0 %collective-permute-done.13.refs_3_ = bf16[320,1024]{1,0:T(8,128)(2,1)S(1)} collective-permute-done((bf16[320,1024]{1,0:T(8,128)(2,1)S(1)}, bf16[320,1024]{1,0:T(8,128)(2,1)S(1)}, u32[]{:S(2)}, u32[]{:S(2)}) %collective-permute-start.13) | collective-permute-done | bytes 655392 | tf_op jit(solution)/shard_map/ppermute | solution.py:396
  112.9 0.8 copy-done.12
  113.7 10.9 %shard_map.97 = bf16[320,4096]{1,0:T(8,128)(2,1)} custom-call(bf16[320,1024]{1,0:T(8,128)(2,1)} %get-tuple-element.107.dgate_ref.refs_7_, bf16[320,1024]{1,0:T(8,128)(2,1)} %get-tuple-element.108.dup_ref.refs_7_, bf16[4096,1024]{1,0:T(8,128)(2,1)} %w_gate_ref.3, bf16[4096,1024]{1,0:T(8,128)(2,1)} %w_up_ref.3), custom_call_target="tpu_custom_call" | custom-call | tf_op jit(solution)/shard_map/pallas_call | solution.py:39
  124.7 1.2 collective-permute-done.12.refs_8_
  126.6 1.5 collective-permute-start.21
  128.6 1.5 collective-permute-start.17
  130.6 1.8 %collective-permute-done.20.refs_10_ = bf16[160,1024]{1,0:T(8,128)(2,1)S(1)} collective-permute-done((bf16[160,1024]{1,0:T(8,128)(2,1)}, bf16[160,1024]{1,0:T(8,128)(2,1)S(1)}, u32[]{:S(2)}, u32[]{:S(2)}) %collective-permute-start.20) | collective-permute-done | bytes 327712 | tf_op jit(solution)/shard_map/ppermute | solution.py:345
  133.2 7.9 %shard_map.98 = bf16[1024,1024]{1,0:T(8,128)(2,1)} custom-call(s32[3]{0:T(128)} %pad_add_fusion.where_ref, bf16[320,1024]{1,0:T(8,128)(2,1)} %get-tuple-element.126.hidden_ref.refs_0_, bf16[320,1024]{1,0:T(8,128)(2,1)} %copy-done.9, bf16[320,1024]{1,0:T(8,128)(2,1)} %copy-done.10, bf16[320,1024]{1,0:T(8,128)(2,1)} %copy-done.12, ...), custom_call_target="tpu_custom_call" | custom-call | tf_op jit(solution)/shard_map/pallas_call | solution.py:39
  141.2 3.0 %collective-permute-done.22.refs_10_ = bf16[320,1024]{1,0:T(8,128)(2,1)S(1)} collective-permute-done((bf16[320,1024]{1,0:T(8,128)(2,1)}, bf16[320,1024]{1,0:T(8,128)(2,1)S(1)}, u32[]{:S(2)}, u32[]{:S(2)}) %collective-permute-start.22) | collective-permute-done | bytes 655392 | tf_op jit(solution)/shard_map/ppermute | solution.py:396
  144.2 0.9 copy-done.16
  145.1 8.0 %shard_map.99 = bf16[1024,1024]{1,0:T(8,128)(2,1)} custom-call(s32[3]{0:T(128)} %pad_add_fusion.where_ref, bf16[320,4096]{1,0:T(8,128)(2,1)} %all-gather.3.cloned.1.call-done.rows_ref.x_in.refs_0_, bf16[160,1024]{1,0:T(8,128)(2,1)} %copy-done.3, bf16[160,1024]{1,0:T(8,128)(2,1)} %copy-done.4, bf16[160,1024]{1,0:T(8,128)(2,1)} %copy-done.5, ...), custom_call_target="tpu_custom_call" | custom-call | tf_op jit(solution)/shard_map/pallas_call | solution.py:39
  153.1 5.1 %collective-permute-done.18.refs_10_ = bf16[320,1024]{1,0:T(8,128)(2,1)S(1)} collective-permute-done((bf16[320,1024]{1,0:T(8,128)(2,1)S(1)}, bf16[320,1024]{1,0:T(8,128)(2,1)S(1)}, u32[]{:S(2)}, u32[]{:S(2)}) %collective-permute-start.18) | collective-permute-done | bytes 655392 | tf_op jit(solution)/shard_map/ppermute | solution.py:396
  158.2 0.8 copy-done.14
  159.0 8.0 %shard_map.100 = bf16[1024,1024]{1,0:T(8,128)(2,1)} custom-call(s32[3]{0:T(128)} %pad_add_fusion.where_ref, bf16[320,4096]{1,0:T(8,128)(2,1)} %all-gather.3.cloned.1.call-done.rows_ref.x_in.refs_0_, bf16[160,1024]{1,0:T(8,128)(2,1)} %copy-done.3, bf16[160,1024]{1,0:T(8,128)(2,1)} %copy-done.4, bf16[160,1024]{1,0:T(8,128)(2,1)} %copy-done.5, ...), custom_call_target="tpu_custom_call" | custom-call | tf_op jit(solution)/shard_map/pallas_call | solution.py:39
  (74 shorter events, 8.6 us)
Async XLA Ops:
  7.2 39.1 %all-gather.3.cloned.1.call-start = ((), (), s32[]{:S(2)}) async-start(), calls=%async_computation.2 | async-start | bytes 2949120 | tf_op jit(solution)/shard_map/all_gather | solution.py:429
  7.9 72.9 %all-gather.5.cloned.1.call-start = ((), (), s32[]{:S(2)}) async-start(), calls=%async_computation.3 | async-start | bytes 2949120 | tf_op jit(solution)/shard_map/all_gather | solution.py:429
  8.6 158.5 %reduce-scatter.3.cloned.1.call-start = ((), (), s32[]{:S(2)}) async-start(), calls=%async_computation.4 | async-start | bytes 2949120 | tf_op jit(solution)/shard_map/reduce_scatter | solution.py:432
  49.1 15.4 %collective-permute-start = (bf16[160,1024]{1,0:T(8,128)(2,1)}, bf16[160,1024]{1,0:T(8,128)(2,1)S(1)}, u32[]{:S(2)}, u32[]{:S(2)}) collective-permute-start(bf16[160,1024]{1,0:T(8,128)(2,1)} %get-tuple-element.79), channel_id=1, source_target_pairs={{0,8},{1,17},{2,10},{3,19},{4,12},{5,21},{6,14},{7,23},{8,0},{9,25... | collective-permute-start | bytes 983048 | tf_op jit(solution)/shard_map/ppermute | solution.py:411
  50.6 13.9 %collective-permute-start.1 = (bf16[160,1024]{1,0:T(8,128)(2,1)}, bf16[160,1024]{1,0:T(8,128)(2,1)S(1)}, u32[]{:S(2)}, u32[]{:S(2)}) collective-permute-start(bf16[160,1024]{1,0:T(8,128)(2,1)} %get-tuple-element.80), channel_id=1, source_target_pairs={{0,16},{1,9},{2,18},{3,11},{4,20},{5,13},{6,22},{7,15},{8,24},{9,1... | collective-permute-start | bytes 983048 | tf_op jit(solution)/shard_map/ppermute | solution.py:411
  52.1 12.4 %collective-permute-start.2 = (bf16[160,1024]{1,0:T(8,128)(2,1)}, bf16[160,1024]{1,0:T(8,128)(2,1)S(1)}, u32[]{:S(2)}, u32[]{:S(2)}) collective-permute-start(bf16[160,1024]{1,0:T(8,128)(2,1)} %get-tuple-element.81), channel_id=1, source_target_pairs={{0,8},{1,17},{2,10},{3,19},{4,12},{5,21},{6,14},{7,23},{8,0},{9,25... | collective-permute-start | bytes 983048 | tf_op jit(solution)/shard_map/ppermute | solution.py:411
  64.5 13.8 %collective-permute-start.3 = (bf16[320,1024]{1,0:T(8,128)(2,1)}, bf16[320,1024]{1,0:T(8,128)(2,1)S(1)}, u32[]{:S(2)}, u32[]{:S(2)}) collective-permute-start(bf16[320,1024]{1,0:T(8,128)(2,1)} %get-tuple-element.126.hidden_ref.refs_0_), channel_id=1, source_target_pairs={{0,8},{1,17},{2,10},{3,19},{4,12},{5,21},{6,14},{7,23},{8,0},{9,25... | collective-permute-start | bytes 1966088 | tf_op jit(solution)/shard_map/ppermute | solution.py:396
  66.1 10.7 %collective-permute-start.4 = (bf16[160,1024]{1,0:T(8,128)(2,1)S(1)}, bf16[160,1024]{1,0:T(8,128)(2,1)S(1)}, u32[]{:S(2)}, u32[]{:S(2)}) collective-permute-start(bf16[160,1024]{1,0:T(8,128)(2,1)S(1)} %collective-permute-done.2), channel_id=1, source_target_pairs={{0,16},{1,9},{2,18},{3,11},{4,20},{5,13},{6,22},{7,15},{8,24},{9,1... | collective-permute-start | bytes 983048 | tf_op jit(solution)/shard_map/ppermute | solution.py:411
  66.6 10.2 %collective-permute-start.5 = (bf16[160,1024]{1,0:T(8,128)(2,1)S(1)}, bf16[160,1024]{1,0:T(8,128)(2,1)S(1)}, u32[]{:S(2)}, u32[]{:S(2)}) collective-permute-start(bf16[160,1024]{1,0:T(8,128)(2,1)S(1)} %collective-permute-done.refs_1_), channel_id=1, source_target_pairs={{0,1},{1,0},{2,3},{3,2},{4,5},{5,4},{6,7},{7,6},{8,9},{9,8},{10,11... | collective-permute-start | bytes 983048 | tf_op jit(solution)/shard_map/ppermute | solution.py:345
  66.6 10.2 %collective-permute-start.6 = (bf16[160,1024]{1,0:T(8,128)(2,1)S(1)}, bf16[160,1024]{1,0:T(8,128)(2,1)S(1)}, u32[]{:S(2)}, u32[]{:S(2)}) collective-permute-start(bf16[160,1024]{1,0:T(8,128)(2,1)S(1)} %collective-permute-done.1.refs_2_), channel_id=1, source_target_pairs={{0,1},{1,0},{2,3},{3,2},{4,5},{5,4},{6,7},{7,6},{8,9},{9,8},{10,11... | collective-permute-start | bytes 983048 | tf_op jit(solution)/shard_map/ppermute | solution.py:345
  76.7 49.2 %copy-start.5 = (bf16[160,1024]{1,0:T(8,128)(2,1)}, bf16[160,1024]{1,0:T(8,128)(2,1)S(1)}, u32[]{:S(2)}) copy-start(bf16[160,1024]{1,0:T(8,128)(2,1)S(1)} %collective-permute-done.4.refs_3_) | copy-start | bytes 983044
  80.8 86.3 %reduce-scatter.5.cloned.1.call-start = ((), (), s32[]{:S(2)}) async-start(), calls=%async_computation.5 | async-start | bytes 2949120 | tf_op jit(solution)/shard_map/reduce_scatter | solution.py:432
  80.9 17.2 %collective-permute-start.7 = (bf16[320,1024]{1,0:T(8,128)(2,1)S(1)}, bf16[320,1024]{1,0:T(8,128)(2,1)S(1)}, u32[]{:S(2)}, u32[]{:S(2)}) collective-permute-start(bf16[320,1024]{1,0:T(8,128)(2,1)S(1)} %copy-done), channel_id=1, source_target_pairs={{0,16},{1,9},{2,18},{3,11},{4,20},{5,13},{6,22},{7,15},{8,24},{9,1... | collective-permute-start | bytes 1966088 | tf_op jit(solution)/shard_map/ppermute | solution.py:396
  85.2 12.8 %collective-permute-start.8 = (bf16[160,1024]{1,0:T(8,128)(2,1)}, bf16[160,1024]{1,0:T(8,128)(2,1)S(1)}, u32[]{:S(2)}, u32[]{:S(2)}) collective-permute-start(bf16[160,1024]{1,0:T(8,128)(2,1)} %get-tuple-element.99), channel_id=1, source_target_pairs={{0,8},{1,17},{2,10},{3,19},{4,12},{5,21},{6,14},{7,23},{8,0},{9,25... | collective-permute-start | bytes 983048 | tf_op jit(solution)/shard_map/ppermute | solution.py:411
  86.8 15.3 %collective-permute-start.9 = (bf16[160,1024]{1,0:T(8,128)(2,1)}, bf16[160,1024]{1,0:T(8,128)(2,1)}, u32[]{:S(2)}, u32[]{:S(2)}) collective-permute-start(bf16[160,1024]{1,0:T(8,128)(2,1)} %get-tuple-element.100), channel_id=1, source_target_pairs={{0,16},{1,9},{2,18},{3,11},{4,20},{5,13},{6,22},{7,15},{8,24},{9,1... | collective-permute-start | bytes 983048 | tf_op jit(solution)/shard_map/ppermute | solution.py:411
  87.3 16.0 %collective-permute-start.10 = (bf16[160,1024]{1,0:T(8,128)(2,1)}, bf16[160,1024]{1,0:T(8,128)(2,1)}, u32[]{:S(2)}, u32[]{:S(2)}) collective-permute-start(bf16[160,1024]{1,0:T(8,128)(2,1)} %get-tuple-element.101), channel_id=1, source_target_pairs={{0,8},{1,17},{2,10},{3,19},{4,12},{5,21},{6,14},{7,23},{8,0},{9,25... | collective-permute-start | bytes 983048 | tf_op jit(solution)/shard_map/ppermute | solution.py:411
  87.9 25.0 %collective-permute-start.13 = (bf16[320,1024]{1,0:T(8,128)(2,1)S(1)}, bf16[320,1024]{1,0:T(8,128)(2,1)S(1)}, u32[]{:S(2)}, u32[]{:S(2)}) collective-permute-start(bf16[320,1024]{1,0:T(8,128)(2,1)S(1)} %collective-permute-done.3.refs_1_), channel_id=1, source_target_pairs={{0,16},{1,9},{2,18},{3,11},{4,20},{5,13},{6,22},{7,15},{8,24},{9,1... | collective-permute-start | bytes 1966088 | tf_op jit(solution)/shard_map/ppermute | solution.py:396
  98.1 26.6 %copy-start.10 = (bf16[320,1024]{1,0:T(8,128)(2,1)}, bf16[320,1024]{1,0:T(8,128)(2,1)S(1)}, u32[]{:S(2)}) copy-start(bf16[320,1024]{1,0:T(8,128)(2,1)S(1)} %collective-permute-done.7.refs_2_) | copy-start | bytes 1966084
  98.1 26.6 %copy-start.17 = (bf16[160,1024]{1,0:T(8,128)(2,1)}, bf16[160,1024]{1,0:T(8,128)(2,1)S(1)}, u32[]{:S(2)}) copy-start(bf16[160,1024]{1,0:T(8,128)(2,1)S(1)} %collective-permute-done.8.refs_5_) | copy-start | bytes 983044
  103.3 21.4 %collective-permute-start.11 = (bf16[320,1024]{1,0:T(8,128)(2,1)}, bf16[320,1024]{1,0:T(8,128)(2,1)}, u32[]{:S(2)}, u32[]{:S(2)}) collective-permute-start(bf16[320,1024]{1,0:T(8,128)(2,1)} %get-tuple-element.107.dgate_ref.refs_7_), channel_id=1, source_target_pairs={{0,8},{1,17},{2,10},{3,19},{4,12},{5,21},{6,14},{7,23},{8,0},{9,25... | collective-permute-start | bytes 1966088 | tf_op jit(solution)/shard_map/ppermute | solution.py:396
  104.8 21.1 %collective-permute-start.12 = (bf16[320,1024]{1,0:T(8,128)(2,1)}, bf16[320,1024]{1,0:T(8,128)(2,1)S(1)}, u32[]{:S(2)}, u32[]{:S(2)}) collective-permute-start(bf16[320,1024]{1,0:T(8,128)(2,1)} %get-tuple-element.108.dup_ref.refs_7_), channel_id=1, source_target_pairs={{0,8},{1,17},{2,10},{3,19},{4,12},{5,21},{6,14},{7,23},{8,0},{9,25... | collective-permute-start | bytes 1966088 | tf_op jit(solution)/shard_map/ppermute | solution.py:396
  105.3 19.4 %collective-permute-start.14 = (bf16[160,1024]{1,0:T(8,128)(2,1)}, bf16[160,1024]{1,0:T(8,128)(2,1)}, u32[]{:S(2)}, u32[]{:S(2)}) collective-permute-start(bf16[160,1024]{1,0:T(8,128)(2,1)} %collective-permute-done.10), channel_id=1, source_target_pairs={{0,16},{1,9},{2,18},{3,11},{4,20},{5,13},{6,22},{7,15},{8,24},{9,1... | collective-permute-start | bytes 983048 | tf_op jit(solution)/shard_map/ppermute | solution.py:411
  105.9 18.8 %collective-permute-start.15 = (bf16[160,1024]{1,0:T(8,128)(2,1)S(1)}, bf16[160,1024]{1,0:T(8,128)(2,1)}, u32[]{:S(2)}, u32[]{:S(2)}) collective-permute-start(bf16[160,1024]{1,0:T(8,128)(2,1)S(1)} %collective-permute-done.8.refs_5_), channel_id=1, source_target_pairs={{0,1},{1,0},{2,3},{3,2},{4,5},{5,4},{6,7},{7,6},{8,9},{9,8},{10,11... | collective-permute-start | bytes 983048 | tf_op jit(solution)/shard_map/ppermute | solution.py:345
  112.9 11.8 %collective-permute-start.16 = (bf16[160,1024]{1,0:T(8,128)(2,1)}, bf16[160,1024]{1,0:T(8,128)(2,1)}, u32[]{:S(2)}, u32[]{:S(2)}) collective-permute-start(bf16[160,1024]{1,0:T(8,128)(2,1)} %collective-permute-done.9.refs_6_), channel_id=1, source_target_pairs={{0,1},{1,0},{2,3},{3,2},{4,5},{5,4},{6,7},{7,6},{8,9},{9,8},{10,11... | collective-permute-start | bytes 983048 | tf_op jit(solution)/shard_map/ppermute | solution.py:345
  125.9 15.3 %copy-start.11 = (bf16[320,1024]{1,0:T(8,128)(2,1)}, bf16[320,1024]{1,0:T(8,128)(2,1)S(1)}, u32[]{:S(2)}) copy-start(bf16[320,1024]{1,0:T(8,128)(2,1)S(1)} %collective-permute-done.12.refs_8_) | copy-start | bytes 1966084
  125.9 4.7 %collective-permute-start.19 = (bf16[160,1024]{1,0:T(8,128)(2,1)S(1)}, bf16[160,1024]{1,0:T(8,128)(2,1)S(1)}, u32[]{:S(2)}, u32[]{:S(2)}) collective-permute-start(bf16[160,1024]{1,0:T(8,128)(2,1)S(1)} %collective-permute-done.4.refs_3_), channel_id=1, source_target_pairs={{0,1},{1,0},{2,3},{3,2},{4,5},{5,4},{6,7},{7,6},{8,9},{9,8},{10,11... | collective-permute-start | bytes 983048 | tf_op jit(solution)/shard_map/ppermute | solution.py:345
  126.6 14.6 %collective-permute-start.21 = (bf16[320,1024]{1,0:T(8,128)(2,1)S(1)}, bf16[320,1024]{1,0:T(8,128)(2,1)S(1)}, u32[]{:S(2)}, u32[]{:S(2)}) collective-permute-start(bf16[320,1024]{1,0:T(8,128)(2,1)S(1)} %copy-done.2), channel_id=1, source_target_pairs={{0,16},{1,9},{2,18},{3,11},{4,20},{5,13},{6,22},{7,15},{8,24},{9,1... | collective-permute-start | bytes 1966088 | tf_op jit(solution)/shard_map/ppermute | solution.py:396
  128.0 16.1 %collective-permute-start.22 = (bf16[320,1024]{1,0:T(8,128)(2,1)}, bf16[320,1024]{1,0:T(8,128)(2,1)S(1)}, u32[]{:S(2)}, u32[]{:S(2)}) collective-permute-start(bf16[320,1024]{1,0:T(8,128)(2,1)} %collective-permute-done.11.refs_8_), channel_id=1, source_target_pairs={{0,16},{1,9},{2,18},{3,11},{4,20},{5,13},{6,22},{7,15},{8,24},{9,1... | collective-permute-start | bytes 1966088 | tf_op jit(solution)/shard_map/ppermute | solution.py:396
  128.6 24.5 %collective-permute-start.17 = (bf16[320,1024]{1,0:T(8,128)(2,1)S(1)}, bf16[320,1024]{1,0:T(8,128)(2,1)S(1)}, u32[]{:S(2)}, u32[]{:S(2)}) collective-permute-start(bf16[320,1024]{1,0:T(8,128)(2,1)S(1)} %copy-done.1), channel_id=1, source_target_pairs={{0,16},{1,9},{2,18},{3,11},{4,20},{5,13},{6,22},{7,15},{8,24},{9,1... | collective-permute-start | bytes 1966088 | tf_op jit(solution)/shard_map/ppermute | solution.py:396
  130.1 28.1 %collective-permute-start.18 = (bf16[320,1024]{1,0:T(8,128)(2,1)S(1)}, bf16[320,1024]{1,0:T(8,128)(2,1)S(1)}, u32[]{:S(2)}, u32[]{:S(2)}) collective-permute-start(bf16[320,1024]{1,0:T(8,128)(2,1)S(1)} %collective-permute-done.12.refs_8_), channel_id=1, source_target_pairs={{0,16},{1,9},{2,18},{3,11},{4,20},{5,13},{6,22},{7,15},{8,24},{9,1... | collective-permute-start | bytes 1966088 | tf_op jit(solution)/shard_map/ppermute | solution.py:396
  130.6 10.6 %copy-start.8 = (bf16[160,1024]{1,0:T(8,128)(2,1)}, bf16[160,1024]{1,0:T(8,128)(2,1)S(1)}, u32[]{:S(2)}) copy-start(bf16[160,1024]{1,0:T(8,128)(2,1)S(1)} %collective-permute-done.19.refs_6_) | copy-start | bytes 983044
  130.6 1.8 %collective-permute-start.20 = (bf16[160,1024]{1,0:T(8,128)(2,1)}, bf16[160,1024]{1,0:T(8,128)(2,1)S(1)}, u32[]{:S(2)}, u32[]{:S(2)}) collective-permute-start(bf16[160,1024]{1,0:T(8,128)(2,1)} %collective-permute-done.14.refs_7_), channel_id=1, source_target_pairs={{0,1},{1,0},{2,3},{3,2},{4,5},{5,4},{6,7},{7,6},{8,9},{9,8},{10,11... | collective-permute-start | bytes 983048 | tf_op jit(solution)/shard_map/ppermute | solution.py:345
  (14 other events, 70.1 us)
Sparse Core Ops, SparseCore 0:
  9.6 36.5 all-gather.2
  47.9 32.8 all-gather.4
  83.7 36.4 reduce-scatter.2
  126.0 36.6 reduce-scatter.4

commit v4 on v3

--- a/solution.py
+++ b/solution.py
@@ -471,13 +471,12 @@
 
     gates = over_groups(dgate, all_dgate, [1], range(2, groups))
     ups = over_groups(dup, all_dup, [1], range(2, groups))
-    hiddens.advance()
     gates.advance()
     ups.advance()
     for _ in range(phases - 1):
         across_up.advance()
     (partial,) = fence(
-        [gates, ups, hiddens, across, across_up],
+        [gates, ups, across, across_up],
         input_sum(dgate, dup, w_gate, w_up),
     )
     input_grad = over_line(partial)

time: 174 us -> 178 us (1.023)
  waiting for transfers between devices: 67.9 us -> 71.7 us
    ppermute x9, waiting for transfers between devices: 17.8 us -> 21.5 us  [gather_groups(): held.append(lax.ppermute(held[label - (1 << top)], ('dp', 'mp'), pairs))]
  transfers between devices with their start and end apart: 27 -> 27, of which waited for: 11 -> 10; matrix products, arithmetic and copies ran while one was open for 0% -> 0% of each run, Pallas kernels for 39% -> 38%
where the time goes in v4:
time: 178 us
  waiting for transfers between devices  71.7 us (40%)
  Pallas kernels  68.4 us (38%)
  starting transfers between devices  20.2 us (11%)
  between operations  14.2 us (8%)
  local copies, waits for them, and re-layouts  2.56 us (1%)
    pallas_call x9, Pallas kernels, call(): pl.pallas_call(body, grid=(steps,), in_specs=in_specs, out_specs=out_spec...  68.4 us
    all_gather x2, waiting for transfers between devices, from_line(): return lax.all_gather(value, 'mp', axis=0, tiled=True)  39.3 us
    ppermute x9, waiting for transfers between devices, gather_groups(): held.append(lax.ppermute(held[label - (1 << top)], ('dp', 'mp'), pairs))  21.5 us
    ppermute x9, starting transfers between devices, gather_groups(): held.append(lax.ppermute(held[label - (1 << top)], ('dp', 'mp'), pairs))  10.8 us
    ppermute x8, starting transfers between devices, exchange_groups(): lax.ppermute(mine[at], ('dp', 'mp'), left[at].pop(0))  8.18 us
    ppermute x8, waiting for transfers between devices, exchange_groups(): lax.ppermute(mine[at], ('dp', 'mp'), left[at].pop(0))  7.61 us
  transfers between devices with their start and end apart: 27, of which 10 were waited for; matrix products, arithmetic and copies ran while one was open for 0% of the time, Pallas kernels for 38%

profile of v4, /device:TPU:0, one launch (start us, length us, event | category | flops | bytes accessed | tf_op | source)
XLA Modules:
  0.0 177.6 jit_solution(7078080936789683824)
XLA Ops:
  9.4 36.9 %all-gather.3.cloned.1.call-done.rows_ref.x_in.refs_0_ = bf16[320,4096]{1,0:T(8,128)(2,1)} async-done(((bf16[40,4096]{1,0:T(8,128)(2,1)}), bf16[320,4096]{1,0:T(8,128)(2,1)}) %all-gather.3.cloned.1.call-update) | async-done | bytes 2621456 | tf_op jit(solution)/shard_map/all_gather | solution.py:429
  46.3 2.8 %shard_map.92 = (bf16[160,1024]{1,0:T(8,128)(2,1)}, bf16[160,1024]{1,0:T(8,128)(2,1)}, bf16[160,1024]{1,0:T(8,128)(2,1)}) custom-call(s32[3]{0:T(128)} %pad_add_fusion.where_ref, bf16[320,4096]{1,0:T(8,128)(2,1)} %all-gather.3.cloned.1.call-done.rows_ref.x_in.refs_0_), custom_call_target="tpu_custom_call" | custom-call | tf_op jit(solution)/shard_map/pallas_call | solution.py:39
  49.1 1.5 collective-permute-start
  50.6 1.5 collective-permute-start.1
  52.6 11.8 %shard_map.93 = (bf16[320,1024]{1,0:T(8,128)(2,1)}, f32[320,1024]{1,0:T(8,128)}, f32[320,1024]{1,0:T(8,128)}) custom-call(bf16[320,4096]{1,0:T(8,128)(2,1)} %all-gather.3.cloned.1.call-done.rows_ref.x_in.refs_0_, bf16[4096,1024]{1,0:T(8,128)(2,1)} %w_gate_ref.3, bf16[4096,1024]{1,0:T(8,128)(2,1)} %w_up_ref.3), custom_call_target="tpu_custom_call" | custom-call | tf_op jit(solution)/shard_map/pallas_call | solution.py:39
  64.5 1.6 collective-permute-start.3
  67.1 7.4 %shard_map.94 = bf16[320,4096]{1,0:T(8,128)(2,1)} custom-call(bf16[320,1024]{1,0:T(8,128)(2,1)} %get-tuple-element.124.hidden_ref.refs_0_, bf16[1024,4096]{1,0:T(8,128)(2,1)} %w_ref.3), custom_call_target="tpu_custom_call" | custom-call | tf_op jit(solution)/shard_map/pallas_call | solution.py:39
  74.5 2.2 %collective-permute-done.4.refs_3_ = bf16[160,1024]{1,0:T(8,128)(2,1)S(1)} collective-permute-done((bf16[160,1024]{1,0:T(8,128)(2,1)S(1)}, bf16[160,1024]{1,0:T(8,128)(2,1)S(1)}, u32[]{:S(2)}, u32[]{:S(2)}) %collective-permute-start.4) | collective-permute-done | bytes 327712 | tf_op jit(solution)/shard_map/ppermute | solution.py:411
  76.8 1.6 collective-permute-done.3.refs_1_
  78.3 2.5 %all-gather.5.cloned.1.call-done.rows_ref.x_in.refs_4_ = bf16[320,4096]{1,0:T(8,128)(2,1)} async-done(((bf16[40,4096]{1,0:T(8,128)(2,1)}), bf16[320,4096]{1,0:T(8,128)(2,1)}) %all-gather.5.cloned.1.call-update) | async-done | bytes 2621456 | tf_op jit(solution)/shard_map/all_gather | solution.py:429
  80.9 1.5 collective-permute-start.7
  82.4 2.8 %shard_map.95 = (bf16[160,1024]{1,0:T(8,128)(2,1)}, bf16[160,1024]{1,0:T(8,128)(2,1)}, bf16[160,1024]{1,0:T(8,128)(2,1)}) custom-call(s32[3]{0:T(128)} %pad_add_fusion.where_ref, bf16[320,4096]{1,0:T(8,128)(2,1)} %all-gather.5.cloned.1.call-done.rows_ref.x_in.refs_4_), custom_call_target="tpu_custom_call" | custom-call | tf_op jit(solution)/shard_map/pallas_call | solution.py:39
  85.3 1.5 collective-permute-start.8
  87.9 8.7 %shard_map.96 = (bf16[320,1024]{1,0:T(8,128)(2,1)}, bf16[320,1024]{1,0:T(8,128)(2,1)}) custom-call(bf16[320,4096]{1,0:T(8,128)(2,1)} %all-gather.5.cloned.1.call-done.rows_ref.x_in.refs_4_, bf16[1024,4096]{1,0:T(8,128)(2,1)} %w_ref.3, f32[320,1024]{1,0:T(8,128)} %get-tuple-element.102.swish_ref, f32[320,1024]{1,0:T(8,128)} %get-tuple-element.103.slope_ref), custom_call_target="tpu_custom_call" | custom-call | tf_op jit(solution)/shard_map/pallas_call | solution.py:39
  96.7 5.3 %collective-permute-done.9.refs_6_ = bf16[160,1024]{1,0:T(8,128)(2,1)} collective-permute-done((bf16[160,1024]{1,0:T(8,128)(2,1)}, bf16[160,1024]{1,0:T(8,128)(2,1)}, u32[]{:S(2)}, u32[]{:S(2)}) %collective-permute-start.9) | collective-permute-done | bytes 327712 | tf_op jit(solution)/shard_map/ppermute | solution.py:411
  102.0 1.6 collective-permute-start.11
  104.1 1.5 collective-permute-start.13
  106.1 10.9 %shard_map.97 = bf16[320,4096]{1,0:T(8,128)(2,1)} custom-call(bf16[320,1024]{1,0:T(8,128)(2,1)} %get-tuple-element.106.dgate_ref.refs_7_, bf16[320,1024]{1,0:T(8,128)(2,1)} %get-tuple-element.107.dup_ref.refs_7_, bf16[4096,1024]{1,0:T(8,128)(2,1)} %w_gate_ref.3, bf16[4096,1024]{1,0:T(8,128)(2,1)} %w_up_ref.3), custom_call_target="tpu_custom_call" | custom-call | tf_op jit(solution)/shard_map/pallas_call | solution.py:39
  117.1 6.4 %collective-permute-done.12.refs_8_ = bf16[320,1024]{1,0:T(8,128)(2,1)} collective-permute-done((bf16[320,1024]{1,0:T(8,128)(2,1)}, bf16[320,1024]{1,0:T(8,128)(2,1)}, u32[]{:S(2)}, u32[]{:S(2)}) %collective-permute-start.12) | collective-permute-done | bytes 655392 | tf_op jit(solution)/shard_map/ppermute | solution.py:396
  123.5 1.6 collective-permute-start.18
  125.7 1.5 collective-permute-start.22
  127.7 6.5 %collective-permute-done.18.refs_3_ = bf16[320,1024]{1,0:T(8,128)(2,1)S(1)} collective-permute-done((bf16[320,1024]{1,0:T(8,128)(2,1)S(1)}, bf16[320,1024]{1,0:T(8,128)(2,1)S(1)}, u32[]{:S(2)}, u32[]{:S(2)}) %collective-permute-start.18) | collective-permute-done | bytes 655392 | tf_op jit(solution)/shard_map/ppermute | solution.py:396
  134.2 1.5 collective-permute-start.17
  135.7 1.8 %collective-permute-done.20.refs_10_ = bf16[160,1024]{1,0:T(8,128)(2,1)S(1)} collective-permute-done((bf16[160,1024]{1,0:T(8,128)(2,1)}, bf16[160,1024]{1,0:T(8,128)(2,1)S(1)}, u32[]{:S(2)}, u32[]{:S(2)}) %collective-permute-start.20) | collective-permute-done | bytes 327712 | tf_op jit(solution)/shard_map/ppermute | solution.py:345
  137.5 0.7 copy-done.18
  138.2 8.0 %shard_map.98 = bf16[1024,1024]{1,0:T(8,128)(2,1)} custom-call(s32[3]{0:T(128)} %pad_add_fusion.where_ref, bf16[320,1024]{1,0:T(8,128)(2,1)} %get-tuple-element.124.hidden_ref.refs_0_, bf16[320,1024]{1,0:T(8,128)(2,1)} %copy-done.9, bf16[320,1024]{1,0:T(8,128)(2,1)} %copy-done.11, bf16[320,1024]{1,0:T(8,128)(2,1)} %copy-done.15, ...), custom_call_target="tpu_custom_call" | custom-call | tf_op jit(solution)/shard_map/pallas_call | solution.py:39
  146.3 1.9 %collective-permute-done.22.refs_10_ = bf16[320,1024]{1,0:T(8,128)(2,1)S(1)} collective-permute-done((bf16[320,1024]{1,0:T(8,128)(2,1)}, bf16[320,1024]{1,0:T(8,128)(2,1)S(1)}, u32[]{:S(2)}, u32[]{:S(2)}) %collective-permute-start.22) | collective-permute-done | bytes 655392 | tf_op jit(solution)/shard_map/ppermute | solution.py:396
  148.2 0.9 copy-done.16
  149.1 8.0 %shard_map.99 = bf16[1024,1024]{1,0:T(8,128)(2,1)} custom-call(s32[3]{0:T(128)} %pad_add_fusion.where_ref, bf16[320,4096]{1,0:T(8,128)(2,1)} %all-gather.3.cloned.1.call-done.rows_ref.x_in.refs_0_, bf16[160,1024]{1,0:T(8,128)(2,1)} %copy-done.3, bf16[160,1024]{1,0:T(8,128)(2,1)} %copy-done.4, bf16[160,1024]{1,0:T(8,128)(2,1)} %copy-done.5, ...), custom_call_target="tpu_custom_call" | custom-call | tf_op jit(solution)/shard_map/pallas_call | solution.py:39
  157.2 5.1 %collective-permute-done.17.refs_10_ = bf16[320,1024]{1,0:T(8,128)(2,1)S(1)} collective-permute-done((bf16[320,1024]{1,0:T(8,128)(2,1)}, bf16[320,1024]{1,0:T(8,128)(2,1)S(1)}, u32[]{:S(2)}, u32[]{:S(2)}) %collective-permute-start.17) | collective-permute-done | bytes 655392 | tf_op jit(solution)/shard_map/ppermute | solution.py:396
  162.3 0.8 copy-done.13
  163.1 8.0 %shard_map.100 = bf16[1024,1024]{1,0:T(8,128)(2,1)} custom-call(s32[3]{0:T(128)} %pad_add_fusion.where_ref, bf16[320,4096]{1,0:T(8,128)(2,1)} %all-gather.3.cloned.1.call-done.rows_ref.x_in.refs_0_, bf16[160,1024]{1,0:T(8,128)(2,1)} %copy-done.3, bf16[160,1024]{1,0:T(8,128)(2,1)} %copy-done.4, bf16[160,1024]{1,0:T(8,128)(2,1)} %copy-done.5, ...), custom_call_target="tpu_custom_call" | custom-call | tf_op jit(solution)/shard_map/pallas_call | solution.py:39
  (74 shorter events, 7.1 us)
Async XLA Ops:
  7.2 39.1 %all-gather.3.cloned.1.call-start = ((), (), s32[]{:S(2)}) async-start(), calls=%async_computation.2 | async-start | bytes 2949120 | tf_op jit(solution)/shard_map/all_gather | solution.py:429
  7.9 72.9 %all-gather.5.cloned.1.call-start = ((), (), s32[]{:S(2)}) async-start(), calls=%async_computation.3 | async-start | bytes 2949120 | tf_op jit(solution)/shard_map/all_gather | solution.py:429
  8.6 162.4 %reduce-scatter.3.cloned.1.call-start = ((), (), s32[]{:S(2)}) async-start(), calls=%async_computation.4 | async-start | bytes 2949120 | tf_op jit(solution)/shard_map/reduce_scatter | solution.py:432
  49.1 15.4 %collective-permute-start = (bf16[160,1024]{1,0:T(8,128)(2,1)}, bf16[160,1024]{1,0:T(8,128)(2,1)S(1)}, u32[]{:S(2)}, u32[]{:S(2)}) collective-permute-start(bf16[160,1024]{1,0:T(8,128)(2,1)} %get-tuple-element.78), channel_id=1, source_target_pairs={{0,8},{1,17},{2,10},{3,19},{4,12},{5,21},{6,14},{7,23},{8,0},{9,25... | collective-permute-start | bytes 983048 | tf_op jit(solution)/shard_map/ppermute | solution.py:411
  50.6 13.9 %collective-permute-start.1 = (bf16[160,1024]{1,0:T(8,128)(2,1)}, bf16[160,1024]{1,0:T(8,128)(2,1)S(1)}, u32[]{:S(2)}, u32[]{:S(2)}) collective-permute-start(bf16[160,1024]{1,0:T(8,128)(2,1)} %get-tuple-element.79), channel_id=1, source_target_pairs={{0,16},{1,9},{2,18},{3,11},{4,20},{5,13},{6,22},{7,15},{8,24},{9,1... | collective-permute-start | bytes 983048 | tf_op jit(solution)/shard_map/ppermute | solution.py:411
  52.1 12.4 %collective-permute-start.2 = (bf16[160,1024]{1,0:T(8,128)(2,1)}, bf16[160,1024]{1,0:T(8,128)(2,1)S(1)}, u32[]{:S(2)}, u32[]{:S(2)}) collective-permute-start(bf16[160,1024]{1,0:T(8,128)(2,1)} %get-tuple-element.80), channel_id=1, source_target_pairs={{0,8},{1,17},{2,10},{3,19},{4,12},{5,21},{6,14},{7,23},{8,0},{9,25... | collective-permute-start | bytes 983048 | tf_op jit(solution)/shard_map/ppermute | solution.py:411
  64.5 13.8 %collective-permute-start.3 = (bf16[320,1024]{1,0:T(8,128)(2,1)}, bf16[320,1024]{1,0:T(8,128)(2,1)S(1)}, u32[]{:S(2)}, u32[]{:S(2)}) collective-permute-start(bf16[320,1024]{1,0:T(8,128)(2,1)} %get-tuple-element.124.hidden_ref.refs_0_), channel_id=1, source_target_pairs={{0,8},{1,17},{2,10},{3,19},{4,12},{5,21},{6,14},{7,23},{8,0},{9,25... | collective-permute-start | bytes 1966088 | tf_op jit(solution)/shard_map/ppermute | solution.py:396
  66.1 10.7 %collective-permute-start.4 = (bf16[160,1024]{1,0:T(8,128)(2,1)S(1)}, bf16[160,1024]{1,0:T(8,128)(2,1)S(1)}, u32[]{:S(2)}, u32[]{:S(2)}) collective-permute-start(bf16[160,1024]{1,0:T(8,128)(2,1)S(1)} %collective-permute-done.2), channel_id=1, source_target_pairs={{0,16},{1,9},{2,18},{3,11},{4,20},{5,13},{6,22},{7,15},{8,24},{9,1... | collective-permute-start | bytes 983048 | tf_op jit(solution)/shard_map/ppermute | solution.py:411
  66.6 10.2 %collective-permute-start.5 = (bf16[160,1024]{1,0:T(8,128)(2,1)S(1)}, bf16[160,1024]{1,0:T(8,128)(2,1)S(1)}, u32[]{:S(2)}, u32[]{:S(2)}) collective-permute-start(bf16[160,1024]{1,0:T(8,128)(2,1)S(1)} %collective-permute-done.refs_1_), channel_id=1, source_target_pairs={{0,1},{1,0},{2,3},{3,2},{4,5},{5,4},{6,7},{7,6},{8,9},{9,8},{10,11... | collective-permute-start | bytes 983048 | tf_op jit(solution)/shard_map/ppermute | solution.py:345
  66.6 10.2 %collective-permute-start.6 = (bf16[160,1024]{1,0:T(8,128)(2,1)S(1)}, bf16[160,1024]{1,0:T(8,128)(2,1)S(1)}, u32[]{:S(2)}, u32[]{:S(2)}) collective-permute-start(bf16[160,1024]{1,0:T(8,128)(2,1)S(1)} %collective-permute-done.1.refs_2_), channel_id=1, source_target_pairs={{0,1},{1,0},{2,3},{3,2},{4,5},{5,4},{6,7},{7,6},{8,9},{9,8},{10,11... | collective-permute-start | bytes 983048 | tf_op jit(solution)/shard_map/ppermute | solution.py:345
  76.7 48.3 %copy-start.5 = (bf16[160,1024]{1,0:T(8,128)(2,1)}, bf16[160,1024]{1,0:T(8,128)(2,1)S(1)}, u32[]{:S(2)}) copy-start(bf16[160,1024]{1,0:T(8,128)(2,1)S(1)} %collective-permute-done.4.refs_3_) | copy-start | bytes 983044
  80.8 90.3 %reduce-scatter.5.cloned.1.call-start = ((), (), s32[]{:S(2)}) async-start(), calls=%async_computation.5 | async-start | bytes 2949120 | tf_op jit(solution)/shard_map/reduce_scatter | solution.py:432
  80.9 15.8 %collective-permute-start.7 = (bf16[320,1024]{1,0:T(8,128)(2,1)S(1)}, bf16[320,1024]{1,0:T(8,128)(2,1)S(1)}, u32[]{:S(2)}, u32[]{:S(2)}) collective-permute-start(bf16[320,1024]{1,0:T(8,128)(2,1)S(1)} %copy-done), channel_id=1, source_target_pairs={{0,16},{1,9},{2,18},{3,11},{4,20},{5,13},{6,22},{7,15},{8,24},{9,1... | collective-permute-start | bytes 1966088 | tf_op jit(solution)/shard_map/ppermute | solution.py:396
  85.3 11.4 %collective-permute-start.8 = (bf16[160,1024]{1,0:T(8,128)(2,1)}, bf16[160,1024]{1,0:T(8,128)(2,1)S(1)}, u32[]{:S(2)}, u32[]{:S(2)}) collective-permute-start(bf16[160,1024]{1,0:T(8,128)(2,1)} %get-tuple-element.98), channel_id=1, source_target_pairs={{0,8},{1,17},{2,10},{3,19},{4,12},{5,21},{6,14},{7,23},{8,0},{9,25... | collective-permute-start | bytes 983048 | tf_op jit(solution)/shard_map/ppermute | solution.py:411
  86.8 15.2 %collective-permute-start.9 = (bf16[160,1024]{1,0:T(8,128)(2,1)}, bf16[160,1024]{1,0:T(8,128)(2,1)}, u32[]{:S(2)}, u32[]{:S(2)}) collective-permute-start(bf16[160,1024]{1,0:T(8,128)(2,1)} %get-tuple-element.99), channel_id=1, source_target_pairs={{0,16},{1,9},{2,18},{3,11},{4,20},{5,13},{6,22},{7,15},{8,24},{9,1... | collective-permute-start | bytes 983048 | tf_op jit(solution)/shard_map/ppermute | solution.py:411
  87.3 14.7 %collective-permute-start.10 = (bf16[160,1024]{1,0:T(8,128)(2,1)}, bf16[160,1024]{1,0:T(8,128)(2,1)}, u32[]{:S(2)}, u32[]{:S(2)}) collective-permute-start(bf16[160,1024]{1,0:T(8,128)(2,1)} %get-tuple-element.100), channel_id=1, source_target_pairs={{0,8},{1,17},{2,10},{3,19},{4,12},{5,21},{6,14},{7,23},{8,0},{9,25... | collective-permute-start | bytes 983048 | tf_op jit(solution)/shard_map/ppermute | solution.py:411
  96.7 20.3 %copy-start.11 = (bf16[320,1024]{1,0:T(8,128)(2,1)}, bf16[320,1024]{1,0:T(8,128)(2,1)S(1)}, u32[]{:S(2)}) copy-start(bf16[320,1024]{1,0:T(8,128)(2,1)S(1)} %collective-permute-done.7.refs_2_) | copy-start | bytes 1966084
  96.7 20.3 %copy-start.17 = (bf16[160,1024]{1,0:T(8,128)(2,1)}, bf16[160,1024]{1,0:T(8,128)(2,1)S(1)}, u32[]{:S(2)}) copy-start(bf16[160,1024]{1,0:T(8,128)(2,1)S(1)} %collective-permute-done.8.refs_5_) | copy-start | bytes 983044
  102.0 15.0 %collective-permute-start.11 = (bf16[320,1024]{1,0:T(8,128)(2,1)}, bf16[320,1024]{1,0:T(8,128)(2,1)}, u32[]{:S(2)}, u32[]{:S(2)}) collective-permute-start(bf16[320,1024]{1,0:T(8,128)(2,1)} %get-tuple-element.106.dgate_ref.refs_7_), channel_id=1, source_target_pairs={{0,8},{1,17},{2,10},{3,19},{4,12},{5,21},{6,14},{7,23},{8,0},{9,25... | collective-permute-start | bytes 1966088 | tf_op jit(solution)/shard_map/ppermute | solution.py:396
  103.6 19.8 %collective-permute-start.12 = (bf16[320,1024]{1,0:T(8,128)(2,1)}, bf16[320,1024]{1,0:T(8,128)(2,1)}, u32[]{:S(2)}, u32[]{:S(2)}) collective-permute-start(bf16[320,1024]{1,0:T(8,128)(2,1)} %get-tuple-element.107.dup_ref.refs_7_), channel_id=1, source_target_pairs={{0,8},{1,17},{2,10},{3,19},{4,12},{5,21},{6,14},{7,23},{8,0},{9,25... | collective-permute-start | bytes 1966088 | tf_op jit(solution)/shard_map/ppermute | solution.py:396
  104.1 13.0 %collective-permute-start.13 = (bf16[160,1024]{1,0:T(8,128)(2,1)}, bf16[160,1024]{1,0:T(8,128)(2,1)}, u32[]{:S(2)}, u32[]{:S(2)}) collective-permute-start(bf16[160,1024]{1,0:T(8,128)(2,1)} %collective-permute-done.10), channel_id=1, source_target_pairs={{0,16},{1,9},{2,18},{3,11},{4,20},{5,13},{6,22},{7,15},{8,24},{9,1... | collective-permute-start | bytes 983048 | tf_op jit(solution)/shard_map/ppermute | solution.py:411
  105.6 11.5 %collective-permute-start.14 = (bf16[160,1024]{1,0:T(8,128)(2,1)S(1)}, bf16[160,1024]{1,0:T(8,128)(2,1)}, u32[]{:S(2)}, u32[]{:S(2)}) collective-permute-start(bf16[160,1024]{1,0:T(8,128)(2,1)S(1)} %collective-permute-done.8.refs_5_), channel_id=1, source_target_pairs={{0,1},{1,0},{2,3},{3,2},{4,5},{5,4},{6,7},{7,6},{8,9},{9,8},{10,11... | collective-permute-start | bytes 983048 | tf_op jit(solution)/shard_map/ppermute | solution.py:345
  105.6 11.5 %collective-permute-start.15 = (bf16[160,1024]{1,0:T(8,128)(2,1)}, bf16[160,1024]{1,0:T(8,128)(2,1)}, u32[]{:S(2)}, u32[]{:S(2)}) collective-permute-start(bf16[160,1024]{1,0:T(8,128)(2,1)} %collective-permute-done.9.refs_6_), channel_id=1, source_target_pairs={{0,1},{1,0},{2,3},{3,2},{4,5},{5,4},{6,7},{7,6},{8,9},{9,8},{10,11... | collective-permute-start | bytes 983048 | tf_op jit(solution)/shard_map/ppermute | solution.py:345
  117.0 10.2 %copy-start.1 = (bf16[320,1024]{1,0:T(8,128)(2,1)S(1)}, bf16[320,1024]{1,0:T(8,128)(2,1)}, u32[]{:S(2)}) copy-start(bf16[320,1024]{1,0:T(8,128)(2,1)} %get-tuple-element.107.dup_ref.refs_7_) | copy-start | bytes 1966084
  123.5 10.7 %collective-permute-start.18 = (bf16[320,1024]{1,0:T(8,128)(2,1)S(1)}, bf16[320,1024]{1,0:T(8,128)(2,1)S(1)}, u32[]{:S(2)}, u32[]{:S(2)}) collective-permute-start(bf16[320,1024]{1,0:T(8,128)(2,1)S(1)} %copy-done.10), channel_id=1, source_target_pairs={{0,16},{1,9},{2,18},{3,11},{4,20},{5,13},{6,22},{7,15},{8,24},{9,1... | collective-permute-start | bytes 1966088 | tf_op jit(solution)/shard_map/ppermute | solution.py:396
  125.1 10.6 %collective-permute-start.19 = (bf16[160,1024]{1,0:T(8,128)(2,1)S(1)}, bf16[160,1024]{1,0:T(8,128)(2,1)S(1)}, u32[]{:S(2)}, u32[]{:S(2)}) collective-permute-start(bf16[160,1024]{1,0:T(8,128)(2,1)S(1)} %collective-permute-done.4.refs_3_), channel_id=1, source_target_pairs={{0,1},{1,0},{2,3},{3,2},{4,5},{5,4},{6,7},{7,6},{8,9},{9,8},{10,11... | collective-permute-start | bytes 983048 | tf_op jit(solution)/shard_map/ppermute | solution.py:345
  125.1 21.2 %collective-permute-start.21 = (bf16[320,1024]{1,0:T(8,128)(2,1)S(1)}, bf16[320,1024]{1,0:T(8,128)(2,1)S(1)}, u32[]{:S(2)}, u32[]{:S(2)}) collective-permute-start(bf16[320,1024]{1,0:T(8,128)(2,1)S(1)} %copy-done.2), channel_id=1, source_target_pairs={{0,16},{1,9},{2,18},{3,11},{4,20},{5,13},{6,22},{7,15},{8,24},{9,1... | collective-permute-start | bytes 1966088 | tf_op jit(solution)/shard_map/ppermute | solution.py:396
  125.7 22.5 %collective-permute-start.22 = (bf16[320,1024]{1,0:T(8,128)(2,1)}, bf16[320,1024]{1,0:T(8,128)(2,1)S(1)}, u32[]{:S(2)}, u32[]{:S(2)}) collective-permute-start(bf16[320,1024]{1,0:T(8,128)(2,1)} %collective-permute-done.11.refs_8_), channel_id=1, source_target_pairs={{0,16},{1,9},{2,18},{3,11},{4,20},{5,13},{6,22},{7,15},{8,24},{9,1... | collective-permute-start | bytes 1966088 | tf_op jit(solution)/shard_map/ppermute | solution.py:396
  127.2 30.0 %collective-permute-start.16 = (bf16[320,1024]{1,0:T(8,128)(2,1)S(1)}, bf16[320,1024]{1,0:T(8,128)(2,1)S(1)}, u32[]{:S(2)}, u32[]{:S(2)}) collective-permute-start(bf16[320,1024]{1,0:T(8,128)(2,1)S(1)} %copy-done.1), channel_id=1, source_target_pairs={{0,16},{1,9},{2,18},{3,11},{4,20},{5,13},{6,22},{7,15},{8,24},{9,1... | collective-permute-start | bytes 1966088 | tf_op jit(solution)/shard_map/ppermute | solution.py:396
  134.2 28.1 %collective-permute-start.17 = (bf16[320,1024]{1,0:T(8,128)(2,1)}, bf16[320,1024]{1,0:T(8,128)(2,1)S(1)}, u32[]{:S(2)}, u32[]{:S(2)}) collective-permute-start(bf16[320,1024]{1,0:T(8,128)(2,1)} %collective-permute-done.12.refs_8_), channel_id=1, source_target_pairs={{0,16},{1,9},{2,18},{3,11},{4,20},{5,13},{6,22},{7,15},{8,24},{9,1... | collective-permute-start | bytes 1966088 | tf_op jit(solution)/shard_map/ppermute | solution.py:396
  135.7 10.6 %copy-start.8 = (bf16[160,1024]{1,0:T(8,128)(2,1)}, bf16[160,1024]{1,0:T(8,128)(2,1)S(1)}, u32[]{:S(2)}) copy-start(bf16[160,1024]{1,0:T(8,128)(2,1)S(1)} %collective-permute-done.19.refs_6_) | copy-start | bytes 983044
  135.7 1.8 %collective-permute-start.20 = (bf16[160,1024]{1,0:T(8,128)(2,1)}, bf16[160,1024]{1,0:T(8,128)(2,1)S(1)}, u32[]{:S(2)}, u32[]{:S(2)}) collective-permute-start(bf16[160,1024]{1,0:T(8,128)(2,1)} %collective-permute-done.13.refs_7_), channel_id=1, source_target_pairs={{0,1},{1,0},{2,3},{3,2},{4,5},{5,4},{6,7},{7,6},{8,9},{9,8},{10,11... | collective-permute-start | bytes 983048 | tf_op jit(solution)/shard_map/ppermute | solution.py:345
  (14 other events, 77.7 us)
Sparse Core Ops, SparseCore 0:
  9.6 36.5 all-gather.2
  47.9 32.8 all-gather.4
  83.7 36.4 reduce-scatter.2
  123.6 36.4 reduce-scatter.4

commit v5 on v2

--- a/solution.py
+++ b/solution.py
@@ -452,13 +452,12 @@
         [across], *forward(after(gathered, blocks), w_gate, w_up)
     )
 
-    hiddens = over_groups(hidden, all_hidden, [1], range(2, last), [last])
+    hiddens = over_groups(hidden, all_hidden, range(1, last), [last])
     hiddens.advance()
     for _ in range(phases - 1):
         across.advance()
     (partial,) = fence([hiddens, across], project(hidden, w_down))
 
-    hiddens.advance()
     upstream, partial = fence([across], upstream, partial)
     mixed = over_line(partial)
 

time: 174 us -> 175 us (level)
  waiting for transfers between devices: 67.5 us -> 69.7 us
    ppermute x8, waiting for transfers between devices: 10.4 us -> 16.4 us  [exchange_groups(): lax.ppermute(mine[at], ('dp', 'mp'), left[at].pop(0))]
    ppermute x8, starting transfers between devices: 7.25 us -> 10.1 us  [exchange_groups(): lax.ppermute(mine[at], ('dp', 'mp'), left[at].pop(0))]
    ppermute x9, starting transfers between devices: 12.5 us -> 9.68 us  [gather_groups(): held.append(lax.ppermute(held[label - (1 << top)], ('dp', 'mp'), pairs))]
    all_gather x2, waiting for transfers between devices: 39.3 us -> 36.9 us  [from_line(): return lax.all_gather(value, 'mp', axis=0, tiled=True)]
  transfers between devices with their start and end apart: 27 -> 27, of which waited for: 12 -> 10; matrix products, arithmetic and copies ran while one was open for 0% -> 0% of each run, Pallas kernels for 40% -> 39%
where the time goes in v5:
time: 175 us
  waiting for transfers between devices  69.7 us (40%)
  Pallas kernels  68.2 us (39%)
  starting transfers between devices  21.5 us (12%)
  between operations  14.1 us (8%)
    pallas_call x9, Pallas kernels, call(): pl.pallas_call(body, grid=(steps,), in_specs=in_specs, out_specs=out_spec...  68.2 us
    all_gather x2, waiting for transfers between devices, from_line(): return lax.all_gather(value, 'mp', axis=0, tiled=True)  36.9 us
    ppermute x8, waiting for transfers between devices, exchange_groups(): lax.ppermute(mine[at], ('dp', 'mp'), left[at].pop(0))  16.4 us
    ppermute x9, waiting for transfers between devices, gather_groups(): held.append(lax.ppermute(held[label - (1 << top)], ('dp', 'mp'), pairs))  13.6 us
    ppermute x8, starting transfers between devices, exchange_groups(): lax.ppermute(mine[at], ('dp', 'mp'), left[at].pop(0))  10.1 us
    ppermute x9, starting transfers between devices, gather_groups(): held.append(lax.ppermute(held[label - (1 << top)], ('dp', 'mp'), pairs))  9.68 us
  transfers between devices with their start and end apart: 27, of which 10 were waited for; matrix products, arithmetic and copies ran while one was open for 0% of the time, Pallas kernels for 39%

profile of v5, /device:TPU:0, one launch (start us, length us, event | category | flops | bytes accessed | tf_op | source)
XLA Modules:
  0.0 175.0 jit_solution(15903262980216117456)
XLA Ops:
  9.3 36.9 %all-gather.3.cloned.1.call-done.rows_ref.x_in.refs_0_ = bf16[320,4096]{1,0:T(8,128)(2,1)} async-done(((bf16[40,4096]{1,0:T(8,128)(2,1)}), bf16[320,4096]{1,0:T(8,128)(2,1)}) %all-gather.3.cloned.1.call-update) | async-done | bytes 2621456 | tf_op jit(solution)/shard_map/all_gather | solution.py:429
  46.3 2.8 %shard_map.92 = (bf16[160,1024]{1,0:T(8,128)(2,1)}, bf16[160,1024]{1,0:T(8,128)(2,1)}, bf16[160,1024]{1,0:T(8,128)(2,1)}) custom-call(s32[3]{0:T(128)} %pad_add_fusion.where_ref, bf16[320,4096]{1,0:T(8,128)(2,1)} %all-gather.3.cloned.1.call-done.rows_ref.x_in.refs_0_), custom_call_target="tpu_custom_call" | custom-call | tf_op jit(solution)/shard_map/pallas_call | solution.py:39
  49.1 1.5 collective-permute-start
  50.6 1.5 collective-permute-start.1
  52.6 11.8 %shard_map.93 = (bf16[320,1024]{1,0:T(8,128)(2,1)}, f32[320,1024]{1,0:T(8,128)}, f32[320,1024]{1,0:T(8,128)}) custom-call(bf16[320,4096]{1,0:T(8,128)(2,1)} %all-gather.3.cloned.1.call-done.rows_ref.x_in.refs_0_, bf16[4096,1024]{1,0:T(8,128)(2,1)} %w_gate_ref.3, bf16[4096,1024]{1,0:T(8,128)(2,1)} %w_up_ref.3), custom_call_target="tpu_custom_call" | custom-call | tf_op jit(solution)/shard_map/pallas_call | solution.py:39
  65.1 1.5 collective-permute-start.3
  66.6 1.5 collective-permute-start.5
  68.6 7.2 %shard_map.94 = bf16[320,4096]{1,0:T(8,128)(2,1)} custom-call(bf16[320,1024]{1,0:T(8,128)(2,1)} %get-tuple-element.124.hidden_ref.refs_0_, bf16[1024,4096]{1,0:T(8,128)(2,1)} %w_ref.3), custom_call_target="tpu_custom_call" | custom-call | tf_op jit(solution)/shard_map/pallas_call | solution.py:39
  75.8 8.6 %collective-permute-done.5.refs_3_ = bf16[160,1024]{1,0:T(8,128)(2,1)S(1)} collective-permute-done((bf16[160,1024]{1,0:T(8,128)(2,1)S(1)}, bf16[160,1024]{1,0:T(8,128)(2,1)S(1)}, u32[]{:S(2)}, u32[]{:S(2)}) %collective-permute-start.5) | collective-permute-done | bytes 327712 | tf_op jit(solution)/shard_map/ppermute | solution.py:411
  84.6 2.8 %shard_map.95 = (bf16[160,1024]{1,0:T(8,128)(2,1)}, bf16[160,1024]{1,0:T(8,128)(2,1)}, bf16[160,1024]{1,0:T(8,128)(2,1)}) custom-call(s32[3]{0:T(128)} %pad_add_fusion.where_ref, bf16[320,4096]{1,0:T(8,128)(2,1)} %all-gather.5.cloned.1.call-done.rows_ref.x_in.refs_4_), custom_call_target="tpu_custom_call" | custom-call | tf_op jit(solution)/shard_map/pallas_call | solution.py:39
  87.5 1.7 collective-permute-start.8
  89.2 1.5 collective-permute-start.9
  91.0 8.7 %shard_map.96 = (bf16[320,1024]{1,0:T(8,128)(2,1)}, bf16[320,1024]{1,0:T(8,128)(2,1)}) custom-call(bf16[320,4096]{1,0:T(8,128)(2,1)} %all-gather.5.cloned.1.call-done.rows_ref.x_in.refs_4_, bf16[1024,4096]{1,0:T(8,128)(2,1)} %w_ref.3, f32[320,1024]{1,0:T(8,128)} %get-tuple-element.107.swish_ref, f32[320,1024]{1,0:T(8,128)} %get-tuple-element.108.slope_ref), custom_call_target="tpu_custom_call" | custom-call | tf_op jit(solution)/shard_map/pallas_call | solution.py:39
  100.1 1.8 %collective-permute-done.10 = bf16[160,1024]{1,0:T(8,128)(2,1)} collective-permute-done((bf16[160,1024]{1,0:T(8,128)(2,1)}, bf16[160,1024]{1,0:T(8,128)(2,1)}, u32[]{:S(2)}, u32[]{:S(2)}) %collective-permute-start.10) | collective-permute-done | bytes 327712 | tf_op jit(solution)/shard_map/ppermute | solution.py:411
  101.9 0.8 collective-permute-start.12
  103.1 1.5 collective-permute-start.13
  105.1 10.9 %shard_map.97 = bf16[320,4096]{1,0:T(8,128)(2,1)} custom-call(bf16[320,1024]{1,0:T(8,128)(2,1)} %get-tuple-element.111.dgate_ref.refs_7_, bf16[320,1024]{1,0:T(8,128)(2,1)} %get-tuple-element.119.dup_ref.refs_7_, bf16[4096,1024]{1,0:T(8,128)(2,1)} %w_gate_ref.3, bf16[4096,1024]{1,0:T(8,128)(2,1)} %w_up_ref.3), custom_call_target="tpu_custom_call" | custom-call | tf_op jit(solution)/shard_map/pallas_call | solution.py:39
  116.1 5.6 %collective-permute-done.13.refs_7_ = bf16[160,1024]{1,0:T(8,128)(2,1)} collective-permute-done((bf16[160,1024]{1,0:T(8,128)(2,1)}, bf16[160,1024]{1,0:T(8,128)(2,1)}, u32[]{:S(2)}, u32[]{:S(2)}) %collective-permute-start.13) | collective-permute-done | bytes 327712 | tf_op jit(solution)/shard_map/ppermute | solution.py:411
  121.7 1.5 collective-permute-start.17
  123.3 1.4 collective-permute-start.19
  124.7 0.8 collective-permute-start.18
  126.0 1.3 collective-permute-done.21.refs_10_
  127.3 1.2 collective-permute-start.16
  128.6 8.0 %shard_map.98 = bf16[1024,1024]{1,0:T(8,128)(2,1)} custom-call(s32[3]{0:T(128)} %pad_add_fusion.where_ref, bf16[320,1024]{1,0:T(8,128)(2,1)} %get-tuple-element.124.hidden_ref.refs_0_, bf16[320,1024]{1,0:T(8,128)(2,1)} %collective-permute-done.3.refs_1_, bf16[320,1024]{1,0:T(8,128)(2,1)} %copy-done.8, bf16[320,1024]{1,0:T(8,128)(2,1)} %copy-done.10, ...), custom_call_target="tpu_custom_call" | custom-call | tf_op jit(solution)/shard_map/pallas_call | solution.py:39
  136.6 2.0 %collective-permute-done.17.refs_9_ = bf16[320,1024]{1,0:T(8,128)(2,1)S(1)} collective-permute-done((bf16[320,1024]{1,0:T(8,128)(2,1)S(1)}, bf16[320,1024]{1,0:T(8,128)(2,1)S(1)}, u32[]{:S(2)}, u32[]{:S(2)}) %collective-permute-start.17) | collective-permute-done | bytes 655392 | tf_op jit(solution)/shard_map/ppermute | solution.py:396
  138.6 2.4 %collective-permute-done.19.refs_8_ = bf16[320,1024]{1,0:T(8,128)(2,1)S(1)} collective-permute-done((bf16[320,1024]{1,0:T(8,128)(2,1)S(1)}, bf16[320,1024]{1,0:T(8,128)(2,1)S(1)}, u32[]{:S(2)}, u32[]{:S(2)}) %collective-permute-start.19) | collective-permute-done | bytes 655392 | tf_op jit(solution)/shard_map/ppermute | solution.py:396
  141.0 4.6 %collective-permute-done.18.refs_10_ = bf16[320,1024]{1,0:T(8,128)(2,1)S(1)} collective-permute-done((bf16[320,1024]{1,0:T(8,128)(2,1)S(1)}, bf16[320,1024]{1,0:T(8,128)(2,1)S(1)}, u32[]{:S(2)}, u32[]{:S(2)}) %collective-permute-start.18) | collective-permute-done | bytes 655392 | tf_op jit(solution)/shard_map/ppermute | solution.py:396
  145.6 1.5 collective-permute-start.22
  147.1 8.0 %shard_map.99 = bf16[1024,1024]{1,0:T(8,128)(2,1)} custom-call(s32[3]{0:T(128)} %pad_add_fusion.where_ref, bf16[320,4096]{1,0:T(8,128)(2,1)} %all-gather.3.cloned.1.call-done.rows_ref.x_in.refs_0_, bf16[160,1024]{1,0:T(8,128)(2,1)} %copy-done.2, bf16[160,1024]{1,0:T(8,128)(2,1)} %copy-done.3, bf16[160,1024]{1,0:T(8,128)(2,1)} %copy-done.4, ...), custom_call_target="tpu_custom_call" | custom-call | tf_op jit(solution)/shard_map/pallas_call | solution.py:39
  155.1 4.5 %collective-permute-done.22.refs_10_ = bf16[320,1024]{1,0:T(8,128)(2,1)S(1)} collective-permute-done((bf16[320,1024]{1,0:T(8,128)(2,1)S(1)}, bf16[320,1024]{1,0:T(8,128)(2,1)S(1)}, u32[]{:S(2)}, u32[]{:S(2)}) %collective-permute-start.22) | collective-permute-done | bytes 655392 | tf_op jit(solution)/shard_map/ppermute | solution.py:396
  159.6 0.8 copy-done.15
  160.5 8.0 %shard_map.100 = bf16[1024,1024]{1,0:T(8,128)(2,1)} custom-call(s32[3]{0:T(128)} %pad_add_fusion.where_ref, bf16[320,4096]{1,0:T(8,128)(2,1)} %all-gather.3.cloned.1.call-done.rows_ref.x_in.refs_0_, bf16[160,1024]{1,0:T(8,128)(2,1)} %copy-done.2, bf16[160,1024]{1,0:T(8,128)(2,1)} %copy-done.3, bf16[160,1024]{1,0:T(8,128)(2,1)} %copy-done.4, ...), custom_call_target="tpu_custom_call" | custom-call | tf_op jit(solution)/shard_map/pallas_call | solution.py:39
  (72 shorter events, 6.2 us)
Async XLA Ops:
  7.2 39.1 %all-gather.3.cloned.1.call-start = ((), (), s32[]{:S(2)}) async-start(), calls=%async_computation.2 | async-start | bytes 2949120 | tf_op jit(solution)/shard_map/all_gather | solution.py:429
  7.9 76.6 %all-gather.5.cloned.1.call-start = ((), (), s32[]{:S(2)}) async-start(), calls=%async_computation.3 | async-start | bytes 2949120 | tf_op jit(solution)/shard_map/all_gather | solution.py:429
  8.6 159.8 %reduce-scatter.3.cloned.1.call-start = ((), (), s32[]{:S(2)}) async-start(), calls=%async_computation.4 | async-start | bytes 2949120 | tf_op jit(solution)/shard_map/reduce_scatter | solution.py:432
  49.1 15.4 %collective-permute-start = (bf16[160,1024]{1,0:T(8,128)(2,1)}, bf16[160,1024]{1,0:T(8,128)(2,1)S(1)}, u32[]{:S(2)}, u32[]{:S(2)}) collective-permute-start(bf16[160,1024]{1,0:T(8,128)(2,1)} %get-tuple-element.81), channel_id=1, source_target_pairs={{0,8},{1,17},{2,10},{3,19},{4,12},{5,21},{6,14},{7,23},{8,0},{9,25... | collective-permute-start | bytes 983048 | tf_op jit(solution)/shard_map/ppermute | solution.py:411
  50.6 13.9 %collective-permute-start.1 = (bf16[160,1024]{1,0:T(8,128)(2,1)}, bf16[160,1024]{1,0:T(8,128)(2,1)S(1)}, u32[]{:S(2)}, u32[]{:S(2)}) collective-permute-start(bf16[160,1024]{1,0:T(8,128)(2,1)} %get-tuple-element.82), channel_id=1, source_target_pairs={{0,16},{1,9},{2,18},{3,11},{4,20},{5,13},{6,22},{7,15},{8,24},{9,1... | collective-permute-start | bytes 983048 | tf_op jit(solution)/shard_map/ppermute | solution.py:411
  52.1 12.4 %collective-permute-start.2 = (bf16[160,1024]{1,0:T(8,128)(2,1)}, bf16[160,1024]{1,0:T(8,128)(2,1)S(1)}, u32[]{:S(2)}, u32[]{:S(2)}) collective-permute-start(bf16[160,1024]{1,0:T(8,128)(2,1)} %get-tuple-element.83), channel_id=1, source_target_pairs={{0,8},{1,17},{2,10},{3,19},{4,12},{5,21},{6,14},{7,23},{8,0},{9,25... | collective-permute-start | bytes 983048 | tf_op jit(solution)/shard_map/ppermute | solution.py:411
  64.5 11.4 %copy-start.2 = (bf16[160,1024]{1,0:T(8,128)(2,1)}, bf16[160,1024]{1,0:T(8,128)(2,1)S(1)}, u32[]{:S(2)}) copy-start(bf16[160,1024]{1,0:T(8,128)(2,1)S(1)} %collective-permute-done.refs_1_) | copy-start | bytes 983044
  64.5 20.0 %collective-permute-start.4 = (bf16[320,1024]{1,0:T(8,128)(2,1)}, bf16[320,1024]{1,0:T(8,128)(2,1)S(1)}, u32[]{:S(2)}, u32[]{:S(2)}) collective-permute-start(bf16[320,1024]{1,0:T(8,128)(2,1)} %get-tuple-element.124.hidden_ref.refs_0_), channel_id=1, source_target_pairs={{0,16},{1,9},{2,18},{3,11},{4,20},{5,13},{6,22},{7,15},{8,24},{9,1... | collective-permute-start | bytes 1966088 | tf_op jit(solution)/shard_map/ppermute | solution.py:396
  65.1 19.4 %collective-permute-start.3 = (bf16[320,1024]{1,0:T(8,128)(2,1)}, bf16[320,1024]{1,0:T(8,128)(2,1)}, u32[]{:S(2)}, u32[]{:S(2)}) collective-permute-start(bf16[320,1024]{1,0:T(8,128)(2,1)} %get-tuple-element.124.hidden_ref.refs_0_), channel_id=1, source_target_pairs={{0,8},{1,17},{2,10},{3,19},{4,12},{5,21},{6,14},{7,23},{8,0},{9,25... | collective-permute-start | bytes 1966088 | tf_op jit(solution)/shard_map/ppermute | solution.py:396
  66.6 17.9 %collective-permute-start.5 = (bf16[160,1024]{1,0:T(8,128)(2,1)S(1)}, bf16[160,1024]{1,0:T(8,128)(2,1)S(1)}, u32[]{:S(2)}, u32[]{:S(2)}) collective-permute-start(bf16[160,1024]{1,0:T(8,128)(2,1)S(1)} %collective-permute-done.2), channel_id=1, source_target_pairs={{0,16},{1,9},{2,18},{3,11},{4,20},{5,13},{6,22},{7,15},{8,24},{9,1... | collective-permute-start | bytes 983048 | tf_op jit(solution)/shard_map/ppermute | solution.py:411
  68.1 16.4 %collective-permute-start.6 = (bf16[160,1024]{1,0:T(8,128)(2,1)S(1)}, bf16[160,1024]{1,0:T(8,128)(2,1)S(1)}, u32[]{:S(2)}, u32[]{:S(2)}) collective-permute-start(bf16[160,1024]{1,0:T(8,128)(2,1)S(1)} %collective-permute-done.refs_1_), channel_id=1, source_target_pairs={{0,1},{1,0},{2,3},{3,2},{4,5},{5,4},{6,7},{7,6},{8,9},{9,8},{10,11... | collective-permute-start | bytes 983048 | tf_op jit(solution)/shard_map/ppermute | solution.py:345
  68.1 16.4 %collective-permute-start.7 = (bf16[160,1024]{1,0:T(8,128)(2,1)S(1)}, bf16[160,1024]{1,0:T(8,128)(2,1)S(1)}, u32[]{:S(2)}, u32[]{:S(2)}) collective-permute-start(bf16[160,1024]{1,0:T(8,128)(2,1)S(1)} %collective-permute-done.1.refs_2_), channel_id=1, source_target_pairs={{0,1},{1,0},{2,3},{3,2},{4,5},{5,4},{6,7},{7,6},{8,9},{9,8},{10,11... | collective-permute-start | bytes 983048 | tf_op jit(solution)/shard_map/ppermute | solution.py:345
  84.5 41.0 %copy-start.4 = (bf16[160,1024]{1,0:T(8,128)(2,1)}, bf16[160,1024]{1,0:T(8,128)(2,1)S(1)}, u32[]{:S(2)}) copy-start(bf16[160,1024]{1,0:T(8,128)(2,1)S(1)} %collective-permute-done.5.refs_3_) | copy-start | bytes 983044
  84.6 83.9 %reduce-scatter.5.cloned.1.call-start = ((), (), s32[]{:S(2)}) async-start(), calls=%async_computation.5 | async-start | bytes 2949120 | tf_op jit(solution)/shard_map/reduce_scatter | solution.py:432
  87.5 12.2 %collective-permute-start.8 = (bf16[160,1024]{1,0:T(8,128)(2,1)}, bf16[160,1024]{1,0:T(8,128)(2,1)S(1)}, u32[]{:S(2)}, u32[]{:S(2)}) collective-permute-start(bf16[160,1024]{1,0:T(8,128)(2,1)} %get-tuple-element.103), channel_id=1, source_target_pairs={{0,8},{1,17},{2,10},{3,19},{4,12},{5,21},{6,14},{7,23},{8,0},{9,25... | collective-permute-start | bytes 983048 | tf_op jit(solution)/shard_map/ppermute | solution.py:411
  89.2 11.0 %collective-permute-start.9 = (bf16[160,1024]{1,0:T(8,128)(2,1)}, bf16[160,1024]{1,0:T(8,128)(2,1)}, u32[]{:S(2)}, u32[]{:S(2)}) collective-permute-start(bf16[160,1024]{1,0:T(8,128)(2,1)} %get-tuple-element.104), channel_id=1, source_target_pairs={{0,16},{1,9},{2,18},{3,11},{4,20},{5,13},{6,22},{7,15},{8,24},{9,1... | collective-permute-start | bytes 983048 | tf_op jit(solution)/shard_map/ppermute | solution.py:411
  90.6 11.3 %collective-permute-start.10 = (bf16[160,1024]{1,0:T(8,128)(2,1)}, bf16[160,1024]{1,0:T(8,128)(2,1)}, u32[]{:S(2)}, u32[]{:S(2)}) collective-permute-start(bf16[160,1024]{1,0:T(8,128)(2,1)} %get-tuple-element.105), channel_id=1, source_target_pairs={{0,8},{1,17},{2,10},{3,19},{4,12},{5,21},{6,14},{7,23},{8,0},{9,25... | collective-permute-start | bytes 983048 | tf_op jit(solution)/shard_map/ppermute | solution.py:411
  99.7 16.3 %copy-start.16 = (bf16[160,1024]{1,0:T(8,128)(2,1)}, bf16[160,1024]{1,0:T(8,128)(2,1)S(1)}, u32[]{:S(2)}) copy-start(bf16[160,1024]{1,0:T(8,128)(2,1)S(1)} %collective-permute-done.8.refs_5_) | copy-start | bytes 983044
  101.9 19.7 %collective-permute-start.12 = (bf16[320,1024]{1,0:T(8,128)(2,1)}, bf16[320,1024]{1,0:T(8,128)(2,1)S(1)}, u32[]{:S(2)}, u32[]{:S(2)}) collective-permute-start(bf16[320,1024]{1,0:T(8,128)(2,1)} %collective-permute-done.3.refs_1_), channel_id=1, source_target_pairs={{0,16},{1,9},{2,18},{3,11},{4,20},{5,13},{6,22},{7,15},{8,24},{9,1... | collective-permute-start | bytes 1966088 | tf_op jit(solution)/shard_map/ppermute | solution.py:396
  102.7 19.0 %collective-permute-start.11 = (bf16[320,1024]{1,0:T(8,128)(2,1)}, bf16[320,1024]{1,0:T(8,128)(2,1)S(1)}, u32[]{:S(2)}, u32[]{:S(2)}) collective-permute-start(bf16[320,1024]{1,0:T(8,128)(2,1)} %get-tuple-element.111.dgate_ref.refs_7_), channel_id=1, source_target_pairs={{0,8},{1,17},{2,10},{3,19},{4,12},{5,21},{6,14},{7,23},{8,0},{9,25... | collective-permute-start | bytes 1966088 | tf_op jit(solution)/shard_map/ppermute | solution.py:396
  103.1 18.6 %collective-permute-start.13 = (bf16[160,1024]{1,0:T(8,128)(2,1)}, bf16[160,1024]{1,0:T(8,128)(2,1)}, u32[]{:S(2)}, u32[]{:S(2)}) collective-permute-start(bf16[160,1024]{1,0:T(8,128)(2,1)} %collective-permute-done.10), channel_id=1, source_target_pairs={{0,16},{1,9},{2,18},{3,11},{4,20},{5,13},{6,22},{7,15},{8,24},{9,1... | collective-permute-start | bytes 983048 | tf_op jit(solution)/shard_map/ppermute | solution.py:411
  104.6 17.1 %collective-permute-start.14 = (bf16[160,1024]{1,0:T(8,128)(2,1)S(1)}, bf16[160,1024]{1,0:T(8,128)(2,1)}, u32[]{:S(2)}, u32[]{:S(2)}) collective-permute-start(bf16[160,1024]{1,0:T(8,128)(2,1)S(1)} %collective-permute-done.8.refs_5_), channel_id=1, source_target_pairs={{0,1},{1,0},{2,3},{3,2},{4,5},{5,4},{6,7},{7,6},{8,9},{9,8},{10,11... | collective-permute-start | bytes 983048 | tf_op jit(solution)/shard_map/ppermute | solution.py:345
  104.6 17.1 %collective-permute-start.15 = (bf16[160,1024]{1,0:T(8,128)(2,1)}, bf16[160,1024]{1,0:T(8,128)(2,1)}, u32[]{:S(2)}, u32[]{:S(2)}) collective-permute-start(bf16[160,1024]{1,0:T(8,128)(2,1)} %collective-permute-done.9.refs_6_), channel_id=1, source_target_pairs={{0,1},{1,0},{2,3},{3,2},{4,5},{5,4},{6,7},{7,6},{8,9},{9,8},{10,11... | collective-permute-start | bytes 983048 | tf_op jit(solution)/shard_map/ppermute | solution.py:345
  121.7 14.9 %copy-start.9 = (bf16[320,1024]{1,0:T(8,128)(2,1)}, bf16[320,1024]{1,0:T(8,128)(2,1)S(1)}, u32[]{:S(2)}) copy-start(bf16[320,1024]{1,0:T(8,128)(2,1)S(1)} %collective-permute-done.11.refs_8_) | copy-start | bytes 1966084
  121.7 16.8 %collective-permute-start.17 = (bf16[320,1024]{1,0:T(8,128)(2,1)S(1)}, bf16[320,1024]{1,0:T(8,128)(2,1)S(1)}, u32[]{:S(2)}, u32[]{:S(2)}) collective-permute-start(bf16[320,1024]{1,0:T(8,128)(2,1)S(1)} %copy-done.1), channel_id=1, source_target_pairs={{0,16},{1,9},{2,18},{3,11},{4,20},{5,13},{6,22},{7,15},{8,24},{9,1... | collective-permute-start | bytes 1966088 | tf_op jit(solution)/shard_map/ppermute | solution.py:396
  123.3 17.7 %collective-permute-start.19 = (bf16[320,1024]{1,0:T(8,128)(2,1)S(1)}, bf16[320,1024]{1,0:T(8,128)(2,1)S(1)}, u32[]{:S(2)}, u32[]{:S(2)}) collective-permute-start(bf16[320,1024]{1,0:T(8,128)(2,1)S(1)} %copy-done), channel_id=1, source_target_pairs={{0,8},{1,17},{2,10},{3,19},{4,12},{5,21},{6,14},{7,23},{8,0},{9,25... | collective-permute-start | bytes 1966088 | tf_op jit(solution)/shard_map/ppermute | solution.py:396
  124.7 20.9 %collective-permute-start.18 = (bf16[320,1024]{1,0:T(8,128)(2,1)S(1)}, bf16[320,1024]{1,0:T(8,128)(2,1)S(1)}, u32[]{:S(2)}, u32[]{:S(2)}) collective-permute-start(bf16[320,1024]{1,0:T(8,128)(2,1)S(1)} %collective-permute-done.11.refs_8_), channel_id=1, source_target_pairs={{0,16},{1,9},{2,18},{3,11},{4,20},{5,13},{6,22},{7,15},{8,24},{9,1... | collective-permute-start | bytes 1966088 | tf_op jit(solution)/shard_map/ppermute | solution.py:396
  125.5 1.8 %collective-permute-start.21 = (bf16[160,1024]{1,0:T(8,128)(2,1)}, bf16[160,1024]{1,0:T(8,128)(2,1)S(1)}, u32[]{:S(2)}, u32[]{:S(2)}) collective-permute-start(bf16[160,1024]{1,0:T(8,128)(2,1)} %collective-permute-done.13.refs_7_), channel_id=1, source_target_pairs={{0,1},{1,0},{2,3},{3,2},{4,5},{5,4},{6,7},{7,6},{8,9},{9,8},{10,11... | collective-permute-start | bytes 983048 | tf_op jit(solution)/shard_map/ppermute | solution.py:345
  125.5 3.1 %collective-permute-start.20 = (bf16[160,1024]{1,0:T(8,128)(2,1)S(1)}, bf16[160,1024]{1,0:T(8,128)(2,1)S(1)}, u32[]{:S(2)}, u32[]{:S(2)}) collective-permute-start(bf16[160,1024]{1,0:T(8,128)(2,1)S(1)} %collective-permute-done.5.refs_3_), channel_id=1, source_target_pairs={{0,1},{1,0},{2,3},{3,2},{4,5},{5,4},{6,7},{7,6},{8,9},{9,8},{10,11... | collective-permute-start | bytes 983048 | tf_op jit(solution)/shard_map/ppermute | solution.py:345
  127.3 27.7 %collective-permute-start.16 = (bf16[320,1024]{1,0:T(8,128)(2,1)S(1)}, bf16[320,1024]{1,0:T(8,128)(2,1)S(1)}, u32[]{:S(2)}, u32[]{:S(2)}) collective-permute-start(bf16[320,1024]{1,0:T(8,128)(2,1)S(1)} %copy-done), channel_id=1, source_target_pairs={{0,16},{1,9},{2,18},{3,11},{4,20},{5,13},{6,22},{7,15},{8,24},{9,1... | collective-permute-start | bytes 1966088 | tf_op jit(solution)/shard_map/ppermute | solution.py:396
  141.0 14.1 %copy-start.11 = (bf16[320,1024]{1,0:T(8,128)(2,1)}, bf16[320,1024]{1,0:T(8,128)(2,1)S(1)}, u32[]{:S(2)}) copy-start(bf16[320,1024]{1,0:T(8,128)(2,1)S(1)} %collective-permute-done.19.refs_8_) | copy-start | bytes 1966084
  145.6 14.0 %collective-permute-start.22 = (bf16[320,1024]{1,0:T(8,128)(2,1)S(1)}, bf16[320,1024]{1,0:T(8,128)(2,1)S(1)}, u32[]{:S(2)}, u32[]{:S(2)}) collective-permute-start(bf16[320,1024]{1,0:T(8,128)(2,1)S(1)} %collective-permute-done.19.refs_8_), channel_id=1, source_target_pairs={{0,16},{1,9},{2,18},{3,11},{4,20},{5,13},{6,22},{7,15},{8,24},{9,1... | collective-permute-start | bytes 1966088 | tf_op jit(solution)/shard_map/ppermute | solution.py:396
  (13 other events, 61.6 us)
Sparse Core Ops, SparseCore 0:
  9.6 36.5 all-gather.2
  47.9 32.8 all-gather.4
  84.7 36.3 reduce-scatter.2
  123.8 36.6 reduce-scatter.4

commit v6 on v4

--- a/solution.py
+++ b/solution.py
@@ -452,13 +452,12 @@
         [across], *forward(after(gathered, blocks), w_gate, w_up)
     )
 
-    hiddens = over_groups(hidden, all_hidden, [1], range(2, last), [last])
+    hiddens = over_groups(hidden, all_hidden, range(1, last), [last])
     hiddens.advance()
     for _ in range(phases - 1):
         across.advance()
     (partial,) = fence([hiddens, across], project(hidden, w_down))
 
-    hiddens.advance()
     upstream, partial = fence([across], upstream, partial)
     mixed = over_line(partial)
 
@@ -466,8 +465,10 @@
     all_dgate, all_dup, mine_up, theirs_up = [], [], {}, {}
     across_up = exchange(blocks, mine_up, theirs_up)
     across_up.advance()
+    hiddens.advance()
     dgate, dup = backward(after(upstream, blocks), w_down, swish, slope)
     dgate, dup = fence([hiddens, across, across_up], dgate, dup)
+    hiddens.advance()
 
     gates = over_groups(dgate, all_dgate, [1], range(2, groups))
     ups = over_groups(dup, all_dup, [1], range(2, groups))
@@ -481,12 +482,11 @@
     )
     input_grad = over_line(partial)
 
-    hiddens.advance()
     gates.advance()
     ups.advance()
     across.advance()
     across_up.advance()
-    (mark,) = fence([hiddens, across, across_up], partial)
+    (mark,) = fence([across, across_up], partial)
     across.advance()
     across_up.advance()
 

time: 178 us -> 174 us (0.978)
  waiting for transfers between devices: 71.7 us -> 68.2 us
    ppermute x9, waiting for transfers between devices: 21.5 us -> 13.8 us  [gather_groups(): held.append(lax.ppermute(held[label - (1 << top)], ('dp', 'mp'), pairs))]
    ppermute x8, waiting for transfers between devices: 7.61 us -> 14.2 us  [exchange_groups(): lax.ppermute(mine[at], ('dp', 'mp'), left[at].pop(0))]
    all_gather x2, waiting for transfers between devices: 39.3 us -> 37 us  [from_line(): return lax.all_gather(value, 'mp', axis=0, tiled=True)]
  transfers between devices with their start and end apart: 27 -> 27, of which waited for: 10 -> 7; matrix products, arithmetic and copies ran while one was open for 0% -> 0% of each run, Pallas kernels for 38% -> 39%
where the time goes in v6:
time: 174 us
  waiting for transfers between devices  68.2 us (39%)
  Pallas kernels  68.2 us (39%)
  starting transfers between devices  20.3 us (12%)
  between operations  14.2 us (8%)
  local copies, waits for them, and re-layouts  2.49 us (1%)
    pallas_call x9, Pallas kernels, call(): pl.pallas_call(body, grid=(steps,), in_specs=in_specs, out_specs=out_spec...  68.2 us
    all_gather x2, waiting for transfers between devices, from_line(): return lax.all_gather(value, 'mp', axis=0, tiled=True)  37 us
    ppermute x8, waiting for transfers between devices, exchange_groups(): lax.ppermute(mine[at], ('dp', 'mp'), left[at].pop(0))  14.2 us
    ppermute x9, waiting for transfers between devices, gather_groups(): held.append(lax.ppermute(held[label - (1 << top)], ('dp', 'mp'), pairs))  13.8 us
    ppermute x9, starting transfers between devices, gather_groups(): held.append(lax.ppermute(held[label - (1 << top)], ('dp', 'mp'), pairs))  9.84 us
    ppermute x8, starting transfers between devices, exchange_groups(): lax.ppermute(mine[at], ('dp', 'mp'), left[at].pop(0))  9.21 us
  transfers between devices with their start and end apart: 27, of which 7 were waited for; matrix products, arithmetic and copies ran while one was open for 0% of the time, Pallas kernels for 39%

profile of v6, /device:TPU:0, one launch (start us, length us, event | category | flops | bytes accessed | tf_op | source)
XLA Modules:
  0.0 174.0 jit_solution(10367820353561871457)
XLA Ops:
  7.2 0.7 all-gather.3.cloned.1.call-update
  7.9 0.7 all-gather.5.cloned.1.call-update
  9.3 37.0 %all-gather.3.cloned.1.call-done.rows_ref.x_in.refs_0_ = bf16[320,4096]{1,0:T(8,128)(2,1)} async-done(((bf16[40,4096]{1,0:T(8,128)(2,1)}), bf16[320,4096]{1,0:T(8,128)(2,1)}) %all-gather.3.cloned.1.call-update) | async-done | bytes 2621456 | tf_op jit(solution)/shard_map/all_gather | solution.py:429
  46.3 2.8 %shard_map.92 = (bf16[160,1024]{1,0:T(8,128)(2,1)}, bf16[160,1024]{1,0:T(8,128)(2,1)}, bf16[160,1024]{1,0:T(8,128)(2,1)}) custom-call(s32[3]{0:T(128)} %pad_add_fusion.where_ref, bf16[320,4096]{1,0:T(8,128)(2,1)} %all-gather.3.cloned.1.call-done.rows_ref.x_in.refs_0_), custom_call_target="tpu_custom_call" | custom-call | tf_op jit(solution)/shard_map/pallas_call | solution.py:39
  49.1 1.5 collective-permute-start
  50.6 1.5 collective-permute-start.1
  52.6 11.8 %shard_map.93 = (bf16[320,1024]{1,0:T(8,128)(2,1)}, f32[320,1024]{1,0:T(8,128)}, f32[320,1024]{1,0:T(8,128)}) custom-call(bf16[320,4096]{1,0:T(8,128)(2,1)} %all-gather.3.cloned.1.call-done.rows_ref.x_in.refs_0_, bf16[4096,1024]{1,0:T(8,128)(2,1)} %w_gate_ref.3, bf16[4096,1024]{1,0:T(8,128)(2,1)} %w_up_ref.3), custom_call_target="tpu_custom_call" | custom-call | tf_op jit(solution)/shard_map/pallas_call | solution.py:39
  64.5 0.6 collective-permute-start.4
  65.1 1.5 collective-permute-start.3
  66.6 1.5 collective-permute-start.5
  68.6 7.2 %shard_map.94 = bf16[320,4096]{1,0:T(8,128)(2,1)} custom-call(bf16[320,1024]{1,0:T(8,128)(2,1)} %get-tuple-element.126.hidden_ref.refs_0_, bf16[1024,4096]{1,0:T(8,128)(2,1)} %w_ref.3), custom_call_target="tpu_custom_call" | custom-call | tf_op jit(solution)/shard_map/pallas_call | solution.py:39
  75.8 8.6 %collective-permute-done.5.refs_3_ = bf16[160,1024]{1,0:T(8,128)(2,1)S(1)} collective-permute-done((bf16[160,1024]{1,0:T(8,128)(2,1)S(1)}, bf16[160,1024]{1,0:T(8,128)(2,1)S(1)}, u32[]{:S(2)}, u32[]{:S(2)}) %collective-permute-start.5) | collective-permute-done | bytes 327712 | tf_op jit(solution)/shard_map/ppermute | solution.py:411
  84.6 1.5 collective-permute-start.8
  86.2 2.8 %shard_map.95 = (bf16[160,1024]{1,0:T(8,128)(2,1)}, bf16[160,1024]{1,0:T(8,128)(2,1)}, bf16[160,1024]{1,0:T(8,128)(2,1)}) custom-call(s32[3]{0:T(128)} %pad_add_fusion.where_ref, bf16[320,4096]{1,0:T(8,128)(2,1)} %all-gather.5.cloned.1.call-done.rows_ref.x_in.refs_4_), custom_call_target="tpu_custom_call" | custom-call | tf_op jit(solution)/shard_map/pallas_call | solution.py:39
  89.0 1.7 collective-permute-start.9
  91.7 8.7 %shard_map.96 = (bf16[320,1024]{1,0:T(8,128)(2,1)}, bf16[320,1024]{1,0:T(8,128)(2,1)}) custom-call(bf16[320,4096]{1,0:T(8,128)(2,1)} %all-gather.5.cloned.1.call-done.rows_ref.x_in.refs_4_, bf16[1024,4096]{1,0:T(8,128)(2,1)} %w_ref.3, f32[320,1024]{1,0:T(8,128)} %get-tuple-element.104.swish_ref, f32[320,1024]{1,0:T(8,128)} %get-tuple-element.105.slope_ref), custom_call_target="tpu_custom_call" | custom-call | tf_op jit(solution)/shard_map/pallas_call | solution.py:39
  100.4 5.5 %collective-permute-done.10.refs_6_ = bf16[160,1024]{1,0:T(8,128)(2,1)} collective-permute-done((bf16[160,1024]{1,0:T(8,128)(2,1)}, bf16[160,1024]{1,0:T(8,128)(2,1)}, u32[]{:S(2)}, u32[]{:S(2)}) %collective-permute-start.10) | collective-permute-done | bytes 327712 | tf_op jit(solution)/shard_map/ppermute | solution.py:411
  105.9 1.7 collective-permute-start.12
  108.0 1.5 collective-permute-start.14
  110.0 11.0 %shard_map.97 = bf16[320,4096]{1,0:T(8,128)(2,1)} custom-call(bf16[320,1024]{1,0:T(8,128)(2,1)} %get-tuple-element.108.dgate_ref.refs_7_, bf16[320,1024]{1,0:T(8,128)(2,1)} %get-tuple-element.109.dup_ref.refs_7_, bf16[4096,1024]{1,0:T(8,128)(2,1)} %w_gate_ref.3, bf16[4096,1024]{1,0:T(8,128)(2,1)} %w_up_ref.3), custom_call_target="tpu_custom_call" | custom-call | tf_op jit(solution)/shard_map/pallas_call | solution.py:39
  121.0 5.6 %collective-permute-done.13.refs_8_ = bf16[320,1024]{1,0:T(8,128)(2,1)S(1)} collective-permute-done((bf16[320,1024]{1,0:T(8,128)(2,1)}, bf16[320,1024]{1,0:T(8,128)(2,1)S(1)}, u32[]{:S(2)}, u32[]{:S(2)}) %collective-permute-start.13) | collective-permute-done | bytes 655392 | tf_op jit(solution)/shard_map/ppermute | solution.py:396
  126.8 1.5 collective-permute-start.21
  128.9 1.4 collective-permute-start.17
  131.0 1.8 %collective-permute-done.20.refs_10_ = bf16[160,1024]{1,0:T(8,128)(2,1)S(1)} collective-permute-done((bf16[160,1024]{1,0:T(8,128)(2,1)}, bf16[160,1024]{1,0:T(8,128)(2,1)S(1)}, u32[]{:S(2)}, u32[]{:S(2)}) %collective-permute-start.20) | collective-permute-done | bytes 327712 | tf_op jit(solution)/shard_map/ppermute | solution.py:345
  132.8 0.7 copy-done.17
  133.6 7.9 %shard_map.98 = bf16[1024,1024]{1,0:T(8,128)(2,1)} custom-call(s32[3]{0:T(128)} %pad_add_fusion.where_ref, bf16[320,1024]{1,0:T(8,128)(2,1)} %get-tuple-element.126.hidden_ref.refs_0_, bf16[320,1024]{1,0:T(8,128)(2,1)} %copy-done.9, bf16[320,1024]{1,0:T(8,128)(2,1)} %copy-done.8, bf16[320,1024]{1,0:T(8,128)(2,1)} %copy-done.10, ...), custom_call_target="tpu_custom_call" | custom-call | tf_op jit(solution)/shard_map/pallas_call | solution.py:39
  141.5 2.9 %collective-permute-done.22.refs_10_ = bf16[320,1024]{1,0:T(8,128)(2,1)S(1)} collective-permute-done((bf16[320,1024]{1,0:T(8,128)(2,1)}, bf16[320,1024]{1,0:T(8,128)(2,1)S(1)}, u32[]{:S(2)}, u32[]{:S(2)}) %collective-permute-start.22) | collective-permute-done | bytes 655392 | tf_op jit(solution)/shard_map/ppermute | solution.py:396
  144.5 0.8 copy-done.15
  145.3 8.0 %shard_map.99 = bf16[1024,1024]{1,0:T(8,128)(2,1)} custom-call(s32[3]{0:T(128)} %pad_add_fusion.where_ref, bf16[320,4096]{1,0:T(8,128)(2,1)} %all-gather.3.cloned.1.call-done.rows_ref.x_in.refs_0_, bf16[160,1024]{1,0:T(8,128)(2,1)} %copy-done.2, bf16[160,1024]{1,0:T(8,128)(2,1)} %copy-done.3, bf16[160,1024]{1,0:T(8,128)(2,1)} %copy-done.4, ...), custom_call_target="tpu_custom_call" | custom-call | tf_op jit(solution)/shard_map/pallas_call | solution.py:39
  153.4 5.2 %collective-permute-done.18.refs_10_ = bf16[320,1024]{1,0:T(8,128)(2,1)S(1)} collective-permute-done((bf16[320,1024]{1,0:T(8,128)(2,1)S(1)}, bf16[320,1024]{1,0:T(8,128)(2,1)S(1)}, u32[]{:S(2)}, u32[]{:S(2)}) %collective-permute-start.18) | collective-permute-done | bytes 655392 | tf_op jit(solution)/shard_map/ppermute | solution.py:396
  158.5 0.8 copy-done.13
  159.4 8.0 %shard_map.100 = bf16[1024,1024]{1,0:T(8,128)(2,1)} custom-call(s32[3]{0:T(128)} %pad_add_fusion.where_ref, bf16[320,4096]{1,0:T(8,128)(2,1)} %all-gather.3.cloned.1.call-done.rows_ref.x_in.refs_0_, bf16[160,1024]{1,0:T(8,128)(2,1)} %copy-done.2, bf16[160,1024]{1,0:T(8,128)(2,1)} %copy-done.3, bf16[160,1024]{1,0:T(8,128)(2,1)} %copy-done.4, ...), custom_call_target="tpu_custom_call" | custom-call | tf_op jit(solution)/shard_map/pallas_call | solution.py:39
  (72 shorter events, 5.1 us)
Async XLA Ops:
  7.2 39.1 %all-gather.3.cloned.1.call-start = ((), (), s32[]{:S(2)}) async-start(), calls=%async_computation.2 | async-start | bytes 2949120 | tf_op jit(solution)/shard_map/all_gather | solution.py:429
  7.9 76.6 %all-gather.5.cloned.1.call-start = ((), (), s32[]{:S(2)}) async-start(), calls=%async_computation.3 | async-start | bytes 2949120 | tf_op jit(solution)/shard_map/all_gather | solution.py:429
  8.6 158.7 %reduce-scatter.3.cloned.1.call-start = ((), (), s32[]{:S(2)}) async-start(), calls=%async_computation.4 | async-start | bytes 2949120 | tf_op jit(solution)/shard_map/reduce_scatter | solution.py:432
  49.1 15.4 %collective-permute-start = (bf16[160,1024]{1,0:T(8,128)(2,1)}, bf16[160,1024]{1,0:T(8,128)(2,1)S(1)}, u32[]{:S(2)}, u32[]{:S(2)}) collective-permute-start(bf16[160,1024]{1,0:T(8,128)(2,1)} %get-tuple-element.79), channel_id=1, source_target_pairs={{0,8},{1,17},{2,10},{3,19},{4,12},{5,21},{6,14},{7,23},{8,0},{9,25... | collective-permute-start | bytes 983048 | tf_op jit(solution)/shard_map/ppermute | solution.py:411
  50.6 13.9 %collective-permute-start.1 = (bf16[160,1024]{1,0:T(8,128)(2,1)}, bf16[160,1024]{1,0:T(8,128)(2,1)S(1)}, u32[]{:S(2)}, u32[]{:S(2)}) collective-permute-start(bf16[160,1024]{1,0:T(8,128)(2,1)} %get-tuple-element.80), channel_id=1, source_target_pairs={{0,16},{1,9},{2,18},{3,11},{4,20},{5,13},{6,22},{7,15},{8,24},{9,1... | collective-permute-start | bytes 983048 | tf_op jit(solution)/shard_map/ppermute | solution.py:411
  52.1 12.4 %collective-permute-start.2 = (bf16[160,1024]{1,0:T(8,128)(2,1)}, bf16[160,1024]{1,0:T(8,128)(2,1)S(1)}, u32[]{:S(2)}, u32[]{:S(2)}) collective-permute-start(bf16[160,1024]{1,0:T(8,128)(2,1)} %get-tuple-element.81), channel_id=1, source_target_pairs={{0,8},{1,17},{2,10},{3,19},{4,12},{5,21},{6,14},{7,23},{8,0},{9,25... | collective-permute-start | bytes 983048 | tf_op jit(solution)/shard_map/ppermute | solution.py:411
  64.5 11.4 %copy-start.2 = (bf16[160,1024]{1,0:T(8,128)(2,1)}, bf16[160,1024]{1,0:T(8,128)(2,1)S(1)}, u32[]{:S(2)}) copy-start(bf16[160,1024]{1,0:T(8,128)(2,1)S(1)} %collective-permute-done.refs_1_) | copy-start | bytes 983044
  64.5 20.0 %collective-permute-start.4 = (bf16[320,1024]{1,0:T(8,128)(2,1)}, bf16[320,1024]{1,0:T(8,128)(2,1)S(1)}, u32[]{:S(2)}, u32[]{:S(2)}) collective-permute-start(bf16[320,1024]{1,0:T(8,128)(2,1)} %get-tuple-element.126.hidden_ref.refs_0_), channel_id=1, source_target_pairs={{0,16},{1,9},{2,18},{3,11},{4,20},{5,13},{6,22},{7,15},{8,24},{9,1... | collective-permute-start | bytes 1966088 | tf_op jit(solution)/shard_map/ppermute | solution.py:396
  65.1 19.4 %collective-permute-start.3 = (bf16[320,1024]{1,0:T(8,128)(2,1)}, bf16[320,1024]{1,0:T(8,128)(2,1)S(1)}, u32[]{:S(2)}, u32[]{:S(2)}) collective-permute-start(bf16[320,1024]{1,0:T(8,128)(2,1)} %get-tuple-element.126.hidden_ref.refs_0_), channel_id=1, source_target_pairs={{0,8},{1,17},{2,10},{3,19},{4,12},{5,21},{6,14},{7,23},{8,0},{9,25... | collective-permute-start | bytes 1966088 | tf_op jit(solution)/shard_map/ppermute | solution.py:396
  66.6 17.9 %collective-permute-start.5 = (bf16[160,1024]{1,0:T(8,128)(2,1)S(1)}, bf16[160,1024]{1,0:T(8,128)(2,1)S(1)}, u32[]{:S(2)}, u32[]{:S(2)}) collective-permute-start(bf16[160,1024]{1,0:T(8,128)(2,1)S(1)} %collective-permute-done.2), channel_id=1, source_target_pairs={{0,16},{1,9},{2,18},{3,11},{4,20},{5,13},{6,22},{7,15},{8,24},{9,1... | collective-permute-start | bytes 983048 | tf_op jit(solution)/shard_map/ppermute | solution.py:411
  68.1 16.4 %collective-permute-start.6 = (bf16[160,1024]{1,0:T(8,128)(2,1)S(1)}, bf16[160,1024]{1,0:T(8,128)(2,1)S(1)}, u32[]{:S(2)}, u32[]{:S(2)}) collective-permute-start(bf16[160,1024]{1,0:T(8,128)(2,1)S(1)} %collective-permute-done.refs_1_), channel_id=1, source_target_pairs={{0,1},{1,0},{2,3},{3,2},{4,5},{5,4},{6,7},{7,6},{8,9},{9,8},{10,11... | collective-permute-start | bytes 983048 | tf_op jit(solution)/shard_map/ppermute | solution.py:345
  68.1 16.4 %collective-permute-start.7 = (bf16[160,1024]{1,0:T(8,128)(2,1)S(1)}, bf16[160,1024]{1,0:T(8,128)(2,1)S(1)}, u32[]{:S(2)}, u32[]{:S(2)}) collective-permute-start(bf16[160,1024]{1,0:T(8,128)(2,1)S(1)} %collective-permute-done.1.refs_2_), channel_id=1, source_target_pairs={{0,1},{1,0},{2,3},{3,2},{4,5},{5,4},{6,7},{7,6},{8,9},{9,8},{10,11... | collective-permute-start | bytes 983048 | tf_op jit(solution)/shard_map/ppermute | solution.py:345
  84.5 42.3 %copy-start.4 = (bf16[160,1024]{1,0:T(8,128)(2,1)}, bf16[160,1024]{1,0:T(8,128)(2,1)S(1)}, u32[]{:S(2)}) copy-start(bf16[160,1024]{1,0:T(8,128)(2,1)S(1)} %collective-permute-done.5.refs_3_) | copy-start | bytes 983044
  84.6 82.8 %reduce-scatter.5.cloned.1.call-start = ((), (), s32[]{:S(2)}) async-start(), calls=%async_computation.5 | async-start | bytes 2949120 | tf_op jit(solution)/shard_map/reduce_scatter | solution.py:432
  84.6 21.3 %collective-permute-start.8 = (bf16[320,1024]{1,0:T(8,128)(2,1)S(1)}, bf16[320,1024]{1,0:T(8,128)(2,1)S(1)}, u32[]{:S(2)}, u32[]{:S(2)}) collective-permute-start(bf16[320,1024]{1,0:T(8,128)(2,1)S(1)} %collective-permute-done.3.refs_1_), channel_id=1, source_target_pairs={{0,16},{1,9},{2,18},{3,11},{4,20},{5,13},{6,22},{7,15},{8,24},{9,1... | collective-permute-start | bytes 1966088 | tf_op jit(solution)/shard_map/ppermute | solution.py:396
  89.0 11.3 %collective-permute-start.9 = (bf16[160,1024]{1,0:T(8,128)(2,1)}, bf16[160,1024]{1,0:T(8,128)(2,1)S(1)}, u32[]{:S(2)}, u32[]{:S(2)}) collective-permute-start(bf16[160,1024]{1,0:T(8,128)(2,1)} %get-tuple-element.100), channel_id=1, source_target_pairs={{0,8},{1,17},{2,10},{3,19},{4,12},{5,21},{6,14},{7,23},{8,0},{9,25... | collective-permute-start | bytes 983048 | tf_op jit(solution)/shard_map/ppermute | solution.py:411
  90.7 15.2 %collective-permute-start.10 = (bf16[160,1024]{1,0:T(8,128)(2,1)}, bf16[160,1024]{1,0:T(8,128)(2,1)}, u32[]{:S(2)}, u32[]{:S(2)}) collective-permute-start(bf16[160,1024]{1,0:T(8,128)(2,1)} %get-tuple-element.101), channel_id=1, source_target_pairs={{0,16},{1,9},{2,18},{3,11},{4,20},{5,13},{6,22},{7,15},{8,24},{9,1... | collective-permute-start | bytes 983048 | tf_op jit(solution)/shard_map/ppermute | solution.py:411
  91.3 14.6 %collective-permute-start.11 = (bf16[160,1024]{1,0:T(8,128)(2,1)}, bf16[160,1024]{1,0:T(8,128)(2,1)}, u32[]{:S(2)}, u32[]{:S(2)}) collective-permute-start(bf16[160,1024]{1,0:T(8,128)(2,1)} %get-tuple-element.102), channel_id=1, source_target_pairs={{0,8},{1,17},{2,10},{3,19},{4,12},{5,21},{6,14},{7,23},{8,0},{9,25... | collective-permute-start | bytes 983048 | tf_op jit(solution)/shard_map/ppermute | solution.py:411
  100.4 20.6 %copy-start.16 = (bf16[160,1024]{1,0:T(8,128)(2,1)}, bf16[160,1024]{1,0:T(8,128)(2,1)S(1)}, u32[]{:S(2)}) copy-start(bf16[160,1024]{1,0:T(8,128)(2,1)S(1)} %collective-permute-done.9.refs_5_) | copy-start | bytes 983044
  105.9 15.1 %copy-start.10 = (bf16[320,1024]{1,0:T(8,128)(2,1)}, bf16[320,1024]{1,0:T(8,128)(2,1)S(1)}, u32[]{:S(2)}) copy-start(bf16[320,1024]{1,0:T(8,128)(2,1)S(1)} %collective-permute-done.8.refs_3_) | copy-start | bytes 1966084
  105.9 15.1 %collective-permute-start.12 = (bf16[320,1024]{1,0:T(8,128)(2,1)}, bf16[320,1024]{1,0:T(8,128)(2,1)}, u32[]{:S(2)}, u32[]{:S(2)}) collective-permute-start(bf16[320,1024]{1,0:T(8,128)(2,1)} %get-tuple-element.108.dgate_ref.refs_7_), channel_id=1, source_target_pairs={{0,8},{1,17},{2,10},{3,19},{4,12},{5,21},{6,14},{7,23},{8,0},{9,25... | collective-permute-start | bytes 1966088 | tf_op jit(solution)/shard_map/ppermute | solution.py:396
  107.6 19.1 %collective-permute-start.13 = (bf16[320,1024]{1,0:T(8,128)(2,1)}, bf16[320,1024]{1,0:T(8,128)(2,1)S(1)}, u32[]{:S(2)}, u32[]{:S(2)}) collective-permute-start(bf16[320,1024]{1,0:T(8,128)(2,1)} %get-tuple-element.109.dup_ref.refs_7_), channel_id=1, source_target_pairs={{0,8},{1,17},{2,10},{3,19},{4,12},{5,21},{6,14},{7,23},{8,0},{9,25... | collective-permute-start | bytes 1966088 | tf_op jit(solution)/shard_map/ppermute | solution.py:396
  108.0 13.0 %collective-permute-start.14 = (bf16[160,1024]{1,0:T(8,128)(2,1)}, bf16[160,1024]{1,0:T(8,128)(2,1)}, u32[]{:S(2)}, u32[]{:S(2)}) collective-permute-start(bf16[160,1024]{1,0:T(8,128)(2,1)} %collective-permute-done.11), channel_id=1, source_target_pairs={{0,16},{1,9},{2,18},{3,11},{4,20},{5,13},{6,22},{7,15},{8,24},{9,1... | collective-permute-start | bytes 983048 | tf_op jit(solution)/shard_map/ppermute | solution.py:411
  109.5 11.5 %collective-permute-start.15 = (bf16[160,1024]{1,0:T(8,128)(2,1)S(1)}, bf16[160,1024]{1,0:T(8,128)(2,1)}, u32[]{:S(2)}, u32[]{:S(2)}) collective-permute-start(bf16[160,1024]{1,0:T(8,128)(2,1)S(1)} %collective-permute-done.9.refs_5_), channel_id=1, source_target_pairs={{0,1},{1,0},{2,3},{3,2},{4,5},{5,4},{6,7},{7,6},{8,9},{9,8},{10,11... | collective-permute-start | bytes 983048 | tf_op jit(solution)/shard_map/ppermute | solution.py:345
  109.5 11.5 %collective-permute-start.16 = (bf16[160,1024]{1,0:T(8,128)(2,1)}, bf16[160,1024]{1,0:T(8,128)(2,1)}, u32[]{:S(2)}, u32[]{:S(2)}) collective-permute-start(bf16[160,1024]{1,0:T(8,128)(2,1)} %collective-permute-done.10.refs_6_), channel_id=1, source_target_pairs={{0,1},{1,0},{2,3},{3,2},{4,5},{5,4},{6,7},{7,6},{8,9},{9,8},{10,11... | collective-permute-start | bytes 983048 | tf_op jit(solution)/shard_map/ppermute | solution.py:345
  126.7 14.8 %copy-start.11 = (bf16[320,1024]{1,0:T(8,128)(2,1)}, bf16[320,1024]{1,0:T(8,128)(2,1)S(1)}, u32[]{:S(2)}) copy-start(bf16[320,1024]{1,0:T(8,128)(2,1)S(1)} %collective-permute-done.13.refs_8_) | copy-start | bytes 1966084
  126.7 4.2 %collective-permute-start.19 = (bf16[160,1024]{1,0:T(8,128)(2,1)S(1)}, bf16[160,1024]{1,0:T(8,128)(2,1)S(1)}, u32[]{:S(2)}, u32[]{:S(2)}) collective-permute-start(bf16[160,1024]{1,0:T(8,128)(2,1)S(1)} %collective-permute-done.5.refs_3_), channel_id=1, source_target_pairs={{0,1},{1,0},{2,3},{3,2},{4,5},{5,4},{6,7},{7,6},{8,9},{9,8},{10,11... | collective-permute-start | bytes 983048 | tf_op jit(solution)/shard_map/ppermute | solution.py:345
  126.8 14.7 %collective-permute-start.21 = (bf16[320,1024]{1,0:T(8,128)(2,1)S(1)}, bf16[320,1024]{1,0:T(8,128)(2,1)S(1)}, u32[]{:S(2)}, u32[]{:S(2)}) collective-permute-start(bf16[320,1024]{1,0:T(8,128)(2,1)S(1)} %copy-done.1), channel_id=1, source_target_pairs={{0,16},{1,9},{2,18},{3,11},{4,20},{5,13},{6,22},{7,15},{8,24},{9,1... | collective-permute-start | bytes 1966088 | tf_op jit(solution)/shard_map/ppermute | solution.py:396
  128.3 16.1 %collective-permute-start.22 = (bf16[320,1024]{1,0:T(8,128)(2,1)}, bf16[320,1024]{1,0:T(8,128)(2,1)S(1)}, u32[]{:S(2)}, u32[]{:S(2)}) collective-permute-start(bf16[320,1024]{1,0:T(8,128)(2,1)} %collective-permute-done.12.refs_8_), channel_id=1, source_target_pairs={{0,16},{1,9},{2,18},{3,11},{4,20},{5,13},{6,22},{7,15},{8,24},{9,1... | collective-permute-start | bytes 1966088 | tf_op jit(solution)/shard_map/ppermute | solution.py:396
  128.9 24.4 %collective-permute-start.17 = (bf16[320,1024]{1,0:T(8,128)(2,1)S(1)}, bf16[320,1024]{1,0:T(8,128)(2,1)S(1)}, u32[]{:S(2)}, u32[]{:S(2)}) collective-permute-start(bf16[320,1024]{1,0:T(8,128)(2,1)S(1)} %copy-done), channel_id=1, source_target_pairs={{0,16},{1,9},{2,18},{3,11},{4,20},{5,13},{6,22},{7,15},{8,24},{9,1... | collective-permute-start | bytes 1966088 | tf_op jit(solution)/shard_map/ppermute | solution.py:396
  130.4 28.1 %collective-permute-start.18 = (bf16[320,1024]{1,0:T(8,128)(2,1)S(1)}, bf16[320,1024]{1,0:T(8,128)(2,1)S(1)}, u32[]{:S(2)}, u32[]{:S(2)}) collective-permute-start(bf16[320,1024]{1,0:T(8,128)(2,1)S(1)} %collective-permute-done.13.refs_8_), channel_id=1, source_target_pairs={{0,16},{1,9},{2,18},{3,11},{4,20},{5,13},{6,22},{7,15},{8,24},{9,1... | collective-permute-start | bytes 1966088 | tf_op jit(solution)/shard_map/ppermute | solution.py:396
  131.0 1.8 %collective-permute-start.20 = (bf16[160,1024]{1,0:T(8,128)(2,1)}, bf16[160,1024]{1,0:T(8,128)(2,1)S(1)}, u32[]{:S(2)}, u32[]{:S(2)}) collective-permute-start(bf16[160,1024]{1,0:T(8,128)(2,1)} %collective-permute-done.14.refs_7_), channel_id=1, source_target_pairs={{0,1},{1,0},{2,3},{3,2},{4,5},{5,4},{6,7},{7,6},{8,9},{9,8},{10,11... | collective-permute-start | bytes 983048 | tf_op jit(solution)/shard_map/ppermute | solution.py:345
  (13 other events, 64.2 us)
Sparse Core Ops, SparseCore 0:
  9.6 36.5 all-gather.2
  47.9 32.8 all-gather.4
  84.7 36.4 reduce-scatter.2
  126.8 36.2 reduce-scatter.4
